TPU v7x, 128 devices: a whole 4x4x4 slice. The times are simulated.
128 devices in a mesh: seq: 128 (over z, x, y, core).
Axes of the slice: x: 4, y: 4, z: 4, core: 2. Of those that a mesh axis runs over, the one named last changes fastest.
Arguments:
- block_in: bfloat16 [2, 16384, 512], P(None, 'seq'), may hold values from -6 to 6
- out_grad: bfloat16 [2, 16384, 512], P(None, 'seq'), may hold values from -6 to 6
- lengths: int32 [2, 16], replicated, may hold values from 0 to 8192, as said below
- ln_gain: float32 [512], replicated, may hold values from 0.25 to 1.75
- ln_bias: float32 [512], replicated, may hold values from -3 to 3
- b_proj: bfloat16 [512, 512], replicated, may hold values from -0.25 to 0.25
- c_proj: bfloat16 [512, 512], replicated, may hold values from -0.25 to 0.25
- glu_weight: bfloat16 [512, 1024], replicated, may hold values from -0.25 to 0.25
- skip_gain: float32 [512], replicated, may hold values from -4 to 4
- log_rate: float32 [256], replicated
- angle: float32 [256], replicated, may hold values from -3.140625 to 3.140625
Outputs:
- block_out: bfloat16 [2, 16384, 512], P(None, 'seq')
- in_grad: bfloat16 [2, 16384, 512], P(None, 'seq')
- gain_grad: float32 [512], P('seq')
- bias_grad: float32 [512], P('seq')
- b_grad: float32 [512, 512], P('seq')
- c_grad: float32 [512, 512], P('seq')
- glu_grad: float32 [512, 1024], P('seq')
- skip_grad: float32 [512], P('seq')
- rate_grad: float32 [256], P('seq')
- angle_grad: float32 [256], P('seq')
Inputs may be any that keep to these rules, and one draw needn't show every extreme that they name: Each row lists one micro-batch's image sequence lengths in token order, each 1024 or 8192, followed by zeros, summing to 16384.
All inputs are finite; a program needn't handle non-finite values.
Results may differ from a plain program's by a relative error of at most 0.035.
Values may be sent and summed in bfloat16 or wider, within the bound.
No kernel may reach another device: no remote copies, remote signals or barrier semaphores. Data moves between devices by JAX's collectives and lax.ppermute only.
A program may use at most 128 MiB of HBM per device.

v0:
```python
import jax
import jax.numpy as jnp
from jax import lax
from jax.sharding import PartitionSpec as P


def normalize(rows, gain, bias):
    mean = jnp.mean(rows, axis=-1, keepdims=True)
    centered = rows - mean
    variance = jnp.mean(centered * centered, axis=-1, keepdims=True)
    return centered * lax.rsqrt(variance + 1e-05) * gain + bias


def complex_step(earlier, later):
    return (
        later[0] * earlier[0] - later[1] * earlier[1],
        later[0] * earlier[1] + later[1] * earlier[0],
        later[0] * earlier[2] - later[1] * earlier[3] + later[2],
        later[0] * earlier[3] + later[1] * earlier[2] + later[3],
    )


def decay_params(log_rate, angle):
    radius = jnp.exp(-jnp.exp(log_rate))
    scale = jnp.sqrt(-jnp.expm1(-2.0 * jnp.exp(log_rate)))
    return (radius * jnp.cos(angle), radius * jnp.sin(angle), scale)


def glu_gate(gated):
    half = gated.shape[-1] // 2
    return gated[..., :half] * jax.nn.sigmoid(gated[..., half:])


def start_flags(positions, lens):
    offsets = jnp.cumsum(lens) - lens
    return jnp.any(positions[:, None] == offsets[None, :], axis=1)


def decay_terms(lam_re, lam_im, starts):
    keep = jnp.logical_not(starts)[None, :]
    return (jnp.where(keep, lam_re[:, None], 0.0), jnp.where(keep, lam_im[:, None], 0.0))


def scan_ahead(pairs, decay_re, decay_im, input_scale):
    return lax.associative_scan(
        complex_step,
        (
            decay_re,
            decay_im,
            input_scale[:, None] * pairs[:, 0],
            input_scale[:, None] * pairs[:, 1],
        ),
        axis=1,
    )


def scan_behind(grad_pairs, decay_re, decay_im):
    weight_re = jnp.concatenate([decay_re[:, 1:], jnp.ones_like(decay_re[:, :1])], axis=1)
    weight_im = jnp.concatenate([-decay_im[:, 1:], jnp.zeros_like(decay_im[:, :1])], axis=1)
    return lax.associative_scan(
        complex_step,
        (weight_re, weight_im, grad_pairs[:, 0], grad_pairs[:, 1]),
        axis=1,
        reverse=True,
    )


def body(
    block_in,
    out_grad,
    lengths,
    ln_gain,
    ln_bias,
    b_proj,
    c_proj,
    glu_weight,
    skip_gain,
    log_rate,
    angle,
):
    micro_count, tok_rows, width = block_in.shape
    states = b_proj.shape[1] // 2
    place = lax.axis_index("seq")
    (lam_full_re, lam_full_im, scale_full), param_back = jax.vjp(decay_params, log_rate, angle)
    grad_gain = jnp.zeros((width,), jnp.float32)
    grad_bias = jnp.zeros((width,), jnp.float32)
    grad_skip = jnp.zeros((width,), jnp.float32)
    grad_b = jnp.zeros(b_proj.shape, jnp.float32)
    grad_c = jnp.zeros(c_proj.shape, jnp.float32)
    grad_glu = jnp.zeros(glu_weight.shape, jnp.float32)
    grad_lam_re = jnp.zeros((states,), jnp.float32)
    grad_lam_im = jnp.zeros((states,), jnp.float32)
    grad_scale = jnp.zeros((states,), jnp.float32)
    outputs = []
    input_grads = []
    for batch_index in range(micro_count):
        rows = block_in[batch_index].astype(jnp.float32)
        cotangent = out_grad[batch_index].astype(jnp.float32)
        normed, norm_back = jax.vjp(normalize, rows, ln_gain, ln_bias)
        normed_low = normed.astype(jnp.bfloat16)
        proj = lax.dot_general(
            b_proj, normed_low, (((0,), (1,)), ((), ())), preferred_element_type=jnp.float32
        ).astype(jnp.bfloat16)
        chan = lax.all_to_all(proj, "seq", split_axis=0, concat_axis=1, tiled=True)
        channels = chan.shape[0] // 2
        length = chan.shape[1]
        first = place * channels
        lam_re = lax.dynamic_slice_in_dim(lam_full_re, first, channels)
        lam_im = lax.dynamic_slice_in_dim(lam_full_im, first, channels)
        input_scale = lax.dynamic_slice_in_dim(scale_full, first, channels)
        starts = start_flags(jnp.arange(length, dtype=jnp.int32), lengths[batch_index])
        pairs = chan.astype(jnp.float32).reshape(channels, 2, length)
        decay_re, decay_im = decay_terms(lam_re, lam_im, starts)
        prefix = scan_ahead(pairs, decay_re, decay_im, input_scale)
        state_re, state_im = (prefix[2], prefix[3])
        zero_col = jnp.zeros((channels, 1), jnp.float32)
        prior_re = jnp.concatenate([zero_col, state_re[:, :-1]], axis=1)
        prior_im = jnp.concatenate([zero_col, state_im[:, :-1]], axis=1)
        states_low = (
            jnp.stack([state_re, state_im], axis=1)
            .reshape(2 * channels, length)
            .astype(jnp.bfloat16)
        )
        hidden = lax.all_to_all(states_low, "seq", split_axis=1, concat_axis=0, tiled=True)
        mixed = lax.dot_general(
            hidden, c_proj, (((0,), (0,)), ((), ())), preferred_element_type=jnp.float32
        )
        mixed = mixed + skip_gain * normed_low.astype(jnp.float32)
        active, gelu_back = jax.vjp(jax.nn.gelu, mixed)
        active_low = active.astype(jnp.bfloat16)
        gated = jnp.dot(active_low, glu_weight, preferred_element_type=jnp.float32)
        branch, glu_back = jax.vjp(glu_gate, gated)
        outputs.append((rows + branch).astype(jnp.bfloat16))
        gated_grad = glu_back(cotangent)[0].astype(jnp.bfloat16)
        grad_glu = grad_glu + lax.dot_general(
            active_low, gated_grad, (((0,), (0,)), ((), ())), preferred_element_type=jnp.float32
        )
        active_grad = lax.dot_general(
            gated_grad, glu_weight, (((1,), (1,)), ((), ())), preferred_element_type=jnp.float32
        )
        mixed_grad = gelu_back(active_grad)[0].astype(jnp.bfloat16)
        grad_c = grad_c + lax.dot_general(
            hidden, mixed_grad, (((1,), (0,)), ((), ())), preferred_element_type=jnp.float32
        )
        mixed_grad_f = mixed_grad.astype(jnp.float32)
        grad_skip = grad_skip + jnp.sum(mixed_grad_f * normed_low.astype(jnp.float32), axis=0)
        hidden_grad = lax.dot_general(
            c_proj, mixed_grad, (((1,), (1,)), ((), ())), preferred_element_type=jnp.float32
        ).astype(jnp.bfloat16)
        grad_chan = lax.all_to_all(hidden_grad, "seq", split_axis=0, concat_axis=1, tiled=True)
        grad_pairs = grad_chan.astype(jnp.float32).reshape(channels, 2, length)
        suffix = scan_behind(grad_pairs, decay_re, decay_im)
        back_re, back_im = (suffix[2], suffix[3])
        keep = jnp.logical_not(starts)[None, :]
        part_re = jnp.sum(jnp.where(keep, back_re * prior_re + back_im * prior_im, 0.0), axis=1)
        part_im = jnp.sum(jnp.where(keep, back_im * prior_re - back_re * prior_im, 0.0), axis=1)
        part_scale = jnp.sum(back_re * pairs[:, 0] + back_im * pairs[:, 1], axis=1)
        proj_grad_low = (
            jnp.stack([input_scale[:, None] * back_re, input_scale[:, None] * back_im], axis=1)
            .reshape(2 * channels, length)
            .astype(jnp.bfloat16)
        )
        proj_grad = lax.all_to_all(proj_grad_low, "seq", split_axis=1, concat_axis=0, tiled=True)
        blank = jnp.zeros((states,), jnp.float32)
        grad_lam_re = grad_lam_re + lax.dynamic_update_slice_in_dim(blank, part_re, first, 0)
        grad_lam_im = grad_lam_im + lax.dynamic_update_slice_in_dim(blank, part_im, first, 0)
        grad_scale = grad_scale + lax.dynamic_update_slice_in_dim(blank, part_scale, first, 0)
        grad_b = grad_b + lax.dot_general(
            normed_low, proj_grad, (((0,), (1,)), ((), ())), preferred_element_type=jnp.float32
        )
        normed_grad = lax.dot_general(
            proj_grad, b_proj, (((0,), (1,)), ((), ())), preferred_element_type=jnp.float32
        )
        normed_grad = normed_grad + skip_gain * mixed_grad_f
        rows_grad, gain_part, bias_part = norm_back(normed_grad)
        grad_gain = grad_gain + gain_part
        grad_bias = grad_bias + bias_part
        input_grads.append((cotangent + rows_grad).astype(jnp.bfloat16))
    grad_rate, grad_angle = param_back((grad_lam_re, grad_lam_im, grad_scale))
    summed = (
        lax.psum_scatter(grad_gain, "seq", scatter_dimension=0, tiled=True),
        lax.psum_scatter(grad_bias, "seq", scatter_dimension=0, tiled=True),
        lax.psum_scatter(grad_b, "seq", scatter_dimension=0, tiled=True),
        lax.psum_scatter(grad_c, "seq", scatter_dimension=0, tiled=True),
        lax.psum_scatter(grad_glu, "seq", scatter_dimension=0, tiled=True),
        lax.psum_scatter(grad_skip, "seq", scatter_dimension=0, tiled=True),
        lax.psum_scatter(grad_rate, "seq", scatter_dimension=0, tiled=True),
        lax.psum_scatter(grad_angle, "seq", scatter_dimension=0, tiled=True),
    )
    return (
        jnp.stack(outputs),
        jnp.stack(input_grads),
        summed[0],
        summed[1],
        summed[2],
        summed[3],
        summed[4],
        summed[5],
        summed[6],
        summed[7],
    )


def solution(mesh):
    in_specs = (
        P(None, "seq", None),
        P(None, "seq", None),
        P(),
        P(),
        P(),
        P(),
        P(),
        P(),
        P(),
        P(),
        P(),
    )
    out_specs = (
        P(None, "seq", None),
        P(None, "seq", None),
        P("seq"),
        P("seq"),
        P("seq", None),
        P("seq", None),
        P("seq", None),
        P("seq"),
        P("seq"),
        P("seq"),
    )
    return jax.shard_map(body, mesh=mesh, in_specs=in_specs, out_specs=out_specs, check_vma=False)
```

profile of v0, /device:TPU:0, one launch (start us, length us, event | category | flops | bytes accessed | tf_op | source)
XLA Modules:
  0.0 1234.3 jit_solution(6251252019772864899)
XLA Ops:
  12.8 11.2 all-to-all-start.2
  58.0 3.7 slice.3001
  69.1 3.6 slice.3456
  90.7 4.4 slice.3225
  106.0 4.0 slice.3233
  113.5 4.0 slice.3218
  122.8 20.8 %slice.3465 = f32[2,8192]{1,0:T(2,128)} reverse(f32[2,8192]{1,0:T(2,128)S(1)} %slice.3464), dimensions={1} | reverse | bytes 131072 | tf_op jit(solution)/shard_map/slice | solution.py:60
  143.6 20.9 %reverse.30 = f32[2,8192]{1,0:T(2,128)} reverse(f32[2,8192]{1,0:T(2,128)S(1)} %bitcast.293), dimensions={1} | reverse | bytes 131072
  164.5 20.9 %slice.3452 = f32[2,8192]{1,0:T(2,128)} reverse(f32[2,8192]{1,0:T(2,128)S(1)} %slice.3451), dimensions={1} | reverse | bytes 131072 | tf_op jit(solution)/shard_map/slice | solution.py:60
  185.4 20.8 %reverse.29 = f32[2,8192]{1,0:T(2,128)} reverse(f32[2,8192]{1,0:T(2,128)S(1)} %bitcast.294), dimensions={1} | reverse | bytes 131072
  206.2 20.9 %slice.3457 = f32[2,8192]{1,0:T(2,128)} reverse(f32[2,8192]{1,0:T(2,128)S(1)} %slice.3456), dimensions={1} | reverse | bytes 131072 | tf_op jit(solution)/shard_map/slice | solution.py:60
  227.1 20.9 %slice.3467 = f32[2,8192]{1,0:T(2,128)} reverse(f32[2,8192]{1,0:T(2,128)S(1)} %slice.3466), dimensions={1} | reverse | bytes 131072 | tf_op jit(solution)/shard_map/slice | solution.py:60
  248.0 20.8 %reverse.33 = f32[2,8192]{1,0:T(2,128)} reverse(f32[2,8192]{1,0:T(2,128)S(1)} %bitcast.295), dimensions={1} | reverse | bytes 131072
  268.8 20.8 %slice.3226 = f32[2,8192]{1,0:T(2,128)} reverse(f32[2,8192]{1,0:T(2,128)S(1)} %copy-done.37), dimensions={1} | reverse | bytes 131072 | tf_op jit(solution)/shard_map/slice | solution.py:60
  289.6 20.8 %slice.3236 = f32[2,8192]{1,0:T(2,128)} reverse(f32[2,8192]{1,0:T(2,128)S(1)} %slice.3235), dimensions={1} | reverse | bytes 131072 | tf_op jit(solution)/shard_map/slice | solution.py:60
  310.4 20.6 %slice.3234 = f32[2,8192]{1,0:T(2,128)} reverse(f32[2,8192]{1,0:T(2,128)S(1)} %copy-done.38), dimensions={1} | reverse | bytes 131072 | tf_op jit(solution)/shard_map/slice | solution.py:60
  331.0 20.8 %reverse.34 = f32[2,8192]{1,0:T(2,128)} reverse(f32[2,8192]{1,0:T(2,128)S(1)} %bitcast.296), dimensions={1} | reverse | bytes 131072
  351.8 20.6 %slice.3221 = f32[2,8192]{1,0:T(2,128)} reverse(f32[2,8192]{1,0:T(2,128)S(1)} %slice.3220), dimensions={1} | reverse | bytes 131072 | tf_op jit(solution)/shard_map/slice | solution.py:60
  372.5 9.9 all-to-all-start
  382.9 9.0 all-to-all-done
  600.5 4.7 all-to-all-start.3
  606.5 8.2 all-to-all-done.3
  614.7 4.7 all-to-all-start.1
  619.7 9.1 all-to-all-done.1
  635.5 5.7 all-to-all-start.4
  650.6 7.5 all-to-all-start.6
  682.2 5.6 slice.3223
  687.8 5.6 slice.3231
  693.4 5.6 slice.3229
  698.9 5.6 slice.3242
  789.7 3.7 slice.3453
  804.7 5.6 slice.3454
  810.3 5.6 slice.3462
  815.9 5.6 slice.3460
  821.5 5.6 slice.3473
  892.7 5.6 reverse.35
  898.3 5.7 reverse.32
  937.5 11.5 rev.9
  955.7 11.1 rev.8
  968.8 9.9 all-to-all-start.5
  978.7 5.6 reverse.31
  984.3 5.7 reverse.28
  1018.6 11.3 rev.11
  1036.7 11.1 rev.10
  1050.7 9.8 all-to-all-start.7
  1061.0 8.9 all-to-all-done.7
  1073.3 63.9 %all-reduce.244 = (f32[512]{0:T(512)S(1)}, f32[512]{0:T(512)S(1)}, f32[512]{0:T(512)S(1)}, f32[256]{0:T(256)S(1)}, f32[256]{0:T(256)S(1)}) all-reduce(f32[512]{0:T(512)S(1)} %add.2602, f32[512]{0:T(512)S(1)} %add.2603, f32[512]{0:T(512)S(1)} %add.2610, f32[256]{0:T(256)S(1)} %get-tuple-element.260, ...), channel_id=2, replica_groups=mesh['seq'=128] {'seq'}, use_global_device_ids=true, to_apply=%region_14.15.clone | all-reduce | flops 2048 | bytes 16384
  1141.3 82.0 %all-reduce.248.cloned.1.call-done = (f32[512,512]{1,0:T(8,128)}, f32[512,512]{1,0:T(8,128)}, f32[512,1024]{1,0:T(8,128)}) async-done(((f32[512,512]{1,0:T(8,128)}, f32[512,512]{1,0:T(8,128)}, f32[512,1024]{1,0:T(8,128)}), (f32[512,512]{1,0:T(8,128)}, f32[512,512]{1,0:T(8,128)}, f32[512,1024]{1,0:T(8,128)})) %all-reduce.248.cloned.1.call-update) | async-done | bytes 4194320
  (1635 shorter events, 584.1 us)
Async XLA Ops:
  7.2 621.9 %copy-start = (bf16[512,1024]{1,0:T(8,128)(2,1)S(1)}, bf16[512,1024]{1,0:T(8,128)(2,1)}, u32[]{:S(2)}) copy-start(bf16[512,1024]{1,0:T(8,128)(2,1)} %param.18) | copy-start | bytes 3145732
  12.8 359.7 %all-to-all-start.2 = ((bf16[128,4,128]{2,1,0:T(4,128)(2,1)}), bf16[128,4,128]{2,1,0:T(4,128)(2,1)S(1)}, u32[]{:S(2)}, u32[]{:S(2)}) async-start(bf16[128,4,128]{2,1,0:T(4,128)(2,1)} %bitcast.13), calls=%async_computation.2 | async-start | bytes 262144 | tf_op jit(solution)/shard_map/all_to_all | solution.py:104
  95.1 173.7 %copy-start.37 = (f32[2,8192]{1,0:T(2,128)S(1)}, f32[2,8192]{1,0:T(2,128)}, u32[]{:S(2)}) copy-start(f32[2,8192]{1,0:T(2,128)} %slice.3225) | copy-start | bytes 196612
  117.5 192.9 %copy-start.38 = (f32[2,8192]{1,0:T(2,128)S(1)}, f32[2,8192]{1,0:T(2,128)}, u32[]{:S(2)}) copy-start(f32[2,8192]{1,0:T(2,128)} %slice.3233) | copy-start | bytes 196612
  117.5 213.5 %copy-start.39 = (f32[2,8191]{1,0:T(2,128)S(1)}, f32[2,8191]{1,0:T(2,128)}, u32[]{:S(2)}) copy-start(f32[2,8191]{1,0:T(2,128)} %slice.3218) | copy-start | bytes 196588
  372.5 19.4 %all-to-all-start = ((bf16[128,4,128]{2,1,0:T(4,128)(2,1)}), bf16[128,4,128]{2,1,0:T(4,128)(2,1)S(1)}, u32[]{:S(2)}, u32[]{:S(2)}) async-start(bf16[128,4,128]{2,1,0:T(4,128)(2,1)} %bitcast.2), calls=%async_computation | async-start | bytes 262144 | tf_op jit(solution)/shard_map/all_to_all | solution.py:104
  600.5 14.1 %all-to-all-start.3 = ((bf16[4,128,128]{2,0,1:T(4,128)(2,1)}), bf16[4,128,128]{2,0,1:T(4,128)(2,1)S(1)}, u32[]{:S(2)}, u32[]{:S(2)}) async-start(bf16[4,128,128]{2,0,1:T(4,128)(2,1)} %copy.77), calls=%async_computation.3 | async-start | bytes 262144 | tf_op jit(solution)/shard_map/all_to_all | solution.py:124
  614.7 14.1 %all-to-all-start.1 = ((bf16[4,128,128]{2,0,1:T(4,128)(2,1)}), bf16[4,128,128]{2,0,1:T(4,128)(2,1)S(1)}, u32[]{:S(2)}, u32[]{:S(2)}) async-start(bf16[4,128,128]{2,0,1:T(4,128)(2,1)} %copy.71), calls=%async_computation.1 | async-start | bytes 262144 | tf_op jit(solution)/shard_map/all_to_all | solution.py:124
  635.5 15.1 %all-to-all-start.4 = ((bf16[128,4,128]{2,1,0:T(4,128)(2,1)}), bf16[128,4,128]{2,1,0:T(4,128)(2,1)}, u32[]{:S(2)}, u32[]{:S(2)}) async-start(bf16[128,4,128]{2,1,0:T(4,128)(2,1)} %bitcast.26), calls=%async_computation.4 | async-start | bytes 262144 | tf_op jit(solution)/shard_map/all_to_all | solution.py:150
  650.6 130.9 %all-to-all-start.6 = ((bf16[128,4,128]{2,1,0:T(4,128)(2,1)}), bf16[128,4,128]{2,1,0:T(4,128)(2,1)S(1)}, u32[]{:S(2)}, u32[]{:S(2)}) async-start(bf16[128,4,128]{2,1,0:T(4,128)(2,1)} %bitcast.38), calls=%async_computation.6 | async-start | bytes 262144 | tf_op jit(solution)/shard_map/all_to_all | solution.py:150
  745.6 81.5 %copy-start.29 = (f32[2,8192]{1,0:T(2,128)S(1)}, f32[2,8192]{1,0:T(2,128)}, u32[]{:S(2)}) copy-start(f32[2,8192]{1,0:T(2,128)} %slice.3465) | copy-start | bytes 196612
  745.6 81.5 %copy-start.30 = (f32[2,8192]{1,0:T(2,128)S(1)}, f32[2,8192]{1,0:T(2,128)}, u32[]{:S(2)}) copy-start(f32[2,8192]{1,0:T(2,128)} %slice.3452) | copy-start | bytes 196612
  745.6 81.5 %copy-start.31 = (f32[2,8192]{1,0:T(2,128)S(1)}, f32[2,8192]{1,0:T(2,128)}, u32[]{:S(2)}) copy-start(f32[2,8192]{1,0:T(2,128)} %slice.3457) | copy-start | bytes 196612
  745.6 81.5 %copy-start.32 = (f32[2,8192]{1,0:T(2,128)S(1)}, f32[2,8192]{1,0:T(2,128)}, u32[]{:S(2)}) copy-start(f32[2,8192]{1,0:T(2,128)} %slice.3467) | copy-start | bytes 196612
  821.5 93.0 %copy-start.94 = (f32[2,255]{1,0:T(2,128)S(1)}, f32[2,255]{1,0:T(2,128)}, u32[]{:S(2)}) copy-start(f32[2,255]{1,0:T(2,128)} %slice.3278) | copy-start | bytes 6124
  821.5 93.0 %copy-start.95 = (f32[2,255]{1,0:T(2,128)S(1)}, f32[2,255]{1,0:T(2,128)}, u32[]{:S(2)}) copy-start(f32[2,255]{1,0:T(2,128)} %slice.3405) | copy-start | bytes 6124
  821.5 93.0 %copy-start.96 = (f32[2,255]{1,0:T(2,128)S(1)}, f32[2,255]{1,0:T(2,128)}, u32[]{:S(2)}) copy-start(f32[2,255]{1,0:T(2,128)} %slice.3409) | copy-start | bytes 6124
  821.5 93.0 %copy-start.97 = (f32[2,255]{1,0:T(2,128)S(1)}, f32[2,255]{1,0:T(2,128)}, u32[]{:S(2)}) copy-start(f32[2,255]{1,0:T(2,128)} %slice.3413) | copy-start | bytes 6124
  821.5 94.1 %copy-start.76 = (f32[2,511]{1,0:T(2,128)S(1)}, f32[2,511]{1,0:T(2,128)}, u32[]{:S(2)}) copy-start(f32[2,511]{1,0:T(2,128)} %slice.3411) | copy-start | bytes 12268
  821.5 94.1 %copy-start.77 = (f32[2,511]{1,0:T(2,128)S(1)}, f32[2,511]{1,0:T(2,128)}, u32[]{:S(2)}) copy-start(f32[2,511]{1,0:T(2,128)} %slice.3268) | copy-start | bytes 12268
  821.5 94.1 %copy-start.78 = (f32[2,511]{1,0:T(2,128)S(1)}, f32[2,511]{1,0:T(2,128)}, u32[]{:S(2)}) copy-start(f32[2,511]{1,0:T(2,128)} %slice.3419) | copy-start | bytes 12268
  821.5 94.1 %copy-start.79 = (f32[2,511]{1,0:T(2,128)S(1)}, f32[2,511]{1,0:T(2,128)}, u32[]{:S(2)}) copy-start(f32[2,511]{1,0:T(2,128)} %slice.3415) | copy-start | bytes 12268
  827.1 88.5 %copy-start.120 = (f32[2,1]{1,0:T(2,128)S(1)}, f32[2,1]{1,0:T(2,128)}, u32[]{:S(2)}) copy-start(f32[2,1]{1,0:T(2,128)} %slice.3787) | copy-start | bytes 28
  827.1 89.8 %copy-start.44 = (f32[2,1023]{1,0:T(2,128)S(1)}, f32[2,1023]{1,0:T(2,128)}, u32[]{:S(2)}) copy-start(f32[2,1023]{1,0:T(2,128)} %slice.3258) | copy-start | bytes 24556
  827.1 89.8 %copy-start.45 = (f32[2,1023]{1,0:T(2,128)S(1)}, f32[2,1023]{1,0:T(2,128)}, u32[]{:S(2)}) copy-start(f32[2,1023]{1,0:T(2,128)} %slice.3417) | copy-start | bytes 24556
  827.1 89.8 %copy-start.46 = (f32[2,1023]{1,0:T(2,128)S(1)}, f32[2,1023]{1,0:T(2,128)}, u32[]{:S(2)}) copy-start(f32[2,1023]{1,0:T(2,128)} %slice.3421) | copy-start | bytes 24556
  827.1 89.8 %copy-start.47 = (f32[2,1023]{1,0:T(2,128)S(1)}, f32[2,1023]{1,0:T(2,128)}, u32[]{:S(2)}) copy-start(f32[2,1023]{1,0:T(2,128)} %slice.3425) | copy-start | bytes 24556
  827.2 89.8 %copy-start.119 = (f32[2,1]{1,0:T(2,128)S(1)}, f32[2,1]{1,0:T(2,128)}, u32[]{:S(2)}) copy-start(f32[2,1]{1,0:T(2,128)} %slice.3792) | copy-start | bytes 28
  827.2 89.9 %copy-start.118 = (f32[2,1]{1,0:T(2,128)S(1)}, f32[2,1]{1,0:T(2,128)}, u32[]{:S(2)}) copy-start(f32[2,1]{1,0:T(2,128)} %slice.3771) | copy-start | bytes 28
  827.5 91.6 %copy-start.116 = (f32[2,1]{1,0:T(2,128)S(1)}, f32[2,1]{1,0:T(2,128)}, u32[]{:S(2)}) copy-start(f32[2,1]{1,0:T(2,128)} %slice.3797) | copy-start | bytes 28
  827.5 91.7 %copy-start.117 = (f32[2,1]{1,0:T(2,128)S(1)}, f32[2,1]{1,0:T(2,128)}, u32[]{:S(2)}) copy-start(f32[2,1]{1,0:T(2,128)} %slice.3770) | copy-start | bytes 28
  827.5 80.1 %copy-start.65 = (f32[2,16]{1,0:T(2,128)S(1)}, f32[2,16]{1,0:T(2,128)}, u32[]{:S(2)}) copy-start(f32[2,16]{1,0:T(2,128)} %copy-done.64) | copy-start | bytes 388
  827.6 80.3 %copy-start.63 = (f32[2,16]{1,0:T(2,128)S(1)}, f32[2,16]{1,0:T(2,128)}, u32[]{:S(2)}) copy-start(f32[2,16]{1,0:T(2,128)} %copy-done.62) | copy-start | bytes 388
  827.6 81.3 %copy-start.61 = (f32[2,32]{1,0:T(2,128)S(1)}, f32[2,32]{1,0:T(2,128)}, u32[]{:S(2)}) copy-start(f32[2,32]{1,0:T(2,128)} %copy-done.60) | copy-start | bytes 772
  827.6 81.5 %copy-start.59 = (f32[2,32]{1,0:T(2,128)S(1)}, f32[2,32]{1,0:T(2,128)}, u32[]{:S(2)}) copy-start(f32[2,32]{1,0:T(2,128)} %copy-done.58) | copy-start | bytes 772
  827.6 82.6 %copy-start.57 = (f32[2,64]{1,0:T(2,128)S(1)}, f32[2,64]{1,0:T(2,128)}, u32[]{:S(2)}) copy-start(f32[2,64]{1,0:T(2,128)} %copy-done.56) | copy-start | bytes 1540
  827.6 82.8 %copy-start.55 = (f32[2,64]{1,0:T(2,128)S(1)}, f32[2,64]{1,0:T(2,128)}, u32[]{:S(2)}) copy-start(f32[2,64]{1,0:T(2,128)} %copy-done.54) | copy-start | bytes 1540
  827.6 84.0 %copy-start.53 = (f32[2,128]{1,0:T(2,128)S(1)}, f32[2,128]{1,0:T(2,128)}, u32[]{:S(2)}) copy-start(f32[2,128]{1,0:T(2,128)} %copy-done.52) | copy-start | bytes 3076
  827.6 84.2 %copy-start.51 = (f32[2,128]{1,0:T(2,128)S(1)}, f32[2,128]{1,0:T(2,128)}, u32[]{:S(2)}) copy-start(f32[2,128]{1,0:T(2,128)} %copy-done.50) | copy-start | bytes 3076
  827.6 85.6 %copy-start.125 = (f32[2,1]{1,0:T(2,128)S(1)}, f32[2,1]{1,0:T(2,128)}, u32[]{:S(2)}) copy-start(f32[2,1]{1,0:T(2,128)} %slice.3777) | copy-start | bytes 28
  827.6 86.9 %copy-start.123 = (f32[2,1]{1,0:T(2,128)S(1)}, f32[2,1]{1,0:T(2,128)}, u32[]{:S(2)}) copy-start(f32[2,1]{1,0:T(2,128)} %slice.3782) | copy-start | bytes 28
  827.6 87.0 %copy-start.122 = (f32[2,1]{1,0:T(2,128)S(1)}, f32[2,1]{1,0:T(2,128)}, u32[]{:S(2)}) copy-start(f32[2,1]{1,0:T(2,128)} %slice.3773) | copy-start | bytes 28
  827.7 88.1 %copy-start.121 = (f32[2,1]{1,0:T(2,128)S(1)}, f32[2,1]{1,0:T(2,128)}, u32[]{:S(2)}) copy-start(f32[2,1]{1,0:T(2,128)} %slice.3772) | copy-start | bytes 28
  840.5 82.4 %copy-start.113 = (f32[2,1]{1,0:T(2,128)S(1)}, f32[2,1]{1,0:T(2,128)}, u32[]{:S(2)}) copy-start(f32[2,1]{1,0:T(2,128)} %slice.3802) | copy-start | bytes 28
  841.1 81.9 %copy-start.112 = (f32[2,1]{1,0:T(2,128)S(1)}, f32[2,1]{1,0:T(2,128)}, u32[]{:S(2)}) copy-start(f32[2,1]{1,0:T(2,128)} %slice.3769) | copy-start | bytes 28
  968.8 82.0 %all-to-all-start.5 = ((bf16[4,128,128]{2,0,1:T(4,128)(2,1)}), bf16[4,128,128]{2,0,1:T(4,128)(2,1)S(1)}, u32[]{:S(2)}, u32[]{:S(2)}) async-start(bf16[4,128,128]{2,0,1:T(4,128)(2,1)} %copy.83), calls=%async_computation.5 | async-start | bytes 262144 | tf_op jit(solution)/shard_map/all_to_all | solution.py:163
  1050.7 19.2 %all-to-all-start.7 = ((bf16[4,128,128]{2,0,1:T(4,128)(2,1)}), bf16[4,128,128]{2,0,1:T(4,128)(2,1)S(1)}, u32[]{:S(2)}, u32[]{:S(2)}) async-start(bf16[4,128,128]{2,0,1:T(4,128)(2,1)} %copy.89), calls=%async_computation.7 | async-start | bytes 262144 | tf_op jit(solution)/shard_map/all_to_all | solution.py:163
  1060.5 162.8 %all-reduce.248.cloned.1.call-start = ((), (), s32[]{:S(2)}) async-start(), calls=%async_computation.8 | async-start | bytes 8388608
  (119 other events, 5039.0 us)
Sparse Core Ops, SparseCore 0:
  1071.5 151.7 all-reduce.247
where the time goes:
time: 1240 us; the launch traced here: 1230 us
  local copies, waits for them, and re-layouts  913 us (74%)
  waiting for transfers between devices  120 us (10%)
  blocking collectives  63.9 us (5%)
  starting transfers between devices  63.4 us (5%)
  other arithmetic  38 us (3%)
  between operations  20.3 us (2%)
  matrix products  15.7 us (1%)
    slice x348, local copies, waits for them, and re-layouts, scan_behind(): lax.associative_scan(complex_step, (weight_re, weight_im, grad_pairs[:, 0...  441 us
    slice x332, local copies, waits for them, and re-layouts, scan_ahead(): lax.associative_scan(complex_step, (decay_re, decay_im, input_scale[:, No...  176 us
    unnamed x336, local copies, waits for them, and re-layouts  116 us
    unnamed x2, waiting for transfers between devices  82 us
    unnamed x1, blocking collectives  63.9 us
    pad x104, local copies, waits for them, and re-layouts, scan_ahead(): lax.associative_scan(complex_step, (decay_re, decay_im, input_scale[:, No...  61.6 us
    pad x104, local copies, waits for them, and re-layouts, scan_behind(): lax.associative_scan(complex_step, (weight_re, weight_im, grad_pairs[:, 0...  60.5 us
    rev x4, local copies, waits for them, and re-layouts, scan_behind(): lax.associative_scan(complex_step, (weight_re, weight_im, grad_pairs[:, 0...  45.1 us
  transfers between devices with their start and end apart: 9, of which 6 were waited for; matrix products, arithmetic and copies ran while one was open for 45% of the time, Pallas kernels for 0%

commit v1 on v0

v1 whole, which is shorter than its diff:
```python
import functools

import jax
import jax.numpy as jnp
import numpy as np
from jax import lax
from jax.experimental import pallas as pl
from jax.experimental.pallas import tpu as pltpu
from jax.sharding import PartitionSpec as P

F32 = jnp.float32
BF16 = jnp.bfloat16
VMEM_LIMIT = 56 * 1024 * 1024
TOK = 128
GROUPS = TOK // 8
MICRO = 2
HALVES = 2
N = 128


def deal():
    out = np.zeros((256, 256), np.float32)
    for n in range(128):
        out[2 * n, n] = 1.0
        out[2 * n + 1, 128 + n] = 1.0
    return out


def dot(a, b):
    return jnp.dot(a, b, preferred_element_type=F32)


def dot_tn(a, b):
    return lax.dot_general(a, b, (((0,), (0,)), ((), ())), preferred_element_type=F32)


def dot_nt(a, b):
    return lax.dot_general(a, b, (((1,), (1,)), ((), ())), preferred_element_type=F32)


def cmul(a, b):
    return (a[0] * b[0] - a[1] * b[1], a[0] * b[1] + a[1] * b[0])


def conj(a):
    return (a[0], -a[1])


def rows_iota(shape=(8, 128)):
    return lax.broadcasted_iota(jnp.int32, shape, len(shape) - 2)


def params(log_rate, angle):
    u = jnp.exp(log_rate)
    r = jnp.exp(-u)
    lam = (r * jnp.cos(angle), r * jnp.sin(angle))
    w = 2.0 * u
    small = jnp.minimum(w, 0.5)
    poly = 1.0 - small * (1.0 / 11.0)
    for k in range(10, 1, -1):
        poly = 1.0 - small * (1.0 / k) * poly
    gap = jnp.where(w < 0.5, small * poly, 1.0 - jnp.exp(-w))
    scale = jnp.sqrt(gap)
    return u, r, lam, scale


def powers(lam, count):
    out = [lam]
    for _ in range(count):
        out.append(cmul(out[-1], out[-1]))
    return out


def lam_tiles(log_rate_ref, angle_ref):
    out = []
    for half in range(HALVES):
        lr = jnp.broadcast_to(log_rate_ref[half : half + 1, :], (8, 128))
        an = jnp.broadcast_to(angle_ref[half : half + 1, :], (8, 128))
        out.append(params(lr, an))
    return out


def scan_tables(pows, reverse):
    row = rows_iota()
    pos = (7 - row) if reverse else row
    levels = []
    for s, p in ((1, pows[0]), (2, pows[1]), (4, pows[2])):
        keep = pos >= s
        levels.append((s, (jnp.where(keep, p[0], 0.0), jnp.where(keep, p[1], 0.0))))
    e = pos + 1
    table = (jnp.ones((8, 128), F32), jnp.zeros((8, 128), F32))
    for bit in range(4):
        on = (lax.shift_right_logical(e, bit) & 1) == 1
        table = cmul(table, (jnp.where(on, pows[bit][0], 1.0), jnp.where(on, pows[bit][1], 0.0)))
    return levels, table


def group_scan(x, levels, reverse):
    xr, xi = x
    for s, (mr, mi) in levels:
        shift = 8 - s if reverse else s
        rr = pltpu.roll(xr, shift, 1)
        ri = pltpu.roll(xi, shift, 1)
        xr, xi = xr + (mr * rr - mi * ri), xi + (mr * ri + mi * rr)
    return xr, xi


def tile_rows(parts):
    rows = []
    for comp in range(2):
        for micro in range(MICRO):
            for half in range(HALVES):
                rows.append(parts[(micro, half)][comp])
    return jnp.concatenate(rows, axis=0)


def tile_lam(p):
    row = rows_iota()
    odd = (row & 1) == 1
    re = jnp.where(odd, p[1][0], p[0][0])
    im = jnp.where(odd, p[1][1], p[0][1])
    return re, jnp.where(row < 4, -im, im)


def tile_mul(c, coef):
    return c * coef[0] + pltpu.roll(c, 4, 0) * coef[1]


def gather_carry(ends_ref, me, step, dmax, coef, coef8):
    chains = []
    for chain in range(8):
        acc = jnp.zeros((8, 128), F32)
        for i in range(7, -1, -1):
            d = chain * 8 + i
            at = jnp.clip(me + step * (1 + d), 0, N - 1)
            e = ends_ref[at].astype(F32)
            e = jnp.where(d <= dmax, e, 0.0)
            acc = e if i == 7 else tile_mul(acc, coef) + e
        chains.append(acc)
    total = chains[7]
    for chain in range(6, -1, -1):
        total = tile_mul(total, coef8) + chains[chain]
    return total


def segment(lengths_ref, micro, base):
    first = jnp.int32(0)
    last = jnp.int32(N * TOK)
    at = jnp.int32(0)
    for slot in range(16):
        first = jnp.where(at <= base, jnp.maximum(first, at), first)
        last = jnp.where(at > base, jnp.minimum(last, at), last)
        at = at + lengths_ref[micro, slot]
    return first, last


def distance_tiles(lengths_ref, me):
    base = me * TOK
    row = rows_iota()
    second = (row & 2) == 2
    ahead, behind = [], []
    for micro in range(MICRO):
        first, last = segment(lengths_ref, micro, base)
        ahead.append((base - first) // TOK - 1)
        behind.append((last - base) // TOK - 2)
    pick = lambda two: jnp.where(second, two[1], two[0])
    return pick(ahead), pick(behind)


def groups_of(value, micro_groups=MICRO * GROUPS):
    return value.reshape(micro_groups, 8, 128)


def split_channels(value):
    out = []
    for half in range(HALVES):
        c = 256 * half
        out.append((groups_of(value[:, c : c + 128]), groups_of(value[:, c + 128 : c + 256])))
    return out


def join_channels(halves):
    cols = []
    for re, im in halves:
        cols.append(re.reshape(MICRO * TOK, 128))
        cols.append(im.reshape(MICRO * TOK, 128))
    return jnp.concatenate(cols, axis=1)


def permute(value_bf, matrix):
    return jnp.concatenate([dot(value_bf[:, :256], matrix), dot(value_bf[:, 256:], matrix)], axis=1)


def layer_norm(x):
    mean = jnp.mean(x, axis=1, keepdims=True)
    centered = x - mean
    var = jnp.mean(centered * centered, axis=1, keepdims=True)
    rstd = lax.rsqrt(var + 1e-05)
    return centered * rstd, rstd


def chain_from(x, micro, step8, init, reverse):
    before = {}
    v = init
    order = range(GROUPS - 1, -1, -1) if reverse else range(GROUPS)
    for g in order:
        before[g] = v
        xr, xi = x[0][micro * GROUPS + g], x[1][micro * GROUPS + g]
        if v is None:
            v = (xr, xi)
        else:
            m = cmul(v, step8)
            v = (xr + m[0], xi + m[1])
    return before, v


def edge_bcast(pair, edge):
    return tuple(jnp.broadcast_to(p[edge : edge + 1, :], (8, 128)) for p in pair)


def kernel_first(x_ref, gain_ref, bias_ref, b_ref, deal_ref, log_rate_ref, angle_ref, normed_ref, pairs_ref, local_ref, ends_ref):
    x = x_ref[...].astype(F32)
    xhat, _ = layer_norm(x)
    normed = (xhat * gain_ref[...] + bias_ref[...]).astype(BF16)
    normed_ref[...] = normed
    proj = dot(normed, b_ref[...]).astype(BF16)
    pairs = permute(proj, deal_ref[...])
    pairs_ref[...] = pairs.astype(BF16)
    halves = split_channels(pairs)
    lams = lam_tiles(log_rate_ref, angle_ref)
    parts, scanned = {}, []
    for half in range(HALVES):
        _, _, lam, scale = lams[half]
        pows = powers(lam, 3)
        levels, _ = scan_tables(pows, False)
        re, im = halves[half]
        x8 = group_scan((re * scale, im * scale), levels, False)
        scanned.append(x8)
        for micro in range(MICRO):
            _, v = chain_from(x8, micro, pows[3], None, False)
            parts[(micro, half)] = (v[0][7:8, :], v[1][7:8, :])
    local_ref[...] = join_channels(scanned)
    ends_ref[...] = jnp.broadcast_to(tile_rows(parts).astype(BF16)[None], (N, 8, 128))


def tile_row(tile, comp, micro, half):
    at = comp * 4 + micro * 2 + half
    return jnp.broadcast_to(tile[at : at + 1, :], (8, 128))


def carry_pows(lams):
    long_pows = [powers(lams[half][2], 10) for half in range(HALVES)]
    return long_pows


def kernel_middle(
    lengths_ref, ends_ref, local_ref, normed_ref, x_ref, go_ref, c_ref, glu_ref, skip_ref, deal_ref, deal_back_ref, log_rate_ref, angle_ref,
    out_ref, act_ref, dgated_ref, hidden_ref, dy_ref, back_ref, prior_ref, firsts_ref,
):
    me = lax.axis_index("seq")
    ahead, _ = distance_tiles(lengths_ref, me)
    lams = lam_tiles(log_rate_ref, angle_ref)
    pows = carry_pows(lams)
    coef = tile_lam([p[7] for p in pows])
    coef8 = tile_lam([p[10] for p in pows])
    carry = gather_carry(ends_ref, me, -1, ahead, coef, coef8)
    local = split_channels(local_ref[...])
    row = rows_iota((MICRO * GROUPS, 8, 128))
    states, priors = [], []
    for half in range(HALVES):
        _, table = scan_tables(pows[half], False)
        x8 = local[half]
        before_r, before_i = [], []
        for micro in range(MICRO):
            init = (tile_row(carry, 0, micro, half), tile_row(carry, 1, micro, half))
            before, _ = chain_from(x8, micro, pows[half][3], init, False)
            for g in range(GROUPS):
                edge = edge_bcast(before[g], 7)
                before_r.append(edge[0])
                before_i.append(edge[1])
        br, bi = jnp.stack(before_r), jnp.stack(before_i)
        hr = x8[0] + (table[0] * br - table[1] * bi)
        hi = x8[1] + (table[0] * bi + table[1] * br)
        states.append((hr, hi))
        priors.append((jnp.where(row == 0, br, pltpu.roll(hr, 1, 1)), jnp.where(row == 0, bi, pltpu.roll(hi, 1, 1))))
    prior_ref[...] = join_channels(priors)
    hidden = permute(join_channels(states).astype(BF16), deal_back_ref[...]).astype(BF16)
    hidden_ref[...] = hidden
    y = dot(hidden, c_ref[...]) + skip_ref[...] * normed_ref[...].astype(F32)
    k0, k1 = 0.7978845608028654, 0.044715
    yy = y * y
    t = jnp.tanh(k0 * (y + k1 * (yy * y)))
    act = (0.5 * y * (1.0 + t)).astype(BF16)
    act_ref[...] = act
    slope = 0.5 * (1.0 + t) + 0.5 * y * (1.0 - t * t) * (k0 * (1.0 + 3.0 * k1 * yy))
    gated = dot(act, glu_ref[...])
    value, gate = gated[:, :512], gated[:, 512:]
    sig = jax.nn.sigmoid(gate)
    go = go_ref[...].astype(F32)
    out_ref[...] = (x_ref[...].astype(F32) + value * sig).astype(BF16)
    gs = go * sig
    dgated = jnp.concatenate([gs, gs * value * (1.0 - sig)], axis=1).astype(BF16)
    dgated_ref[...] = dgated
    dy = (dot_nt(dgated, glu_ref[...]) * slope).astype(BF16)
    dy_ref[...] = dy
    dhidden = dot_nt(dy, c_ref[...]).astype(BF16)
    q = split_channels(permute(dhidden, deal_ref[...]))
    parts, scanned = {}, []
    for half in range(HALVES):
        cp = [conj(p) for p in pows[half][:4]]
        levels, _ = scan_tables(cp, True)
        x8 = group_scan(q[half], levels, True)
        scanned.append(x8)
        for micro in range(MICRO):
            _, v = chain_from(x8, micro, cp[3], None, True)
            parts[(micro, half)] = (v[0][0:1, :], v[1][0:1, :])
    back_ref[...] = join_channels(scanned)
    firsts_ref[...] = jnp.broadcast_to(tile_rows(parts).astype(BF16)[None], (N, 8, 128))


def chunk_rows(left, right):
    w = left.shape[1]
    a = left.reshape(64, 8, w)
    b = right.reshape(64, 8, w)
    low = rows_iota((64, 8, w)) < 4
    even = jnp.where(low, a, pltpu.roll(b, 4, 1))
    odd = jnp.where(low, pltpu.roll(a, 4, 1), b)
    return jnp.stack([even, odd], axis=1).reshape(128, 8, w)


def kernel_weights(act_ref, dgated_ref, hidden_ref, dy_ref, out_ref):
    glu = dot_tn(act_ref[...], dgated_ref[...])
    c = dot_tn(hidden_ref[...], dy_ref[...])
    out_ref[...] = chunk_rows(glu[:, :768], jnp.concatenate([glu[:, 768:], c], axis=1)).astype(BF16)


def small_chunks(vectors, channels):
    dest = lax.broadcasted_iota(jnp.int32, (N, 512), 0)
    feature = lax.broadcasted_iota(jnp.int32, (N, 512), 1)
    lane = lax.broadcasted_iota(jnp.int32, (512, 128), 1)
    row = lax.broadcasted_iota(jnp.int32, (512, 128), 0)
    by_four = ((feature // 4) == dest, row % 4)
    by_two = (((feature % 256) // 2) == dest, row % 2 + 2 * (row // 256))
    total = jnp.zeros((N, 128), F32)
    for v, vec in enumerate(vectors + [channels]):
        mine, inner = by_two if v == len(vectors) else by_four
        high = vec.astype(BF16).astype(F32)
        rest = vec - high
        for part, base in ((high, 4 * v), (rest, 64 + 4 * v)):
            spread = jnp.where(mine, part, 0.0).astype(BF16)
            place = jnp.where(lane == base + inner, 1.0, 0.0).astype(BF16)
            total = total + dot(spread, place)
    return total


def kernel_last(
    lengths_ref, firsts_ref, back_ref, prior_ref, pairs_ref, normed_ref, x_ref, go_ref, dy_ref, b_ref, gain_ref, skip_ref, deal_back_ref,
    log_rate_ref, angle_ref, in_grad_ref, out_ref,
):
    me = lax.axis_index("seq")
    _, behind = distance_tiles(lengths_ref, me)
    lams = lam_tiles(log_rate_ref, angle_ref)
    pows = [[conj(p) for p in per_half] for per_half in carry_pows(lams)]
    coef = tile_lam([p[7] for p in pows])
    coef8 = tile_lam([p[10] for p in pows])
    carry = gather_carry(firsts_ref, me, 1, behind, coef, coef8)
    local = split_channels(back_ref[...])
    prior = split_channels(prior_ref[...])
    pairs = split_channels(pairs_ref[...].astype(F32))
    projs, rates, angles = [], [], []
    for half in range(HALVES):
        u, r, lam, scale = lams[half]
        _, table = scan_tables(pows[half], True)
        x8 = local[half]
        after_r, after_i = [], []
        for micro in range(MICRO):
            init = (tile_row(carry, 0, micro, half), tile_row(carry, 1, micro, half))
            after, _ = chain_from(x8, micro, pows[half][3], init, True)
            for g in range(GROUPS):
                edge = edge_bcast(after[g], 0)
                after_r.append(edge[0])
                after_i.append(edge[1])
        ar, ai = jnp.stack(after_r), jnp.stack(after_i)
        gr = x8[0] + (table[0] * ar - table[1] * ai)
        gi = x8[1] + (table[0] * ai + table[1] * ar)
        pr, pi = prior[half]
        total = lambda v: jnp.sum(jnp.sum(v, axis=0), axis=0, keepdims=True)
        d_re = total(gr * pr + gi * pi)
        d_im = total(gi * pr - gr * pi)
        d_scale = total(gr * pairs[half][0] + gi * pairs[half][1])
        one = lambda t: t[0:1, :]
        lr, li = one(lam[0]), one(lam[1])
        rates.append(one(u) * (one(r) * one(r) * d_scale / one(scale) - (lr * d_re + li * d_im)))
        angles.append(lr * d_im - li * d_re)
        projs.append((gr * scale, gi * scale))
    dproj = permute(join_channels(projs).astype(BF16), deal_back_ref[...]).astype(BF16)
    normed = normed_ref[...]
    b_grad = dot_tn(normed, dproj)
    dy = dy_ref[...].astype(F32)
    dnormed = dot_nt(dproj, b_ref[...]) + skip_ref[...] * dy
    go = go_ref[...].astype(F32)
    xhat, rstd = layer_norm(x_ref[...].astype(F32))
    col = lambda v: jnp.sum(v, axis=0, keepdims=True)
    gain_grad = col(dnormed * xhat)
    bias_grad = col(dnormed)
    skip_grad = col(dy * normed.astype(F32))
    smalls = small_chunks([gain_grad, bias_grad, skip_grad], jnp.concatenate(rates + angles, axis=1))
    chunks = chunk_rows(b_grad[:, :256], b_grad[:, 256:])
    out_ref[:, :, 0:256] = chunks.astype(BF16)
    out_ref[:, :, 256:384] = jnp.broadcast_to(smalls[:, None, :], (N, 8, 128)).astype(BF16)
    dx = dnormed * gain_ref[...]
    m1 = jnp.mean(dx, axis=1, keepdims=True)
    m2 = jnp.mean(dx * xhat, axis=1, keepdims=True)
    in_grad_ref[...] = (go + rstd * (dx - m1 - xhat * m2)).astype(BF16)


def kernel_sum(wide_ref, narrow_ref, b_ref, c_ref, glu_ref, small_ref):
    wide = jnp.sum(wide_ref[...].astype(F32), axis=0)
    glu_ref[:, 0:768] = wide[0:4, :]
    glu_ref[:, 768:1024] = wide[4:8, 0:256]
    c_ref[...] = wide[4:8, 256:768]
    narrow = jnp.sum(narrow_ref[...].astype(F32), axis=0)
    b_ref[:, 0:256] = narrow[0:4, 0:256]
    b_ref[:, 256:512] = narrow[4:8, 0:256]
    small = narrow[:, 256:384]
    small_ref[...] = small + pltpu.roll(small, 64, 1)


def call(kernel, outs, args, smem=(), flops=0, nbytes=0):
    space = lambda i: pltpu.SMEM if i in smem else pltpu.VMEM
    return pl.pallas_call(
        kernel,
        out_shape=[jax.ShapeDtypeStruct(s, d) for s, d in outs],
        in_specs=[pl.BlockSpec(memory_space=space(i)) for i in range(len(args))],
        out_specs=[pl.BlockSpec(memory_space=pltpu.VMEM) for _ in outs],
        compiler_params=pltpu.CompilerParams(vmem_limit_bytes=VMEM_LIMIT),
        cost_estimate=pl.CostEstimate(flops=flops, bytes_accessed=nbytes, transcendentals=0),
    )(*args)


def body(block_in, out_grad, lengths, ln_gain, ln_bias, b_proj, c_proj, glu_weight, skip_gain, log_rate, angle):
    rows = MICRO * TOK
    x = block_in.reshape(rows, 512)
    go = out_grad.reshape(rows, 512)
    gain, bias, skip = (v.reshape(1, 512) for v in (ln_gain, ln_bias, skip_gain))
    rate2, angle2 = log_rate.reshape(2, 128), angle.reshape(2, 128)
    spread = deal()
    deal_m = jnp.asarray(spread, BF16)
    back_m = jnp.asarray(spread.T.copy(), BF16)
    full = (rows, 512)
    exchange = functools.partial(lax.all_to_all, axis_name="seq", split_axis=0, concat_axis=0, tiled=True)
    normed, pairs, local, ends = call(
        kernel_first, [(full, BF16), (full, BF16), (full, F32), ((N, 8, 128), BF16)], [x, gain, bias, b_proj, deal_m, rate2, angle2],
        flops=300_000_000, nbytes=3_000_000,
    )
    ends = exchange(ends)
    out, act, dgated, hidden, dy, back, prior, firsts = call(
        kernel_middle,
        [(full, BF16), (full, BF16), ((rows, 1024), BF16), (full, BF16), (full, BF16), (full, F32), (full, F32), ((N, 8, 128), BF16)],
        [lengths, ends, local, normed, x, go, c_proj, glu_weight, skip, deal_m, back_m, rate2, angle2],
        smem=(0,), flops=1_200_000_000, nbytes=6_000_000,
    )
    firsts = exchange(firsts)
    (wide,) = call(
        kernel_weights, [((N, 8, 768), BF16)], [act, dgated, hidden, dy], flops=400_000_000, nbytes=3_000_000
    )
    wide = exchange(wide)
    in_grad, narrow = call(
        kernel_last, [(full, BF16), ((N, 8, 384), BF16)],
        [lengths, firsts, back, prior, pairs, normed, x, go, dy, b_proj, gain, skip, back_m, rate2, angle2],
        smem=(0,), flops=600_000_000, nbytes=5_000_000,
    )
    narrow = exchange(narrow)
    b_grad, c_grad, glu_grad, small = call(
        kernel_sum, [((4, 512), F32), ((4, 512), F32), ((4, 1024), F32), ((8, 128), F32)], [wide, narrow], flops=2_000_000, nbytes=2_500_000
    )
    return (
        out.reshape(block_in.shape),
        in_grad.reshape(block_in.shape),
        small[0, 0:4],
        small[0, 4:8],
        b_grad,
        c_grad,
        glu_grad,
        small[0, 8:12],
        small[0, 12:14],
        small[0, 14:16],
    )


def solution(mesh):
    tokens = P(None, "seq", None)
    in_specs = (tokens, tokens) + (P(),) * 9
    out_specs = (tokens, tokens, P("seq"), P("seq"), P("seq", None), P("seq", None), P("seq", None), P("seq"), P("seq"), P("seq"))
    return jax.shard_map(body, mesh=mesh, in_specs=in_specs, out_specs=out_specs, check_vma=False)
```

time: 1240 us -> 109 us (0.09)
  local copies, waits for them, and re-layouts: 913 us -> 2.73 us
  waiting for transfers between devices: 120 us -> 13.2 us
  starting transfers between devices: 63.4 us -> 4.67 us
  other arithmetic: 38 us -> 0 us
  between operations: 20.3 us -> 0.66 us
  Pallas kernels: 0 us -> 18.6 us
  matrix products: 15.7 us -> 0 us
    slice x687 -> x0, local copies, waits for them, and re-layouts: 619 us -> none  [the longest x348 441 us: scan_behind(): lax.associative_scan(complex_step, (weight_re, weight_im, grad_pairs[:, 0...]
    pad x208 -> x0, local copies, waits for them, and re-layouts: 122 us -> none  [the longest x104 61.6 us: scan_ahead(): lax.associative_scan(complex_step, (decay_re, decay_im, input_scale[:, No...]
    unnamed x336 -> x2, local copies, waits for them, and re-layouts: 116 us -> 0.01 us
    unnamed x2 -> x0, waiting for transfers between devices: 82 us -> none
    all_to_all x0 -> x3, blocking collectives: none -> 68.5 us  [the longest x1 30.3 us: body(): wide = exchange(wide)]
    unnamed x1 -> x0, blocking collectives: 63.9 us -> none
    all_to_all x8 -> x1, starting transfers between devices: 63.4 us -> 4.67 us  [body(): narrow = exchange(narrow)]
    rev x4 -> x0, local copies, waits for them, and re-layouts: 45.1 us -> none  [scan_behind(): lax.associative_scan(complex_step, (weight_re, weight_im, grad_pairs[:, 0...]
  transfers between devices with their start and end apart: 9 -> 1, of which waited for: 6 -> 1; matrix products, arithmetic and copies ran while one was open for 45% -> 0% of each run, Pallas kernels for 0% -> 3%
where the time goes in v1:
time: 109 us; the launch traced here: 108 us
  blocking collectives  68.5 us (63%)
  Pallas kernels  18.6 us (17%)
  waiting for transfers between devices  13.2 us (12%)
  starting transfers between devices  4.67 us (4%)
  local copies, waits for them, and re-layouts  2.73 us (3%)
    all_to_all x1, blocking collectives, body(): wide = exchange(wide)  30.3 us
    all_to_all x1, blocking collectives, body(): ends = exchange(ends)  22 us
    pallas_call x5, Pallas kernels, call(): pl.pallas_call(kernel, out_shape=[jax.ShapeDtypeStruct(s, d) for s, d in...  18.6 us
    all_to_all x1, blocking collectives, body(): firsts = exchange(firsts)  16.2 us
    all_to_all x1, waiting for transfers between devices, body(): narrow = exchange(narrow)  13.2 us
    all_to_all x1, starting transfers between devices, body(): narrow = exchange(narrow)  4.67 us
  transfers between devices with their start and end apart: 1, of which 1 were waited for; matrix products, arithmetic and copies ran while one was open for 0% of the time, Pallas kernels for 3%

profile of v1, /device:TPU:0, one launch (start us, length us, event | category | flops | bytes accessed | tf_op | source)
XLA Modules:
  0.0 108.4 jit_solution(2321532846312041972)
XLA Ops:
  0.6 3.1 %shard_map.204 = (bf16[256,512]{1,0:T(8,128)(2,1)}, bf16[256,512]{1,0:T(8,128)(2,1)}, f32[256,512]{1,0:T(8,128)}, bf16[128,8,128]{2,1,0:T(8,128)(2,1)}) custom-call(bf16[256,512]{1,0:T(8,128)(2,1)} %bitcast.19, f32[1,512]{1,0:T(1,128)} %bitcast.24, f32[1,512]{1,0:T(1,128)} %bitcast.35, bf16[512,512]{1,0:T(8,128)(2,1)} %b_ref.3, ...), custom_call_target="tpu_custom_call" | custom-call | flops 300000000 | bytes 3000000 | tf_op jit(solution)/shard_map/pallas_call | solution.py:431
  3.7 22.0 %all_to_all.20.ends_ref = bf16[128,8,128]{2,1,0:T(8,128)(2,1)} all-to-all(bf16[128,8,128]{2,1,0:T(8,128)(2,1)} %get-tuple-element.28), channel_id=1, replica_groups=mesh['seq'=128] {'seq'}, dimensions={0} | all-to-all | bytes 524288 | tf_op jit(solution)/shard_map/all_to_all | solution.py:456
  25.7 5.2 %shard_map.205 = (bf16[256,512]{1,0:T(8,128)(2,1)}, bf16[256,512]{1,0:T(8,128)(2,1)}, bf16[256,1024]{1,0:T(8,128)(2,1)}, bf16[256,512]{1,0:T(8,128)(2,1)}, bf16[...) custom-call(s32[2,16]{1,0:T(2,128)} %lengths_ref.3, ...), custom_call_target="tpu_custom_call" | custom-call | flops 1200000000 | bytes 6000000 | tf_op jit(solution)/shard_map/pallas_call | solution.py:431
  30.8 16.2 %all_to_all.21.firsts_ref = bf16[128,8,128]{2,1,0:T(8,128)(2,1)} all-to-all(bf16[128,8,128]{2,1,0:T(8,128)(2,1)} %get-tuple-element.32), channel_id=1, replica_groups=mesh['seq'=128] {'seq'}, dimensions={0} | all-to-all | bytes 524288 | tf_op jit(solution)/shard_map/all_to_all | solution.py:463
  47.1 4.6 %shard_map.206 = (bf16[256,512]{1,0:T(8,128)(2,1)}, bf16[128,8,384]{2,1,0:T(8,128)(2,1)}) custom-call(s32[2,16]{1,0:T(2,128)} %lengths_ref.3, bf16[128,8,128]{2,1,0:T(8,128)(2,1)} %all_to_all.21.firsts_ref, f32[256,512]{1,0:T(8,128)} %get-tuple-element.33.back_ref, f32[256,512]{1,0:T(8,128)} %get-tuple-element.34.prior_ref, ...), custom_call_target="tpu_custom_call" | custom-call | flops 600000000 | bytes 5000000 | tf_op jit(solution)/shard_map/pallas_call | solution.py:431
  51.7 4.7 %all-to-all-start.3 = ((bf16[128,8,384]{2,1,0:T(8,128)(2,1)}), bf16[128,8,384]{2,1,0:T(8,128)(2,1)S(1)}, u32[]{:S(2)}, u32[]{:S(2)}) async-start(bf16[128,8,384]{2,1,0:T(8,128)(2,1)} %get-tuple-element.41), calls=%async_computation.3 | async-start | bytes 1572864 | tf_op jit(solution)/shard_map/all_to_all | solution.py:473
  56.4 3.1 %shard_map.207 = bf16[128,8,768]{2,1,0:T(8,128)(2,1)} custom-call(bf16[256,512]{1,0:T(8,128)(2,1)} %get-tuple-element.38.act_ref, bf16[256,1024]{1,0:T(8,128)(2,1)} %get-tuple-element.39.dgated_ref, bf16[256,512]{1,0:T(8,128)(2,1)} %get-tuple-element.40.hidden_ref, bf16[256,512]{1,0:T(8,128)(2,1)} %get-tuple-element.36.dy_ref), custom_call_target="tpu_custom_call" | custom-call | flops 400000000 | bytes 3000000 | tf_op jit(solution)/shard_map/pallas_call | solution.py:431
  59.4 13.2 %all-to-all-done.3.narrow_ref = bf16[128,8,384]{2,1,0:T(8,128)(2,1)S(1)} async-done(((bf16[128,8,384]{2,1,0:T(8,128)(2,1)}), bf16[128,8,384]{2,1,0:T(8,128)(2,1)S(1)}, u32[]{:S(2)}, u32[]{:S(2)}) %all-to-all-start.3) | async-done | bytes 786464 | tf_op jit(solution)/shard_map/all_to_all | solution.py:473
  72.7 0.0 copy-start
  72.7 30.3 %all_to_all.22.wide_ref = bf16[128,8,768]{2,1,0:T(8,128)(2,1)} all-to-all(bf16[128,8,768]{2,1,0:T(8,128)(2,1)} %shard_map.207), channel_id=1, replica_groups=mesh['seq'=128] {'seq'}, dimensions={0} | all-to-all | bytes 3145728 | tf_op jit(solution)/shard_map/all_to_all | solution.py:467
  103.0 0.0 copy-done
  103.0 2.7 %shard_map.208 = (f32[4,512]{1,0:T(4,128)}, f32[4,512]{1,0:T(4,128)}, f32[4,1024]{1,0:T(4,128)}, f32[8,128]{1,0:T(8,128)}) custom-call(bf16[128,8,768]{2,1,0:T(8,128)(2,1)} %all_to_all.22.wide_ref, bf16[128,8,384]{2,1,0:T(8,128)(2,1)} %copy-done), custom_call_target="tpu_custom_call" | custom-call | flops 2000000 | bytes 2500000 | tf_op jit(solution)/shard_map/pallas_call | solution.py:431
  105.7 1.3 %slice_bitcast_fusion = (f32[2]{0:T(128)}, f32[2]{0:T(128)}) fusion(f32[8,128]{1,0:T(8,128)} %get-tuple-element.42), kind=kLoop, calls=%fused_computation | loop fusion | bytes 32 | tf_op jit(solution)/shard_map/squeeze | solution.py:487
  107.0 1.4 %slice_bitcast_fusion.2 = (f32[4]{0:T(128)}, f32[4]{0:T(128)}, f32[4]{0:T(128)}) fusion(f32[8,128]{1,0:T(8,128)} %get-tuple-element.42), kind=kLoop, calls=%fused_computation.2 | loop fusion | bytes 96 | tf_op jit(solution)/shard_map/squeeze | solution.py:485
Async XLA Ops:
  51.7 21.0 %all-to-all-start.3 = ((bf16[128,8,384]{2,1,0:T(8,128)(2,1)}), bf16[128,8,384]{2,1,0:T(8,128)(2,1)S(1)}, u32[]{:S(2)}, u32[]{:S(2)}) async-start(bf16[128,8,384]{2,1,0:T(8,128)(2,1)} %get-tuple-element.41), calls=%async_computation.3 | async-start | bytes 1572864 | tf_op jit(solution)/shard_map/all_to_all | solution.py:473
  72.7 30.3 %copy-start = (bf16[128,8,384]{2,1,0:T(8,128)(2,1)}, bf16[128,8,384]{2,1,0:T(8,128)(2,1)S(1)}, u32[]{:S(2)}) copy-start(bf16[128,8,384]{2,1,0:T(8,128)(2,1)S(1)} %all-to-all-done.3.narrow_ref) | copy-start | bytes 2359300

commit v2 on v1

--- a/solution.py
+++ b/solution.py
@@ -16,6 +16,7 @@
 MICRO = 2
 HALVES = 2
 N = 128
+CHIPS = 64
 
 
 def deal():
@@ -320,28 +321,43 @@
 
 def chunk_rows(left, right):
     w = left.shape[1]
-    a = left.reshape(64, 8, w)
-    b = right.reshape(64, 8, w)
-    low = rows_iota((64, 8, w)) < 4
-    even = jnp.where(low, a, pltpu.roll(b, 4, 1))
-    odd = jnp.where(low, pltpu.roll(a, 4, 1), b)
-    return jnp.stack([even, odd], axis=1).reshape(128, 8, w)
-
-
-def kernel_weights(act_ref, dgated_ref, hidden_ref, dy_ref, out_ref):
+    a = left.reshape(CHIPS, 8, w)
+    b = right.reshape(CHIPS, 8, w)
+    low = rows_iota((CHIPS, 8, w)) < 4
+    return jnp.where(low, a, pltpu.roll(b, 4, 1)), jnp.where(low, pltpu.roll(a, 4, 1), b)
+
+
+def kernel_weights(act_ref, dgated_ref, hidden_ref, dy_ref, keep_ref, send_ref):
+    core = lax.axis_index("seq") % 2
     glu = dot_tn(act_ref[...], dgated_ref[...])
     c = dot_tn(hidden_ref[...], dy_ref[...])
-    out_ref[...] = chunk_rows(glu[:, :768], jnp.concatenate([glu[:, 768:], c], axis=1)).astype(BF16)
-
-
-def small_chunks(vectors, channels):
-    dest = lax.broadcasted_iota(jnp.int32, (N, 512), 0)
-    feature = lax.broadcasted_iota(jnp.int32, (N, 512), 1)
+    even, odd = chunk_rows(glu[:, :768], jnp.concatenate([glu[:, 768:], c], axis=1))
+    keep_ref[...] = jnp.where(core == 0, even, odd).astype(BF16)
+    send_ref[...] = jnp.where(core == 0, odd, even).astype(BF16)
+
+
+def kernel_pack(keep_ref, got_ref, out_ref):
+    out_ref[:, :, 0:768] = (keep_ref[...].astype(F32) + got_ref[...].astype(F32)).astype(BF16)
+
+
+def kernel_pack_rest(keep_ref, got_ref, buffer_ref, out_ref, rest, sem):
+    del buffer_ref
+    rest[:, :, 0:256] = (keep_ref[:, :, 0:256].astype(F32) + got_ref[:, :, 0:256].astype(F32)).astype(BF16)
+    low = rows_iota((CHIPS, 8, 128)) < 4
+    rest[:, :, 256:384] = jnp.where(low, keep_ref[:, :, 256:384].astype(F32), got_ref[:, :, 256:384].astype(F32)).astype(BF16)
+    copy = pltpu.make_async_copy(rest, out_ref.at[:, :, 768:1152], sem)
+    copy.start()
+    copy.wait()
+
+
+def small_chunks(vectors, channels, core):
+    dest = 2 * lax.broadcasted_iota(jnp.int32, (CHIPS, 512), 0) + core
+    feature = lax.broadcasted_iota(jnp.int32, (CHIPS, 512), 1)
     lane = lax.broadcasted_iota(jnp.int32, (512, 128), 1)
     row = lax.broadcasted_iota(jnp.int32, (512, 128), 0)
     by_four = ((feature // 4) == dest, row % 4)
     by_two = (((feature % 256) // 2) == dest, row % 2 + 2 * (row // 256))
-    total = jnp.zeros((N, 128), F32)
+    total = jnp.zeros((CHIPS, 128), F32)
     for v, vec in enumerate(vectors + [channels]):
         mine, inner = by_two if v == len(vectors) else by_four
         high = vec.astype(BF16).astype(F32)
@@ -355,9 +371,11 @@
 
 def kernel_last(
     lengths_ref, firsts_ref, back_ref, prior_ref, pairs_ref, normed_ref, x_ref, go_ref, dy_ref, b_ref, gain_ref, skip_ref, deal_back_ref,
-    log_rate_ref, angle_ref, in_grad_ref, out_ref,
+    log_rate_ref, angle_ref, buffer_ref, in_grad_ref, keep_ref, send_ref,
 ):
+    del buffer_ref
     me = lax.axis_index("seq")
+    core = me % 2
     _, behind = distance_tiles(lengths_ref, me)
     lams = lam_tiles(log_rate_ref, angle_ref)
     pows = [[conj(p) for p in per_half] for per_half in carry_pows(lams)]
@@ -404,35 +422,46 @@
     gain_grad = col(dnormed * xhat)
     bias_grad = col(dnormed)
     skip_grad = col(dy * normed.astype(F32))
-    smalls = small_chunks([gain_grad, bias_grad, skip_grad], jnp.concatenate(rates + angles, axis=1))
-    chunks = chunk_rows(b_grad[:, :256], b_grad[:, 256:])
-    out_ref[:, :, 0:256] = chunks.astype(BF16)
-    out_ref[:, :, 256:384] = jnp.broadcast_to(smalls[:, None, :], (N, 8, 128)).astype(BF16)
+    channels = jnp.concatenate(rates + angles, axis=1)
+    even, odd = chunk_rows(b_grad[:, :256], b_grad[:, 256:])
+    keep_ref[:, :, 0:256] = jnp.where(core == 0, even, odd).astype(BF16)
+    send_ref[:, :, 0:256] = jnp.where(core == 0, odd, even).astype(BF16)
+    for ref, mine in ((keep_ref, core), (send_ref, 1 - core)):
+        smalls = small_chunks([gain_grad, bias_grad, skip_grad], channels, mine)
+        ref[:, :, 256:384] = jnp.broadcast_to(smalls[:, None, :], (CHIPS, 8, 128)).astype(BF16)
     dx = dnormed * gain_ref[...]
     m1 = jnp.mean(dx, axis=1, keepdims=True)
     m2 = jnp.mean(dx * xhat, axis=1, keepdims=True)
     in_grad_ref[...] = (go + rstd * (dx - m1 - xhat * m2)).astype(BF16)
 
 
-def kernel_sum(wide_ref, narrow_ref, b_ref, c_ref, glu_ref, small_ref):
-    wide = jnp.sum(wide_ref[...].astype(F32), axis=0)
-    glu_ref[:, 0:768] = wide[0:4, :]
-    glu_ref[:, 768:1024] = wide[4:8, 0:256]
-    c_ref[...] = wide[4:8, 256:768]
-    narrow = jnp.sum(narrow_ref[...].astype(F32), axis=0)
-    b_ref[:, 0:256] = narrow[0:4, 0:256]
-    b_ref[:, 256:512] = narrow[4:8, 0:256]
-    small = narrow[:, 256:384]
-    small_ref[...] = small + pltpu.roll(small, 64, 1)
-
-
-def call(kernel, outs, args, smem=(), flops=0, nbytes=0):
-    space = lambda i: pltpu.SMEM if i in smem else pltpu.VMEM
+def kernel_sum(parts_ref, b_ref, c_ref, glu_ref, gain_ref, bias_ref, skip_ref, rate_ref, angle_ref):
+    total = jnp.sum(parts_ref[...].astype(F32), axis=0)
+    glu_ref[:, 0:768] = total[0:4, 0:768]
+    glu_ref[:, 768:1024] = total[4:8, 0:256]
+    c_ref[...] = total[4:8, 256:768]
+    b_ref[:, 0:256] = total[0:4, 768:1024]
+    b_ref[:, 256:512] = total[4:8, 768:1024]
+    small = total[:, 1024:1152]
+    small = small + pltpu.roll(small, 4, 0)
+    small = small + pltpu.roll(small, 64, 1)
+    for ref, at in ((gain_ref, 0), (bias_ref, 4), (skip_ref, 8), (rate_ref, 12), (angle_ref, 14)):
+        ref[...] = (pltpu.roll(small, 128 - at, 1) if at else small)[0:1, 0 : ref.shape[1]]
+
+
+def call(kernel, outs, args, smem=(), anywhere=(), out_any=(), scratch=(), alias=None, flops=0, nbytes=0):
+    def space(i):
+        if i in smem:
+            return pltpu.SMEM
+        return pl.ANY if i in anywhere else pltpu.VMEM
+
     return pl.pallas_call(
         kernel,
         out_shape=[jax.ShapeDtypeStruct(s, d) for s, d in outs],
         in_specs=[pl.BlockSpec(memory_space=space(i)) for i in range(len(args))],
-        out_specs=[pl.BlockSpec(memory_space=pltpu.VMEM) for _ in outs],
+        out_specs=[pl.BlockSpec(memory_space=pl.ANY if i in out_any else pltpu.VMEM) for i in range(len(outs))],
+        scratch_shapes=list(scratch),
+        input_output_aliases=alias or {},
         compiler_params=pltpu.CompilerParams(vmem_limit_bytes=VMEM_LIMIT),
         cost_estimate=pl.CostEstimate(flops=flops, bytes_accessed=nbytes, transcendentals=0),
     )(*args)
@@ -461,30 +490,39 @@
         smem=(0,), flops=1_200_000_000, nbytes=6_000_000,
     )
     firsts = exchange(firsts)
-    (wide,) = call(
-        kernel_weights, [((N, 8, 768), BF16)], [act, dgated, hidden, dy], flops=400_000_000, nbytes=3_000_000
-    )
-    wide = exchange(wide)
-    in_grad, narrow = call(
-        kernel_last, [(full, BF16), ((N, 8, 384), BF16)],
-        [lengths, firsts, back, prior, pairs, normed, x, go, dy, b_proj, gain, skip, back_m, rate2, angle2],
-        smem=(0,), flops=600_000_000, nbytes=5_000_000,
-    )
-    narrow = exchange(narrow)
-    b_grad, c_grad, glu_grad, small = call(
-        kernel_sum, [((4, 512), F32), ((4, 512), F32), ((4, 1024), F32), ((8, 128), F32)], [wide, narrow], flops=2_000_000, nbytes=2_500_000
+    swap = functools.partial(lax.ppermute, axis_name="seq", perm=[(i, i ^ 1) for i in range(N)])
+    same_core = [[2 * t + core for t in range(CHIPS)] for core in range(2)]
+    wide_shape, rest_shape = (CHIPS, 8, 768), (CHIPS, 8, 384)
+    keep, send = call(
+        kernel_weights, [(wide_shape, BF16), (wide_shape, BF16)], [act, dgated, hidden, dy], flops=400_000_000, nbytes=3_000_000
+    )
+    (packed,) = call(kernel_pack, [((CHIPS, 8, 1152), BF16)], [keep, swap(send)], flops=1_000_000, nbytes=2_400_000)
+    in_grad, keep, send = call(
+        kernel_last, [(full, BF16), (rest_shape, BF16), (rest_shape, BF16)],
+        [lengths, firsts, back, prior, pairs, normed, x, go, dy, b_proj, gain, skip, back_m, rate2, angle2, packed],
+        smem=(0,), anywhere=(15,), flops=600_000_000, nbytes=5_000_000,
+    )
+    (packed,) = call(
+        kernel_pack_rest, [((CHIPS, 8, 1152), BF16)], [keep, swap(send), packed], anywhere=(2,), out_any=(0,), alias={2: 0},
+        scratch=[pltpu.VMEM(rest_shape, BF16), pltpu.SemaphoreType.DMA], flops=1_000_000, nbytes=1_200_000,
+    )
+    parts = lax.all_to_all(packed, "seq", split_axis=0, concat_axis=0, tiled=True, axis_index_groups=same_core)
+    b_grad, c_grad, glu_grad, gain_grad, bias_grad, skip_grad, rate_grad, angle_grad = call(
+        kernel_sum,
+        [((4, 512), F32), ((4, 512), F32), ((4, 1024), F32)] + [((1, w), F32) for w in (4, 4, 4, 2, 2)],
+        [parts], flops=1_000_000, nbytes=1_300_000,
     )
     return (
         out.reshape(block_in.shape),
         in_grad.reshape(block_in.shape),
-        small[0, 0:4],
-        small[0, 4:8],
+        gain_grad.reshape(4),
+        bias_grad.reshape(4),
         b_grad,
         c_grad,
         glu_grad,
-        small[0, 8:12],
-        small[0, 12:14],
-        small[0, 14:16],
+        skip_grad.reshape(4),
+        rate_grad.reshape(2),
+        angle_grad.reshape(2),
     )
 
 

time: 109 us -> 88.3 us (0.81)
  blocking collectives: 68.5 us -> 48.1 us
  Pallas kernels: 18.6 us -> 22.8 us
  waiting for transfers between devices: 13.2 us -> 9.18 us
    all_to_all x2 -> x1, blocking collectives: 46.5 us -> 26.1 us  [body(): lax.all_to_all(packed, 'seq', split_axis=0, concat_axis=0, tiled=True, ax...]
    all_to_all x1, waiting for transfers between devices: 13.2 us -> 7.25 us  [body(): firsts = exchange(firsts)]
    pallas_call x5 -> x7, Pallas kernels: 18.6 us -> 22.8 us  [call(): pl.pallas_call(kernel, out_shape=[jax.ShapeDtypeStruct(s, d) for s, d in...]
    squeeze x2 -> x0, local copies, waits for them, and re-layouts: 2.73 us -> none  [the longest x1 1.39 us: body(): small[0, 8:12]]
    unnamed x2 -> x6, local copies, waits for them, and re-layouts: 0.01 us -> 2.35 us
    ppermute x0 -> x2, waiting for transfers between devices: none -> 1.93 us  [body(): swap(send)]
  transfers between devices with their start and end apart: 1 -> 3, of which waited for: 1 -> 2; matrix products, arithmetic and copies ran while one was open for 0% -> 0% of each run, Pallas kernels for 3% -> 3%
where the time goes in v2:
time: 88.3 us; the launch traced here: 87.8 us
  blocking collectives  48.1 us (54%)
  Pallas kernels  22.8 us (26%)
  waiting for transfers between devices  9.18 us (10%)
  starting transfers between devices  4.79 us (5%)
  local copies, waits for them, and re-layouts  2.35 us (3%)
    all_to_all x1, blocking collectives, body(): lax.all_to_all(packed, 'seq', split_axis=0, concat_axis=0, tiled=True, ax...  26.1 us
    pallas_call x7, Pallas kernels, call(): pl.pallas_call(kernel, out_shape=[jax.ShapeDtypeStruct(s, d) for s, d in...  22.8 us
    all_to_all x1, blocking collectives, body(): ends = exchange(ends)  22 us
    all_to_all x1, waiting for transfers between devices, body(): firsts = exchange(firsts)  7.25 us
    all_to_all x1, starting transfers between devices, body(): firsts = exchange(firsts)  4.79 us
    unnamed x6, local copies, waits for them, and re-layouts  2.35 us
    ppermute x2, waiting for transfers between devices, body(): swap(send)  1.93 us
  transfers between devices with their start and end apart: 3, of which 2 were waited for; matrix products, arithmetic and copies ran while one was open for 0% of the time, Pallas kernels for 3%

profile of v2, /device:TPU:0, one launch (start us, length us, event | category | flops | bytes accessed | tf_op | source)
XLA Modules:
  0.0 87.8 jit_solution(18095611418561716602)
XLA Ops:
  0.6 3.1 %shard_map.204 = (bf16[256,512]{1,0:T(8,128)(2,1)}, bf16[256,512]{1,0:T(8,128)(2,1)}, f32[256,512]{1,0:T(8,128)}, bf16[128,8,128]{2,1,0:T(8,128)(2,1)}) custom-call(bf16[256,512]{1,0:T(8,128)(2,1)} %bitcast.14, f32[1,512]{1,0:T(1,128)} %bitcast.19, f32[1,512]{1,0:T(1,128)} %bitcast.30, bf16[512,512]{1,0:T(8,128)(2,1)} %b_ref.3, ...), custom_call_target="tpu_custom_call" | custom-call | flops 300000000 | bytes 3000000 | tf_op jit(solution)/shard_map/pallas_call | solution.py:458
  3.7 22.0 %all_to_all.15.ends_ref = bf16[128,8,128]{2,1,0:T(8,128)(2,1)} all-to-all(bf16[128,8,128]{2,1,0:T(8,128)(2,1)} %get-tuple-element.35), channel_id=1, replica_groups=mesh['seq'=128] {'seq'}, dimensions={0} | all-to-all | bytes 524288 | tf_op jit(solution)/shard_map/all_to_all | solution.py:485
  25.7 5.2 %shard_map.205 = (bf16[256,512]{1,0:T(8,128)(2,1)}, bf16[256,512]{1,0:T(8,128)(2,1)}, bf16[256,1024]{1,0:T(8,128)(2,1)}, bf16[256,512]{1,0:T(8,128)(2,1)}, bf16[...) custom-call(s32[2,16]{1,0:T(2,128)} %lengths_ref.3, ...), custom_call_target="tpu_custom_call" | custom-call | flops 1200000000 | bytes 6000000 | tf_op jit(solution)/shard_map/pallas_call | solution.py:458
  30.8 3.1 %shard_map.206 = (bf16[64,8,768]{2,1,0:T(8,128)(2,1)}, bf16[64,8,768]{2,1,0:T(8,128)(2,1)}) custom-call(bf16[256,512]{1,0:T(8,128)(2,1)} %get-tuple-element.44.act_ref, bf16[256,1024]{1,0:T(8,128)(2,1)} %get-tuple-element.45.dgated_ref, bf16[256,512]{1,0:T(8,128)(2,1)} %get-tuple-element.46.hidden_ref, bf16[256,512]{1,0:T(8,128)(2,1)} %get-tuple-element.43.dy_ref), custom_call_target="tpu_custom_call" | custom-call | flops 400000000 | bytes 3000000 | tf_op jit(solution)/shard_map/pallas_call | solution.py:458
  34.0 0.0 collective-permute-start
  34.0 4.8 %all-to-all-start.1 = ((bf16[128,8,128]{2,1,0:T(8,128)(2,1)}), bf16[128,8,128]{2,1,0:T(8,128)(2,1)S(1)}, u32[]{:S(2)}, u32[]{:S(2)}) async-start(bf16[128,8,128]{2,1,0:T(8,128)(2,1)} %get-tuple-element.39), calls=%async_computation.1 | async-start | bytes 524288 | tf_op jit(solution)/shard_map/all_to_all | solution.py:492
  38.8 0.0 collective-permute-done.got_ref
  38.8 0.0 copy-start.1
  38.8 0.9 %copy-done.1 = bf16[64,8,768]{2,1,0:T(8,128)(2,1)} copy-done((bf16[64,8,768]{2,1,0:T(8,128)(2,1)}, bf16[64,8,768]{2,1,0:T(8,128)(2,1)S(1)}, u32[]{:S(2)}) %copy-start.1) | copy-done | bytes 786456
  39.7 2.6 %shard_map.207.buffer_ref = bf16[64,8,1152]{2,1,0:T(8,128)(2,1)} custom-call(bf16[64,8,768]{2,1,0:T(8,128)(2,1)} %get-tuple-element.47.keep_ref, bf16[64,8,768]{2,1,0:T(8,128)(2,1)} %copy-done.1), custom_call_target="tpu_custom_call" | custom-call | flops 1000000 | bytes 2400000 | tf_op jit(solution)/shard_map/pallas_call | solution.py:458
  42.2 7.2 %all-to-all-done.1.firsts_ref = bf16[128,8,128]{2,1,0:T(8,128)(2,1)S(1)} async-done(((bf16[128,8,128]{2,1,0:T(8,128)(2,1)}), bf16[128,8,128]{2,1,0:T(8,128)(2,1)S(1)}, u32[]{:S(2)}, u32[]{:S(2)}) %all-to-all-start.1) | async-done | bytes 262176 | tf_op jit(solution)/shard_map/all_to_all | solution.py:492
  49.5 0.0 copy-start
  49.5 0.7 copy-done
  50.2 4.7 %shard_map.208 = (bf16[256,512]{1,0:T(8,128)(2,1)}, bf16[64,8,384]{2,1,0:T(8,128)(2,1)}, bf16[64,8,384]{2,1,0:T(8,128)(2,1)}) custom-call(s32[2,16]{1,0:T(2,128)} %lengths_ref.3, bf16[128,8,128]{2,1,0:T(8,128)(2,1)} %copy-done, f32[256,512]{1,0:T(8,128)} %get-tuple-element.40.back_ref, f32[256,512]{1,0:T(8,128)} %get-tuple-element.41.prior_ref, ...), custom_call_target="tpu_custom_call" | custom-call | flops 600000000 | bytes 5000000 | tf_op jit(solution)/shard_map/pallas_call | solution.py:458
  54.9 0.0 collective-permute-start.1
  54.9 1.9 %collective-permute-done.1.got_ref = bf16[64,8,384]{2,1,0:T(8,128)(2,1)S(1)} collective-permute-done((bf16[64,8,384]{2,1,0:T(8,128)(2,1)}, bf16[64,8,384]{2,1,0:T(8,128)(2,1)S(1)}, u32[]{:S(2)}, u32[]{:S(2)}) %collective-permute-start.1) | collective-permute-done | bytes 393248 | tf_op jit(solution)/shard_map/ppermute | solution.py:506
  56.9 0.0 copy-start.2
  56.9 0.7 copy-done.2
  57.6 2.0 %shard_map.209 = bf16[64,8,1152]{2,1,0:T(8,128)(2,1)} custom-call(bf16[64,8,384]{2,1,0:T(8,128)(2,1)} %get-tuple-element.50.keep_ref, bf16[64,8,384]{2,1,0:T(8,128)(2,1)} %copy-done.2, bf16[64,8,1152]{2,1,0:T(8,128)(2,1)} %shard_map.207.buffer_ref), custom_call_target="tpu_custom_call", output_to_operand_aliasing={{}: (2, {})} | custom-call | flops 1000000 | bytes 1200000 | tf_op jit(solution)/shard_map/pallas_call | solution.py:458
  59.6 26.1 %all_to_all.16.parts_ref = bf16[64,8,1152]{2,1,0:T(8,128)(2,1)} all-to-all(bf16[64,8,1152]{2,1,0:T(8,128)(2,1)} %shard_map.209), channel_id=1, replica_groups={{0,2,4,6,8,10,12,14,16,18,20,22,24,26,28,30,32,34,36,38,40,42,44,46,48,..., dimensions={0} | all-to-all | bytes 2359296 | tf_op jit(solution)/shard_map/all_to_all | solution.py:509
  85.7 2.1 %shard_map.210 = (f32[4,512]{1,0:T(4,128)}, f32[4,512]{1,0:T(4,128)}, f32[4,1024]{1,0:T(4,128)}, f32[1,4]{1,0:T(1,128)}, f32[1,4]{1,0:T(1,128)}, /*index=5*/f32[1,4]{1,0:T(1,128)}, f32[1,2]{1,0:T(1,128)}, f32[1,2]{1,0:T(1,128)}) custom-call(bf16[64,8,1152]{2,1,0:T(8,128)(2,1)} %all_to_all.16.parts_ref), custom_call_target="tpu_custom_call" | custom-call | flops 1000000 | bytes 1300000 | tf_op jit(solution)/shard_map/pallas_call | solution.py:458
Async XLA Ops:
  34.0 4.8 %collective-permute-start = (bf16[64,8,768]{2,1,0:T(8,128)(2,1)}, bf16[64,8,768]{2,1,0:T(8,128)(2,1)S(1)}, u32[]{:S(2)}, u32[]{:S(2)}) collective-permute-start(bf16[64,8,768]{2,1,0:T(8,128)(2,1)} %get-tuple-element.48), channel_id=1, source_target_pairs={{0,1},{1,0},{2,3},{3,2},{4,5},{5,4},{6,7},{7,6},{8,9},{9,8},{10,11... | collective-permute-start | bytes 2359304 | tf_op jit(solution)/shard_map/ppermute | solution.py:499
  34.0 15.5 %all-to-all-start.1 = ((bf16[128,8,128]{2,1,0:T(8,128)(2,1)}), bf16[128,8,128]{2,1,0:T(8,128)(2,1)S(1)}, u32[]{:S(2)}, u32[]{:S(2)}) async-start(bf16[128,8,128]{2,1,0:T(8,128)(2,1)} %get-tuple-element.39), calls=%async_computation.1 | async-start | bytes 524288 | tf_op jit(solution)/shard_map/all_to_all | solution.py:492
  38.8 0.9 %copy-start.1 = (bf16[64,8,768]{2,1,0:T(8,128)(2,1)}, bf16[64,8,768]{2,1,0:T(8,128)(2,1)S(1)}, u32[]{:S(2)}) copy-start(bf16[64,8,768]{2,1,0:T(8,128)(2,1)S(1)} %collective-permute-done.got_ref) | copy-start | bytes 2359300
  49.5 0.7 copy-start
  54.9 1.9 %collective-permute-start.1 = (bf16[64,8,384]{2,1,0:T(8,128)(2,1)}, bf16[64,8,384]{2,1,0:T(8,128)(2,1)S(1)}, u32[]{:S(2)}, u32[]{:S(2)}) collective-permute-start(bf16[64,8,384]{2,1,0:T(8,128)(2,1)} %get-tuple-element.51), channel_id=1, source_target_pairs={{0,1},{1,0},{2,3},{3,2},{4,5},{5,4},{6,7},{7,6},{8,9},{9,8},{10,11... | collective-permute-start | bytes 1179656 | tf_op jit(solution)/shard_map/ppermute | solution.py:506
  56.9 0.7 copy-start.2

commit v3 on v1

v3 whole, which is shorter than its diff:
```python
import functools

import jax
import jax.numpy as jnp
import numpy as np
from jax import lax
from jax.experimental import pallas as pl
from jax.experimental.pallas import tpu as pltpu
from jax.sharding import PartitionSpec as P

F32 = jnp.float32
BF16 = jnp.bfloat16
VMEM_LIMIT = 40 * 1024 * 1024
TOK = 128
GROUPS = TOK // 8
MICRO = 2
HALVES = 2
N = 128
CHIPS = 64


def deal():
    out = np.zeros((256, 256), np.float32)
    for n in range(128):
        out[2 * n, n] = 1.0
        out[2 * n + 1, 128 + n] = 1.0
    return out


def dot(a, b):
    return jnp.dot(a, b, preferred_element_type=F32)


def dot_tn(a, b):
    return lax.dot_general(a, b, (((0,), (0,)), ((), ())), preferred_element_type=F32)


def dot_nt(a, b):
    return lax.dot_general(a, b, (((1,), (1,)), ((), ())), preferred_element_type=F32)


def cmul(a, b):
    return (a[0] * b[0] - a[1] * b[1], a[0] * b[1] + a[1] * b[0])


def conj(a):
    return (a[0], -a[1])


def rows_iota(shape=(8, 128)):
    return lax.broadcasted_iota(jnp.int32, shape, len(shape) - 2)


def params(log_rate, angle):
    u = jnp.exp(log_rate)
    r = jnp.exp(-u)
    lam = (r * jnp.cos(angle), r * jnp.sin(angle))
    w = 2.0 * u
    small = jnp.minimum(w, 0.5)
    poly = 1.0 - small * (1.0 / 11.0)
    for k in range(10, 1, -1):
        poly = 1.0 - small * (1.0 / k) * poly
    gap = jnp.where(w < 0.5, small * poly, 1.0 - jnp.exp(-w))
    scale = jnp.sqrt(gap)
    return u, r, lam, scale


def powers(lam, count):
    out = [lam]
    for _ in range(count):
        out.append(cmul(out[-1], out[-1]))
    return out


def lam_tiles(log_rate_ref, angle_ref):
    out = []
    for half in range(HALVES):
        lr = jnp.broadcast_to(log_rate_ref[half : half + 1, :], (8, 128))
        an = jnp.broadcast_to(angle_ref[half : half + 1, :], (8, 128))
        out.append(params(lr, an))
    return out


def scan_tables(pows, reverse):
    row = rows_iota()
    pos = (7 - row) if reverse else row
    levels = []
    for s, p in ((1, pows[0]), (2, pows[1]), (4, pows[2])):
        keep = pos >= s
        levels.append((s, (jnp.where(keep, p[0], 0.0), jnp.where(keep, p[1], 0.0))))
    e = pos + 1
    table = (jnp.ones((8, 128), F32), jnp.zeros((8, 128), F32))
    for bit in range(4):
        on = (lax.shift_right_logical(e, bit) & 1) == 1
        table = cmul(table, (jnp.where(on, pows[bit][0], 1.0), jnp.where(on, pows[bit][1], 0.0)))
    return levels, table


def group_scan(x, levels, reverse):
    xr, xi = x
    for s, (mr, mi) in levels:
        shift = 8 - s if reverse else s
        rr = pltpu.roll(xr, shift, 1)
        ri = pltpu.roll(xi, shift, 1)
        xr, xi = xr + (mr * rr - mi * ri), xi + (mr * ri + mi * rr)
    return xr, xi


def tile_rows(parts):
    rows = []
    for comp in range(2):
        for micro in range(MICRO):
            for half in range(HALVES):
                rows.append(parts[(micro, half)][comp])
    return jnp.concatenate(rows, axis=0)


def tile_lam(p):
    row = rows_iota()
    odd = (row & 1) == 1
    re = jnp.where(odd, p[1][0], p[0][0])
    im = jnp.where(odd, p[1][1], p[0][1])
    return re, jnp.where(row < 4, -im, im)


def tile_mul(c, coef):
    return c * coef[0] + pltpu.roll(c, 4, 0) * coef[1]


def gather_carry(ends_ref, me, step, dmax, coef, coef8):
    chains = []
    for chain in range(8):
        acc = jnp.zeros((8, 128), F32)
        for i in range(7, -1, -1):
            d = chain * 8 + i
            at = jnp.clip(me + step * (1 + d), 0, N - 1)
            e = ends_ref[at, 0].astype(F32)
            e = jnp.where(d <= dmax, e, 0.0)
            acc = e if i == 7 else tile_mul(acc, coef) + e
        chains.append(acc)
    total = chains[7]
    for chain in range(6, -1, -1):
        total = tile_mul(total, coef8) + chains[chain]
    return total


def segment(lengths_ref, micro, base):
    first = jnp.int32(0)
    last = jnp.int32(N * TOK)
    at = jnp.int32(0)
    for slot in range(16):
        first = jnp.where(at <= base, jnp.maximum(first, at), first)
        last = jnp.where(at > base, jnp.minimum(last, at), last)
        at = at + lengths_ref[micro, slot]
    return first, last


def distance_tiles(lengths_ref, me):
    base = me * TOK
    row = rows_iota()
    second = (row & 2) == 2
    ahead, behind = [], []
    for micro in range(MICRO):
        first, last = segment(lengths_ref, micro, base)
        ahead.append((base - first) // TOK - 1)
        behind.append((last - base) // TOK - 2)
    pick = lambda two: jnp.where(second, two[1], two[0])
    return pick(ahead), pick(behind)


def groups_of(value, micro_groups=MICRO * GROUPS):
    return value.reshape(micro_groups, 8, 128)


def split_channels(value):
    out = []
    for half in range(HALVES):
        c = 256 * half
        out.append((groups_of(value[:, c : c + 128]), groups_of(value[:, c + 128 : c + 256])))
    return out


def join_channels(halves):
    cols = []
    for re, im in halves:
        cols.append(re.reshape(MICRO * TOK, 128))
        cols.append(im.reshape(MICRO * TOK, 128))
    return jnp.concatenate(cols, axis=1)


def permute(value_bf, matrix):
    return jnp.concatenate([dot(value_bf[:, :256], matrix), dot(value_bf[:, 256:], matrix)], axis=1)


def layer_norm(x):
    mean = jnp.mean(x, axis=1, keepdims=True)
    centered = x - mean
    var = jnp.mean(centered * centered, axis=1, keepdims=True)
    rstd = lax.rsqrt(var + 1e-05)
    return centered * rstd, rstd


def chain_from(x, micro, step8, init, reverse):
    before = {}
    v = init
    order = range(GROUPS - 1, -1, -1) if reverse else range(GROUPS)
    for g in order:
        before[g] = v
        xr, xi = x[0][micro * GROUPS + g], x[1][micro * GROUPS + g]
        if v is None:
            v = (xr, xi)
        else:
            m = cmul(v, step8)
            v = (xr + m[0], xi + m[1])
    return before, v


def edge_bcast(pair, edge):
    return tuple(jnp.broadcast_to(p[edge : edge + 1, :], (8, 128)) for p in pair)


class Ports:
    def __init__(self, ins, outs, refs):
        n_in, n_out = len(ins), len(outs)
        scratch = list(refs[n_in + n_out :])
        self.refs, self.pending, self.leaving = {}, {}, []
        self.out_copies = {}
        held_in = [(name, ref) for (name, _, mode), ref in zip(ins, refs) if mode == "hbm"]
        held_out = [(name, ref) for (name, _, _, mode), ref in zip(outs, refs[n_in:]) if mode == "hbm"]
        for (name, _, _mode), ref in zip(ins, refs):
            self.refs[name] = ref
        for (name, _, _, _mode), ref in zip(outs, refs[n_in:]):
            self.refs[name] = ref
        sems = scratch[-1] if held_in or held_out else None
        for i, (name, ref) in enumerate(held_in):
            copy = pltpu.make_async_copy(ref, scratch[i], sems.at[i])
            copy.start()
            self.pending[name] = copy
            self.refs[name] = scratch[i]
        for j, (name, ref) in enumerate(held_out):
            i = len(held_in) + j
            self.refs[name] = scratch[i]
            self.out_copies[name] = pltpu.make_async_copy(scratch[i], ref, sems.at[i])

    def ref(self, name):
        if name in self.pending:
            self.pending.pop(name).wait()
        return self.refs[name]

    def get(self, name):
        return self.ref(name)[...]

    def put(self, name, value):
        self.refs[name][...] = value
        self.send(name)

    def send(self, name):
        if name in self.out_copies:
            self.out_copies[name].start()
            self.leaving.append(name)

    def finish(self):
        for name in list(self.pending):
            self.ref(name)
        for name in self.leaving:
            self.out_copies[name].wait()


def call(kernel, ins, outs, extra=(), flops=0, nbytes=0):
    def run(*refs):
        n_extra = len(extra)
        ports = Ports(ins, outs, refs[: len(refs) - n_extra] if n_extra else refs)
        kernel(ports, *(refs[len(refs) - n_extra :] if n_extra else ()))
        ports.finish()

    spaces = {"hbm": pl.ANY, "vmem": pltpu.VMEM, "auto": pltpu.VMEM, "smem": pltpu.SMEM}
    args = []
    for _, array, mode in ins:
        if mode == "hbm":
            array = pltpu.with_memory_space_constraint(array, pltpu.HBM)
        elif mode == "vmem":
            array = pltpu.with_memory_space_constraint(array, pltpu.VMEM)
        args.append(array)
    shapes = []
    for _, shape, kind, mode in outs:
        shapes.append(pltpu.VMEM(shape, kind) if mode == "vmem" else jax.ShapeDtypeStruct(shape, kind))
    held = [(a.shape, a.dtype) for _, a, mode in ins if mode == "hbm"] + [(s, d) for _, s, d, mode in outs if mode == "hbm"]
    scratch = [pltpu.VMEM(s, d) for s, d in held]
    if held:
        scratch.append(pltpu.SemaphoreType.DMA((len(held),)))
    return pl.pallas_call(
        run,
        out_shape=shapes,
        in_specs=[pl.BlockSpec(memory_space=spaces[mode]) for _, _, mode in ins],
        out_specs=[pl.BlockSpec(memory_space=spaces[mode]) for _, _, _, mode in outs],
        scratch_shapes=scratch + list(extra),
        compiler_params=pltpu.CompilerParams(vmem_limit_bytes=VMEM_LIMIT),
        cost_estimate=pl.CostEstimate(flops=flops, bytes_accessed=nbytes, transcendentals=0),
    )(*args)


def chunk_rows(left, right):
    w = left.shape[1]
    a = left.reshape(CHIPS, 8, w)
    b = right.reshape(CHIPS, 8, w)
    low = rows_iota((CHIPS, 8, w)) < 4
    return jnp.where(low, a, pltpu.roll(b, 4, 1)), jnp.where(low, pltpu.roll(a, 4, 1), b)


def kernel_first(io):
    x = io.get("x").astype(F32)
    xhat, _ = layer_norm(x)
    normed = (xhat * io.get("gain") + io.get("bias")).astype(BF16)
    io.put("normed", normed)
    proj = dot(normed, io.get("b")).astype(BF16)
    pairs = permute(proj, io.get("deal"))
    io.put("pairs", pairs.astype(BF16))
    halves = split_channels(pairs)
    lams = lam_tiles(io.ref("log_rate"), io.ref("angle"))
    parts, scanned = {}, []
    for half in range(HALVES):
        _, _, lam, scale = lams[half]
        pows = powers(lam, 3)
        levels, _ = scan_tables(pows, False)
        re, im = halves[half]
        x8 = group_scan((re * scale, im * scale), levels, False)
        scanned.append(x8)
        for micro in range(MICRO):
            _, v = chain_from(x8, micro, pows[3], None, False)
            parts[(micro, half)] = (v[0][7:8, :], v[1][7:8, :])
    io.put("local", join_channels(scanned))
    ends = io.ref("ends")
    ends[:, 0] = jnp.broadcast_to(tile_rows(parts).astype(BF16)[None], (N, 8, 128))
    even, odd = chunk_rows(xhat[:TOK].T, xhat[TOK:].T)
    ends[:, 1] = jnp.stack([even, odd], axis=1).reshape(N, 8, 128).astype(BF16)


def tile_row(tile, comp, micro, half):
    at = comp * 4 + micro * 2 + half
    return jnp.broadcast_to(tile[at : at + 1, :], (8, 128))


def total(v):
    return jnp.sum(jnp.sum(v, axis=0), axis=0, keepdims=True)


def column_sum(v):
    return jnp.sum(v, axis=0, keepdims=True)


def place_smalls(fours, twos, core):
    dest = 2 * lax.broadcasted_iota(jnp.int32, (CHIPS, 512), 0) + core
    feature = lax.broadcasted_iota(jnp.int32, (CHIPS, 512), 1)
    lane = lax.broadcasted_iota(jnp.int32, (512, 128), 1)
    row = lax.broadcasted_iota(jnp.int32, (512, 128), 0)
    by_four = ((feature // 4) == dest, row % 4)
    by_two = (((feature % 256) // 2) == dest, row % 2 + 2 * (row // 256))
    out = jnp.zeros((CHIPS, 128), F32)
    for v, vec in enumerate(fours + twos):
        mine, inner = by_four if v < len(fours) else by_two
        high = vec.astype(BF16).astype(F32)
        rest = vec - high
        for part, base in ((high, 4 * v), (rest, 64 + 4 * v)):
            spread = jnp.where(mine, part, 0.0).astype(BF16)
            place = jnp.where(lane == base + inner, 1.0, 0.0).astype(BF16)
            out = out + dot(spread, place)
    return out


def kernel_middle(io):
    me = lax.axis_index("seq")
    core = me % 2
    ahead, _ = distance_tiles(io.ref("lengths"), me)
    lams = lam_tiles(io.ref("log_rate"), io.ref("angle"))
    pows = [powers(lams[half][2], 10) for half in range(HALVES)]
    coef = tile_lam([p[7] for p in pows])
    coef8 = tile_lam([p[10] for p in pows])
    carry = gather_carry(io.ref("ends"), me, -1, ahead, coef, coef8)
    local = split_channels(io.get("local"))
    row = rows_iota((MICRO * GROUPS, 8, 128))
    states, priors, heads = [], [], {}
    for half in range(HALVES):
        _, table = scan_tables(pows[half], False)
        x8 = local[half]
        before_r, before_i = [], []
        for micro in range(MICRO):
            init = (tile_row(carry, 0, micro, half), tile_row(carry, 1, micro, half))
            before, _ = chain_from(x8, micro, pows[half][3], init, False)
            for g in range(GROUPS):
                edge = edge_bcast(before[g], 7)
                before_r.append(edge[0])
                before_i.append(edge[1])
        br, bi = jnp.stack(before_r), jnp.stack(before_i)
        hr = x8[0] + (table[0] * br - table[1] * bi)
        hi = x8[1] + (table[0] * bi + table[1] * br)
        states.append((hr, hi))
        prior = (jnp.where(row == 0, br, pltpu.roll(hr, 1, 1)), jnp.where(row == 0, bi, pltpu.roll(hi, 1, 1)))
        priors.append(prior)
        _, back_table = scan_tables([conj(p) for p in pows[half][:4]], True)
        for micro in range(MICRO):
            _, v = chain_from(prior, micro, pows[half][3], None, False)
            m = cmul(v, conj(back_table))
            heads[(micro, half)] = (column_sum(m[0]), column_sum(m[1]))
    hidden = permute(join_channels(states).astype(BF16), io.get("deal_back")).astype(BF16)
    normed = io.get("normed")
    y = dot(hidden, io.get("c")) + io.get("skip") * normed.astype(F32)
    k0, k1 = 0.7978845608028654, 0.044715
    yy = y * y
    t = jnp.tanh(k0 * (y + k1 * (yy * y)))
    act = (0.5 * y * (1.0 + t)).astype(BF16)
    slope = 0.5 * (1.0 + t) + 0.5 * y * (1.0 - t * t) * (k0 * (1.0 + 3.0 * k1 * yy))
    gated = dot(act, io.get("glu"))
    value, gate = gated[:, :512], gated[:, 512:]
    sig = jax.nn.sigmoid(gate)
    go = io.get("go").astype(F32)
    x = io.get("x").astype(F32)
    io.put("out", (x + value * sig).astype(BF16))
    gs = go * sig
    dgated = jnp.concatenate([gs, gs * value * (1.0 - sig)], axis=1).astype(BF16)
    dy = (dot_nt(dgated, io.get("glu")) * slope).astype(BF16)
    dhidden = dot_nt(dy, io.get("c")).astype(BF16)
    q = split_channels(permute(dhidden, io.get("deal")))
    pairs = split_channels(io.get("pairs").astype(F32))
    parts, projs, rates, angles = {}, [], [], []
    for half in range(HALVES):
        u, r, lam, scale = lams[half]
        cp = [conj(p) for p in pows[half][:4]]
        levels, table = scan_tables(cp, True)
        x8 = group_scan(q[half], levels, True)
        after_r, after_i = [], []
        for micro in range(MICRO):
            zero = (jnp.zeros((8, 128), F32), jnp.zeros((8, 128), F32))
            after, v = chain_from(x8, micro, cp[3], zero, True)
            parts[(micro, half)] = (v[0][0:1, :], v[1][0:1, :])
            for g in range(GROUPS):
                edge = edge_bcast(after[g], 0)
                after_r.append(edge[0])
                after_i.append(edge[1])
        ar, ai = jnp.stack(after_r), jnp.stack(after_i)
        gr = x8[0] + (table[0] * ar - table[1] * ai)
        gi = x8[1] + (table[0] * ai + table[1] * ar)
        pr, pi = priors[half]
        d_re = total(gr * pr + gi * pi)
        d_im = total(gi * pr - gr * pi)
        d_scale = total(gr * pairs[half][0] + gi * pairs[half][1])
        rate, turn = chain_rule([t[0:1, :] for t in (u, r, lam[0], lam[1], scale)], d_re, d_im, d_scale)
        rates.append(rate)
        angles.append(turn)
        projs.append((gr * scale, gi * scale))
    dproj = permute(join_channels(projs).astype(BF16), io.get("deal_back")).astype(BF16)
    dyf = dy.astype(F32)
    dnormed = dot_nt(dproj, io.get("b")) + io.get("skip") * dyf
    io.put("dnormed", dnormed)
    xhat, _ = layer_norm(x)
    fours = [column_sum(dnormed * xhat), column_sum(dnormed), column_sum(dyf * normed.astype(F32))]
    twos = [jnp.concatenate(rates + angles, axis=1)]
    for micro in range(MICRO):
        twos.append(jnp.concatenate([heads[(micro, half)][comp] for comp in range(2) for half in range(HALVES)], axis=1))
    first = tile_rows(parts).astype(BF16)
    keep, send = io.ref("keep"), io.ref("send")
    for ref in (keep, send):
        ref[:, :, 1024:1152] = jnp.broadcast_to(first[None], (CHIPS, 8, 128))
    for ref, mine in ((keep, core), (send, 1 - core)):
        ref[:, :, 1152:1280] = jnp.broadcast_to(place_smalls(fours, twos, mine)[:, None, :], (CHIPS, 8, 128)).astype(BF16)
    glu_grad = dot_tn(act, dgated)
    c_grad = dot_tn(hidden, dy)
    b_grad = dot_tn(normed, dproj)
    even, odd = chunk_rows(glu_grad, jnp.concatenate([c_grad, b_grad], axis=1))
    keep[:, :, 0:1024] = jnp.where(core == 0, even, odd).astype(BF16)
    send[:, :, 0:1024] = jnp.where(core == 0, odd, even).astype(BF16)


def chain_rule(rows, d_re, d_im, d_scale):
    u, r, lr, li, scale = rows
    return u * (r * r * d_scale / scale - (lr * d_re + li * d_im)), lr * d_im - li * d_re


def kernel_pack(io):
    keep, got, out = io.ref("keep"), io.ref("got"), io.ref("packed")
    out[:, :, 0:1024] = (keep[:, :, 0:1024].astype(F32) + got[:, :, 0:1024].astype(F32)).astype(BF16)
    out[:, :, 1024:1152] = keep[:, :, 1024:1152]
    out[:, :, 1152:1280] = got[:, :, 1024:1152]
    low = rows_iota((CHIPS, 8, 128)) < 4
    out[:, :, 1280:1408] = jnp.where(low, keep[:, :, 1152:1280].astype(F32), got[:, :, 1152:1280].astype(F32)).astype(BF16)


def start_bits(lengths_ref, micro):
    bits = jnp.int32(0)
    at = jnp.int32(0)
    for slot in range(16):
        unit = at // (8 * TOK)
        bits = jnp.where(at < N * TOK, bits | lax.shift_left(jnp.int32(1), jnp.minimum(unit, 15)), bits)
        at = at + lengths_ref[micro, slot]
    return bits


def all_carries(first, lengths_ref, coefs):
    row = rows_iota()
    second = (row & 2) == 2
    bits = [start_bits(lengths_ref, micro) for micro in range(MICRO)]
    groups = first.reshape(16, 8, 8, 128)
    step = lambda c, coef: c * coef[0] + pltpu.roll(c, 4, 1) * coef[1]
    inner = [None] * 8
    inner[7] = jnp.zeros((16, 8, 128), F32)
    for p in range(6, -1, -1):
        inner[p] = groups[:, p + 1] + step(inner[p + 1], coefs[0])
    whole = groups[:, 0] + step(inner[0], coefs[0])
    entering = [None] * 16
    entering[15] = jnp.zeros((8, 128), F32)
    for g in range(14, -1, -1):
        value = whole[g + 1] + tile_mul(entering[g + 1], coefs[3])
        off = [(lax.shift_right_logical(b, g + 1) & 1) for b in bits]
        entering[g] = jnp.where(jnp.where(second, off[1], off[0]) == 1, 0.0, value)
    enter = jnp.stack(entering)
    out = []
    factor = enter
    for p in range(7, -1, -1):
        out.append(inner[p] + factor)
        factor = step(factor, coefs[0])
    return jnp.stack(out[::-1], axis=1).reshape(N, 8, 128)


def kernel_last(io, carries):
    me = lax.axis_index("seq")
    core, chip = me % 2, me // 2
    lams = lam_tiles(io.ref("log_rate"), io.ref("angle"))
    pows = [[conj(p) for p in powers(lams[half][2], 10)] for half in range(HALVES)]
    coefs = [tile_lam([p[7 + i] for p in pows]) for i in range(4)]
    parts = io.ref("parts")
    own = parts[:, :, 1024:1152].astype(F32)
    other = parts[:, :, 1152:1280].astype(F32)
    first = jnp.stack([jnp.where(core == 0, own, other), jnp.where(core == 0, other, own)], axis=1).reshape(N, 8, 128)
    enter = all_carries(first, io.ref("lengths"), coefs)
    carries[...] = enter
    mine = carries[me]
    reach = []
    for half in range(HALVES):
        _, table = scan_tables(pows[half], True)
        tiles = [table]
        for _ in range(GROUPS - 1):
            tiles.append(cmul(tiles[-1], pows[half][3]))
        reach.append((jnp.concatenate([t[0] for t in tiles[::-1]], axis=0), jnp.concatenate([t[1] for t in tiles[::-1]], axis=0)))
    scale_row = jnp.concatenate([lams[half][3][0:1, :] for half in (0, 0, 1, 1)], axis=1)
    rows = []
    for micro in range(MICRO):
        cols = []
        for half in range(HALVES):
            nr = tile_row(mine, 0, micro, half)[0:1, :]
            ni = tile_row(mine, 1, micro, half)[0:1, :]
            lr, li = reach[half]
            cols += [lr * nr - li * ni, lr * ni + li * nr]
        rows.append(jnp.concatenate(cols, axis=1))
    dproj = jnp.concatenate(rows, axis=0) * scale_row
    dproj = permute(dproj.astype(BF16), io.get("deal_back")).astype(BF16)
    dnormed = dot_nt(dproj, io.get("b")) + io.get("dnormed")
    xhat, rstd = layer_norm(io.get("x").astype(F32))
    dx = dnormed * io.get("gain")
    m1 = jnp.mean(dx, axis=1, keepdims=True)
    m2 = jnp.mean(dx * xhat, axis=1, keepdims=True)
    io.put("in_grad", (io.get("go").astype(F32) + rstd * (dx - m1 - xhat * m2)).astype(BF16))
    ends = io.ref("ends")
    reach_cols = jnp.concatenate([reach[0][0], reach[0][1], reach[1][0], reach[1][1]], axis=1)
    moved = dot(ends[:, 1].reshape(N * 8, 128), reach_cols.astype(BF16))
    low = rows_iota((N, 8, 128)) < 4
    spread = lambda comp, half: jnp.where(low, enter[:, comp * 4 + half : comp * 4 + half + 1, :], enter[:, comp * 4 + 2 + half : comp * 4 + 3 + half, :])
    cols = []
    for half in range(HALVES):
        c = 256 * half
        mr = moved[:, c : c + 128].reshape(N, 8, 128)
        mi = moved[:, c + 128 : c + 256].reshape(N, 8, 128)
        nr, ni = spread(0, half), spread(1, half)
        cols += [jnp.sum(mr * nr - mi * ni, axis=0), jnp.sum(mr * ni + mi * nr, axis=0)]
    rows8 = jnp.concatenate(cols, axis=1)
    rows8 = rows8 + pltpu.roll(rows8, 4, 0)
    enter_sum = jnp.sum(enter, axis=0)
    cols = []
    for half in range(HALVES):
        pick = lambda comp: enter_sum[comp * 4 + half : comp * 4 + half + 1, :] + enter_sum[comp * 4 + 2 + half : comp * 4 + 3 + half, :]
        nr, ni = pick(0), pick(1)
        lr, li = column_sum(reach[half][0]), column_sum(reach[half][1])
        cols += [lr * nr - li * ni, lr * ni + li * nr]
    sums_row = jnp.concatenate(cols, axis=1)
    low512 = rows_iota((8, 512)) < 4
    both = jnp.where(low512, rows8, sums_row) * scale_row
    back = io.get("deal_back").astype(F32)
    exact = functools.partial(jnp.dot, preferred_element_type=F32, precision=lax.Precision.HIGHEST)
    both = jnp.concatenate([exact(both[:, :256], back), exact(both[:, 256:], back)], axis=1)
    moved_x, moved_one = both, jnp.broadcast_to(both[4:5, :], (8, 512))
    feature = lax.broadcasted_iota(jnp.int32, (8, 512), 1)
    here = feature == 4 * me + rows_iota((8, 512)) % 4
    at_row = lambda name: jnp.sum(jnp.where(here, io.get(name), 0.0), axis=1, keepdims=True)
    gain_f, bias_f = at_row("gain"), at_row("bias")
    b_rows = io.ref("b_tiles")[chip].astype(F32)
    b_rows = jnp.where(core == 0, b_rows, pltpu.roll(b_rows, 4, 0))
    gain_carry = jnp.sum(b_rows * moved_x, axis=1, keepdims=True)
    bias_carry = jnp.sum(b_rows * moved_one, axis=1, keepdims=True)
    summed = jnp.sum(parts[:, :, 0:1024].astype(F32), axis=0)
    io.put("glu_grad", summed[0:4, :])
    io.put("c_grad", summed[4:8, 0:512])
    io.put("b_grad", summed[4:8, 512:1024] + (gain_f * moved_x + bias_f * moved_one)[0:4, :])
    small = parts[:, :, 1280:1408].astype(F32)
    small = small + pltpu.roll(small, 64, 2)
    hsel, lane0 = me // 64, (2 * me) % 128
    pick = jnp.where(
        lax.broadcasted_iota(jnp.int32, (128, 128), 0) == lane0 + lax.broadcasted_iota(jnp.int32, (128, 128), 1) % 2, 1.0, 0.0
    )
    picked = exact(enter.reshape(N * 8, 128), pick).reshape(N, 8, 128)
    lane = lax.broadcasted_iota(jnp.int32, (8, 128), 1)
    which = ((lane // 2) % 2) * 4 + ((lane // 4) % 2) * 2 + hsel
    picked = jnp.sum(jnp.where(which == rows_iota(), picked, 0.0), axis=1, keepdims=True).reshape(CHIPS, 2, 1, 128)
    own = jnp.where(core == 0, picked[:, 0], picked[:, 1])
    other = jnp.where(core == 0, picked[:, 1], picked[:, 0])
    picked = jnp.where(rows_iota((CHIPS, 8, 128)) < 4, own, other)
    fold = lambda v: v[0:1, :] + v[4:5, :]
    sums = fold(jnp.sum(small, axis=0))
    same = fold(jnp.sum(picked * small, axis=0))
    cross_re = fold(jnp.sum(pltpu.roll(picked, 126, 2) * small, axis=0))
    cross_im = fold(jnp.sum(pltpu.roll(picked, 2, 2) * small, axis=0))
    shift = lambda v, by: pltpu.roll(v, 128 - by, 1)
    d_re = shift(same, 16) + shift(same, 18) + shift(same, 20) + shift(same, 22)
    d_im = shift(cross_re, 16) + shift(cross_re, 20) - shift(cross_im, 18) - shift(cross_im, 22)
    e = ends[:, 0].astype(F32)
    straight = jnp.sum(enter * e, axis=0)
    crossed = jnp.sum(enter * pltpu.roll(e, 4, 1), axis=0)
    folded = lambda t, at, half: t[at + half : at + half + 1, :] + t[at + 2 + half : at + 3 + half, :]
    stacked = []
    for half in range(HALVES):
        u, r, lam, scale = lams[half]
        z_re = folded(straight, 0, half) + folded(straight, 4, half)
        z_im = folded(crossed, 4, half) - folded(crossed, 0, half)
        d_scale = (lam[0][0:1] * z_re + lam[1][0:1] * z_im) / scale[0:1]
        one = jnp.zeros((1, 128), F32)
        stacked.append(jnp.concatenate([u[0:1], r[0:1], lam[0][0:1], lam[1][0:1], scale[0:1], d_scale, one, one], axis=0))
    local = exact(jnp.where(hsel == 0, stacked[0], stacked[1]), pick)
    rate, turn = chain_rule([local[i : i + 1, :] for i in range(5)], d_re, d_im, local[5:6, :])
    diagonal = lax.broadcasted_iota(jnp.int32, (8, 128), 1) == rows_iota()
    to_lanes = lambda v: column_sum(jnp.where(diagonal, v, 0.0))
    io.put("gain_grad", (sums + to_lanes(gain_carry))[:, 0:4])
    io.put("bias_grad", (shift(sums, 4) + to_lanes(bias_carry))[:, 0:4])
    io.put("skip_grad", shift(sums, 8)[:, 0:4])
    io.put("rate_grad", (shift(sums, 12) + rate)[:, 0:2])
    io.put("angle_grad", (shift(sums, 14) + turn)[:, 0:2])


def body(block_in, out_grad, lengths, ln_gain, ln_bias, b_proj, c_proj, glu_weight, skip_gain, log_rate, angle):
    rows = MICRO * TOK
    x = block_in.reshape(rows, 512)
    go = out_grad.reshape(rows, 512)
    gain, bias, skip = (v.reshape(1, 512) for v in (ln_gain, ln_bias, skip_gain))
    rate2, angle2 = log_rate.reshape(2, 128), angle.reshape(2, 128)
    spread = deal()
    deal_m = jnp.asarray(spread, BF16)
    back_m = jnp.asarray(spread.T.copy(), BF16)
    full = (rows, 512)
    params = [("log_rate", rate2, "hbm"), ("angle", angle2, "hbm")]
    normed, pairs, local, ends = call(
        kernel_first,
        [("x", x, "hbm"), ("gain", gain, "hbm"), ("bias", bias, "hbm"), ("b", b_proj, "hbm"), ("deal", deal_m, "hbm")] + params,
        [("normed", full, BF16, "vmem"), ("pairs", full, BF16, "vmem"), ("local", full, F32, "vmem"), ("ends", (N, 2, 8, 128), BF16, "vmem")],
        flops=300_000_000, nbytes=3_000_000,
    )
    ends = lax.all_to_all(ends, "seq", split_axis=0, concat_axis=0, tiled=True)
    held = (CHIPS, 8, 1280)
    out, dnormed, keep, send = call(
        kernel_middle,
        [("lengths", lengths, "smem"), ("ends", ends, "vmem"), ("local", local, "vmem"), ("normed", normed, "vmem"), ("pairs", pairs, "vmem")]
        + params
        + [("deal_back", back_m, "hbm"), ("c", c_proj, "hbm"), ("skip", skip, "hbm"), ("glu", glu_weight, "hbm"), ("go", go, "hbm")]
        + [("x", x, "hbm"), ("deal", deal_m, "hbm"), ("b", b_proj, "hbm")],
        [("out", full, BF16, "hbm"), ("dnormed", full, F32, "vmem"), ("keep", held, BF16, "vmem"), ("send", held, BF16, "vmem")],
        flops=1_600_000_000, nbytes=6_000_000,
    )
    got = lax.ppermute(send, "seq", [(i, i ^ 1) for i in range(N)])
    (packed,) = call(
        kernel_pack, [("keep", keep, "vmem"), ("got", got, "vmem")], [("packed", (CHIPS, 8, 1408), BF16, "vmem")], flops=1_000_000, nbytes=2_400_000
    )
    same_core = [[2 * t + core for t in range(CHIPS)] for core in range(2)]
    parts = lax.all_to_all(packed, "seq", split_axis=0, concat_axis=0, tiled=True, axis_index_groups=same_core)
    in_grad, b_grad, c_grad, glu_grad, gain_grad, bias_grad, skip_grad, rate_grad, angle_grad = call(
        kernel_last,
        [("lengths", lengths, "smem"), ("ends", ends, "vmem"), ("parts", parts, "vmem"), ("dnormed", dnormed, "vmem")]
        + params
        + [("deal_back", back_m, "hbm"), ("b", b_proj, "hbm"), ("x", x, "hbm"), ("gain", gain, "hbm"), ("go", go, "hbm"), ("bias", bias, "hbm")]
        + [("b_tiles", b_proj.reshape(CHIPS, 8, 512), "hbm")],
        [("in_grad", full, BF16, "hbm"), ("b_grad", (4, 512), F32, "auto"), ("c_grad", (4, 512), F32, "auto"), ("glu_grad", (4, 1024), F32, "auto")]
        + [(name, (1, w), F32, "auto") for name, w in (("gain_grad", 4), ("bias_grad", 4), ("skip_grad", 4), ("rate_grad", 2), ("angle_grad", 2))],
        extra=[pltpu.VMEM((N, 8, 128), F32)], flops=600_000_000, nbytes=5_000_000,
    )
    return (
        out.reshape(block_in.shape),
        in_grad.reshape(block_in.shape),
        gain_grad.reshape(4),
        bias_grad.reshape(4),
        b_grad,
        c_grad,
        glu_grad,
        skip_grad.reshape(4),
        rate_grad.reshape(2),
        angle_grad.reshape(2),
    )


def solution(mesh):
    tokens = P(None, "seq", None)
    in_specs = (tokens, tokens) + (P(),) * 9
    out_specs = (tokens, tokens, P("seq"), P("seq"), P("seq", None), P("seq", None), P("seq", None), P("seq"), P("seq"), P("seq"))
    return jax.shard_map(body, mesh=mesh, in_specs=in_specs, out_specs=out_specs, check_vma=False)
```

time: 109 us -> 72.5 us (0.67)
  blocking collectives: 68.5 us -> 52.3 us
  waiting for transfers between devices: 13.2 us -> 3.02 us
  starting transfers between devices: 4.67 us -> 0.09 us
  local copies, waits for them, and re-layouts: 2.73 us -> 0.01 us
  Pallas kernels: 18.6 us -> 16 us
    all_to_all x3 -> x2, blocking collectives: 68.5 us -> 52.3 us  [the longest x1 27.8 us: body(): lax.all_to_all(packed, 'seq', split_axis=0, concat_axis=0, tiled=True, ax...]
    all_to_all x1 -> x0, waiting for transfers between devices: 13.2 us -> none  [body(): narrow = exchange(narrow)]
    all_to_all x1 -> x0, starting transfers between devices: 4.67 us -> none  [body(): narrow = exchange(narrow)]
    ppermute x0 -> x1, waiting for transfers between devices: none -> 3.02 us  [body(): got = lax.ppermute(send, 'seq', [(i, i ^ 1) for i in range(N)])]
    squeeze x2 -> x0, local copies, waits for them, and re-layouts: 2.73 us -> none  [the longest x1 1.39 us: body(): small[0, 8:12]]
    pallas_call x5 -> x4, Pallas kernels: 18.6 us -> 16 us  [call(): pl.pallas_call(run, out_shape=shapes, in_specs=[pl.BlockSpec(memory_space...]
  transfers between devices with their start and end apart: 1 -> 1, of which waited for: 1 -> 1; matrix products, arithmetic and copies ran while one was open for 0% -> 0% of each run, Pallas kernels for 3% -> 0%
where the time goes in v3:
time: 72.5 us; the launch traced here: 72.3 us
  blocking collectives  52.3 us (72%)
  Pallas kernels  16 us (22%)
  waiting for transfers between devices  3.02 us (4%)
  between operations  0.84 us (1%)
    all_to_all x1, blocking collectives, body(): lax.all_to_all(packed, 'seq', split_axis=0, concat_axis=0, tiled=True, ax...  27.8 us
    all_to_all x1, blocking collectives, body(): ends = lax.all_to_all(ends, 'seq', split_axis=0, concat_axis=0, tiled=True)  24.5 us
    pallas_call x4, Pallas kernels, call(): pl.pallas_call(run, out_shape=shapes, in_specs=[pl.BlockSpec(memory_space...  16 us
    ppermute x1, waiting for transfers between devices, body(): got = lax.ppermute(send, 'seq', [(i, i ^ 1) for i in range(N)])  3.02 us
  transfers between devices with their start and end apart: 1, of which 1 were waited for; matrix products, arithmetic and copies ran while one was open for 0% of the time, Pallas kernels for 0%

profile of v3, /device:TPU:0, one launch (start us, length us, event | category | flops | bytes accessed | tf_op | source)
XLA Modules:
  0.0 72.3 jit_solution(15696196931614177296)
XLA Ops:
  0.6 0.0 copy-start
  0.7 2.6 %shard_map.204 = (bf16[256,512]{1,0:T(8,128)(2,1)S(1)}, bf16[256,512]{1,0:T(8,128)(2,1)S(1)}, f32[256,512]{1,0:T(8,128)S(1)}, bf16[128,2,8,128]{3,2,1,0:T(8,128)(2,1)S(1)}) custom-call(bf16[256,512]{1,0:T(8,128)(2,1)} %bitcast.16, f32[1,512]{1,0:T(1,128)} %bitcast.21, f32[1,512]{1,0:T(1,128)} %bitcast.23, bf16[512,512]{1,0:T(8,128)(2,1)} %refs_7_.2, ...), custom_call_target="tpu_custom_call" | custom-call | flops 300000000 | bytes 3000000 | tf_op jit(solution)/shard_map/pallas_call | solution.py:291
  3.2 24.5 %all_to_all.10.refs_1_ = bf16[128,2,8,128]{3,2,1,0:T(8,128)(2,1)S(1)} all-to-all(bf16[128,2,8,128]{3,2,1,0:T(8,128)(2,1)S(1)} %get-tuple-element.27), channel_id=1, replica_groups=mesh['seq'=128] {'seq'}, dimensions={0} | all-to-all | bytes 1048576 | tf_op jit(solution)/shard_map/all_to_all | solution.py:662
  27.7 0.0 copy-done
  27.7 7.2 %shard_map.205 = (bf16[256,512]{1,0:T(8,128)(2,1)}, f32[256,512]{1,0:T(8,128)S(1)}, bf16[64,8,1280]{2,1,0:T(8,128)(2,1)S(1)}, bf16[64,8,1280]{2,1,0:T(8,128)(2,1)S(1)}) custom-call(s32[2,16]{1,0:T(2,128)S(1)} %copy-done, bf16[128,2,8,128]{3,2,1,0:T(8,128)(2,1)S(1)} %all_to_all.10.refs_1_, f32[256,512]{1,0:T(8,128)S(1)} %get-tuple-element.28.refs_2_, ...), custom_call_target="tpu_custom_call" | custom-call | flops 1600000000 | bytes 6000000 | tf_op jit(solution)/shard_map/pallas_call | solution.py:291
  34.9 0.1 collective-permute-start
  35.0 3.0 %collective-permute-done.refs_1_ = bf16[64,8,1280]{2,1,0:T(8,128)(2,1)S(1)} collective-permute-done((bf16[64,8,1280]{2,1,0:T(8,128)(2,1)S(1)}, bf16[64,8,1280]{2,1,0:T(8,128)(2,1)S(1)}, u32[]{:S(2)}, u32[]{:S(2)}) %collective-permute-start) | collective-permute-done | bytes 1310752 | tf_op jit(solution)/shard_map/ppermute | solution.py:673
  38.0 0.3 shard_map.206
  38.3 27.8 %all_to_all.11.refs_2_ = bf16[64,8,1408]{2,1,0:T(8,128)(2,1)S(1)} all-to-all(bf16[64,8,1408]{2,1,0:T(8,128)(2,1)S(1)} %shard_map.206), channel_id=1, replica_groups={{0,2,4,6,8,10,12,14,16,18,20,22,24,26,28,30,32,34,36,38,40,42,44,46,48,..., dimensions={0} | all-to-all | bytes 2883584 | tf_op jit(solution)/shard_map/all_to_all | solution.py:678
  66.2 6.0 %shard_map.207 = (bf16[256,512]{1,0:T(8,128)(2,1)}, f32[4,512]{1,0:T(4,128)}, f32[4,512]{1,0:T(4,128)}, f32[4,1024]{1,0:T(4,128)}, f32[1,4]{1,0:T(1,128)}, /*ind...) custom-call(s32[2,16]{1,0:T(2,128)S(1)} %copy-done, ...), custom_call_target="tpu_custom_call" | custom-call | flops 600000000 | bytes 5000000 | tf_op jit(solution)/shard_map/pallas_call | solution.py:291
Async XLA Ops:
  0.6 27.1 %copy-start = (s32[2,16]{1,0:T(2,128)S(1)}, s32[2,16]{1,0:T(2,128)}, u32[]{:S(2)}) copy-start(s32[2,16]{1,0:T(2,128)} %refs_0_.3) | copy-start | bytes 388
  34.9 3.1 %collective-permute-start = (bf16[64,8,1280]{2,1,0:T(8,128)(2,1)S(1)}, bf16[64,8,1280]{2,1,0:T(8,128)(2,1)S(1)}, u32[]{:S(2)}, u32[]{:S(2)}) collective-permute-start(bf16[64,8,1280]{2,1,0:T(8,128)(2,1)S(1)} %get-tuple-element.33), channel_id=1, source_target_pairs={{0,1},{1,0},{2,3},{3,2},{4,5},{5,4},{6,7},{7,6},{8,9},{9,8},{10,11... | collective-permute-start | bytes 3932168 | tf_op jit(solution)/shard_map/ppermute | solution.py:673

commit v4 on v3

v4 whole, which is shorter than its diff:
```python
import functools

import jax
import jax.numpy as jnp
import numpy as np
from jax import lax
from jax.experimental import pallas as pl
from jax.experimental.pallas import tpu as pltpu
from jax.sharding import PartitionSpec as P

F32 = jnp.float32
BF16 = jnp.bfloat16
VMEM_LIMIT = 40 * 1024 * 1024
TOK = 128
GROUPS = TOK // 8
MICRO = 2
HALVES = 2
N = 128
CHIPS = 64


def deal():
    out = np.zeros((256, 256), np.float32)
    for n in range(128):
        out[2 * n, n] = 1.0
        out[2 * n + 1, 128 + n] = 1.0
    return out


def dot(a, b):
    return jnp.dot(a, b, preferred_element_type=F32)


def dot_tn(a, b):
    return lax.dot_general(a, b, (((0,), (0,)), ((), ())), preferred_element_type=F32)


def dot_nt(a, b):
    return lax.dot_general(a, b, (((1,), (1,)), ((), ())), preferred_element_type=F32)


def cmul(a, b):
    return (a[0] * b[0] - a[1] * b[1], a[0] * b[1] + a[1] * b[0])


def conj(a):
    return (a[0], -a[1])


def rows_iota(shape=(8, 128)):
    return lax.broadcasted_iota(jnp.int32, shape, len(shape) - 2)


def params(log_rate, angle):
    u = jnp.exp(log_rate)
    r = jnp.exp(-u)
    lam = (r * jnp.cos(angle), r * jnp.sin(angle))
    w = 2.0 * u
    small = jnp.minimum(w, 0.5)
    poly = 1.0 - small * (1.0 / 11.0)
    for k in range(10, 1, -1):
        poly = 1.0 - small * (1.0 / k) * poly
    gap = jnp.where(w < 0.5, small * poly, 1.0 - jnp.exp(-w))
    scale = jnp.sqrt(gap)
    return u, r, lam, scale


def powers(lam, count):
    out = [lam]
    for _ in range(count):
        out.append(cmul(out[-1], out[-1]))
    return out


def spread_rows(pair, half):
    return tuple(jnp.broadcast_to(v[half : half + 1, :], (8, 128)) for v in pair)


def scan_tables(pows, reverse):
    row = rows_iota()
    pos = (7 - row) if reverse else row
    levels = []
    for s, p in ((1, pows[0]), (2, pows[1]), (4, pows[2])):
        keep = pos >= s
        levels.append((s, (jnp.where(keep, p[0], 0.0), jnp.where(keep, p[1], 0.0))))
    e = pos + 1
    table = (jnp.ones((8, 128), F32), jnp.zeros((8, 128), F32))
    for bit in range(4):
        on = (lax.shift_right_logical(e, bit) & 1) == 1
        table = cmul(table, (jnp.where(on, pows[bit][0], 1.0), jnp.where(on, pows[bit][1], 0.0)))
    return levels, table


def group_scan(x, levels, reverse):
    xr, xi = x
    for s, (mr, mi) in levels:
        shift = 8 - s if reverse else s
        rr = pltpu.roll(xr, shift, 1)
        ri = pltpu.roll(xi, shift, 1)
        xr, xi = xr + (mr * rr - mi * ri), xi + (mr * ri + mi * rr)
    return xr, xi


def tile_rows(parts):
    rows = []
    for comp in range(2):
        for micro in range(MICRO):
            for half in range(HALVES):
                rows.append(parts[(micro, half)][comp])
    return jnp.concatenate(rows, axis=0)


def tile_lam(p):
    row = rows_iota()
    odd = (row & 1) == 1
    re = jnp.where(odd, p[1][0], p[0][0])
    im = jnp.where(odd, p[1][1], p[0][1])
    return re, jnp.where(row < 4, -im, im)


def tile_mul(c, coef):
    return c * coef[0] + pltpu.roll(c, 4, 0) * coef[1]


def gather_carry(ends_ref, me, dmax, coef, coef8):
    chains = []
    for chain in range(8):
        acc = jnp.zeros((8, 128), F32)
        for i in range(7, -1, -1):
            d = chain * 8 + i
            e = ends_ref[jnp.maximum(me - 1 - d, 0), 0].astype(F32)
            e = jnp.where(d <= dmax, e, 0.0)
            acc = e if i == 7 else tile_mul(acc, coef) + e
        chains.append(acc)
    out = chains[7]
    for chain in range(6, -1, -1):
        out = tile_mul(out, coef8) + chains[chain]
    return out


def segment_tiles(lengths_ref, me):
    second = (rows_iota() & 2) == 2
    base = me * TOK
    ahead, bits = [], []
    for micro in range(MICRO):
        first, mask, at = jnp.int32(0), jnp.int32(0), jnp.int32(0)
        for slot in range(16):
            first = jnp.where(at <= base, jnp.maximum(first, at), first)
            unit = lax.shift_left(jnp.int32(1), jnp.minimum(at // (8 * TOK), 15))
            mask = jnp.where(at < N * TOK, mask | unit, mask)
            at = at + lengths_ref[micro, slot]
        ahead.append((base - first) // TOK - 1)
        bits.append(mask)
    pick = lambda two: jnp.where(second, two[1], two[0]).astype(F32)
    return pick(ahead), [pick([1 - (lax.shift_right_logical(b, g + 1) & 1) for b in bits]) for g in range(15)]


def groups_of(value, micro_groups=MICRO * GROUPS):
    return value.reshape(micro_groups, 8, 128)


def split_channels(value):
    out = []
    for half in range(HALVES):
        c = 256 * half
        out.append((groups_of(value[:, c : c + 128]), groups_of(value[:, c + 128 : c + 256])))
    return out


def join_channels(halves):
    cols = []
    for re, im in halves:
        cols.append(re.reshape(MICRO * TOK, 128))
        cols.append(im.reshape(MICRO * TOK, 128))
    return jnp.concatenate(cols, axis=1)


def permute(value_bf, matrix):
    return jnp.concatenate([dot(value_bf[:, :256], matrix), dot(value_bf[:, 256:], matrix)], axis=1)


def layer_norm(x):
    mean = jnp.mean(x, axis=1, keepdims=True)
    centered = x - mean
    var = jnp.mean(centered * centered, axis=1, keepdims=True)
    rstd = lax.rsqrt(var + 1e-05)
    return centered * rstd, rstd


def chain_from(x, micro, step8, init, reverse):
    before = {}
    v = init
    order = range(GROUPS - 1, -1, -1) if reverse else range(GROUPS)
    for g in order:
        before[g] = v
        xr, xi = x[0][micro * GROUPS + g], x[1][micro * GROUPS + g]
        if v is None:
            v = (xr, xi)
        else:
            m = cmul(v, step8)
            v = (xr + m[0], xi + m[1])
    return before, v


def edge_bcast(pair, edge):
    return tuple(jnp.broadcast_to(p[edge : edge + 1, :], (8, 128)) for p in pair)


class Ports:
    def __init__(self, ins, outs, refs):
        n_in, n_out = len(ins), len(outs)
        scratch = list(refs[n_in + n_out :])
        out_refs = {name: ref for (name, _, _, _), ref in zip(outs, refs[n_in:])}
        self.refs, self.pending, self.leaving, self.out_copies = {}, {}, [], {}
        sems = scratch.pop() if scratch else None
        i = 0
        for (name, _, mode), ref in zip(ins, refs):
            self.refs[name] = ref
            if mode == "any":
                self.sem = sems.at[i]
                i += 1
            if mode in ("hbm", "smem", "load"):
                target = out_refs[name] if mode == "load" else scratch.pop(0)
                self.pending[name] = pltpu.make_async_copy(ref, target, sems.at[i])
                self.pending[name].start()
                self.refs[name] = target
                i += 1
        for name, _, _, mode in outs:
            if name not in self.refs:
                self.refs[name] = out_refs[name]
            if mode == "hbm":
                self.refs[name] = scratch.pop(0)
                self.out_copies[name] = pltpu.make_async_copy(self.refs[name], out_refs[name], sems.at[i])
                i += 1

    def ref(self, name):
        if name in self.pending:
            self.pending.pop(name).wait()
        return self.refs[name]

    def get(self, name):
        return self.ref(name)[...]

    def put(self, name, value):
        self.refs[name][...] = value
        if name in self.out_copies:
            self.out_copies[name].start()
            self.leaving.append(name)

    def finish(self):
        for name in list(self.pending):
            self.ref(name)
        for name in self.leaving:
            self.out_copies[name].wait()


def call(kernel, ins, outs, extra=(), flops=0, nbytes=0):
    outs = list(outs) + [(name, array.shape, array.dtype, "vmem") for name, array, mode in ins if mode == "load"]

    def run(*refs):
        n_extra = len(extra)
        ports = Ports(ins, outs, refs[: len(refs) - n_extra])
        kernel(ports, *refs[len(refs) - n_extra :])
        ports.finish()

    args, scratch, copies = [], [], 0
    for _, array, mode in ins:
        args.append(pltpu.with_memory_space_constraint(array, pltpu.VMEM if mode == "vmem" else pltpu.HBM))
        copies += mode != "vmem"
        if mode in ("hbm", "smem"):
            scratch.append((pltpu.VMEM if mode == "hbm" else pltpu.SMEM)(array.shape, array.dtype))
    for _, shape, kind, mode in outs:
        if mode == "hbm":
            scratch.append(pltpu.VMEM(shape, kind))
            copies += 1
    if copies:
        scratch.append(pltpu.SemaphoreType.DMA((copies,)))
    out = pl.pallas_call(
        run,
        out_shape=[pltpu.VMEM(s, d) if mode == "vmem" else jax.ShapeDtypeStruct(s, d) for _, s, d, mode in outs],
        in_specs=[pl.BlockSpec(memory_space=pltpu.VMEM if mode == "vmem" else pl.ANY) for _, _, mode in ins],
        out_specs=[pl.BlockSpec(memory_space=pltpu.VMEM if mode == "vmem" else pl.ANY) for _, _, _, mode in outs],
        scratch_shapes=scratch + list(extra),
        compiler_params=pltpu.CompilerParams(vmem_limit_bytes=VMEM_LIMIT),
        cost_estimate=pl.CostEstimate(flops=flops, bytes_accessed=nbytes, transcendentals=0),
    )(*args)
    return {name: array for (name, _, _, _), array in zip(outs, out)}


def chunk_rows(left, right):
    w = left.shape[1]
    a = left.reshape(CHIPS, 8, w)
    b = right.reshape(CHIPS, 8, w)
    low = rows_iota((CHIPS, 8, w)) < 4
    return jnp.where(low, a, pltpu.roll(b, 4, 1)), jnp.where(low, pltpu.roll(a, 4, 1), b)


PER_HALF = ["ahead_r", "ahead_i", "back_r", "back_i", "l1_r", "l1_i", "l2_r", "l2_i", "l4_r", "l4_i", "step_r", "step_i", "scale", "u", "r", "lam_r", "lam_i"]
TABLES = {}
for half in range(HALVES):
    for name in PER_HALF:
        TABLES[name, half] = len(TABLES)
for name in ["coef_r", "coef_i", "coef8_r", "coef8_i", "devices_ahead"]:
    TABLES[name] = len(TABLES)
for group in range(15):
    TABLES["joined", group] = len(TABLES)


def pair_of(tables, name, half):
    return tables[TABLES[name + "_r", half]], tables[TABLES[name + "_i", half]]


def coefs_of(tables, name, forward):
    ci = tables[TABLES[name + "_i"]]
    return tables[TABLES[name + "_r"]], (ci if forward else -ci)


def kernel_first(io):
    me = lax.axis_index("seq")
    tables = io.refs["tables"]
    x = io.get("x").astype(F32)
    xhat, rstd = layer_norm(x)
    normed = (xhat * io.get("gain") + io.get("bias")).astype(BF16)
    io.put("normed", normed)
    io.put("xhat", xhat)
    io.put("rstd", jnp.broadcast_to(rstd, (MICRO * TOK, 128)))
    u, r, lam, scale = params(io.get("log_rate"), io.get("angle"))
    pows = powers(lam, 10)
    proj = dot(normed, io.get("b")).astype(BF16)
    pairs = permute(proj, io.get("deal"))
    io.put("pairs", pairs.astype(BF16))
    halves = split_channels(pairs)
    parts, scanned = {}, []
    for half in range(HALVES):
        mine = [spread_rows(p, half) for p in pows[:4]]
        (scale8,) = spread_rows((scale,), half)
        levels, table = scan_tables(mine, False)
        re, im = halves[half]
        x8 = group_scan((re * scale8, im * scale8), levels, False)
        scanned.append(x8)
        for micro in range(MICRO):
            _, v = chain_from(x8, micro, mine[3], None, False)
            parts[(micro, half)] = (v[0][7:8, :], v[1][7:8, :])
        back_levels, back_table = scan_tables([conj(p) for p in mine], True)
        u8, r8 = spread_rows((u, r), half)
        values = list(table) + list(back_table) + [v for _, level in back_levels for v in level] + list(mine[3])
        values += [scale8, u8, r8] + list(mine[0])
        for name, value in zip(PER_HALF, values):
            tables[TABLES[name, half]] = value
    ends = io.refs["ends"]
    ends[:, 0] = jnp.broadcast_to(tile_rows(parts).astype(BF16)[None], (N, 8, 128))
    even, odd = chunk_rows(xhat[:TOK].T, xhat[TOK:].T)
    ends[:, 1] = jnp.stack([even, odd], axis=1).reshape(N, 8, 128).astype(BF16)
    io.put("local", join_channels(scanned))
    for name, at in (("coef", 7), ("coef8", 10)):
        tables[TABLES[name + "_r"]], tables[TABLES[name + "_i"]] = tile_lam([spread_rows(pows[at], half) for half in range(HALVES)])
    ahead, joined = segment_tiles(io.ref("lengths"), me)
    tables[TABLES["devices_ahead"]] = ahead
    for group in range(15):
        tables[TABLES["joined", group]] = joined[group]
    copy = pltpu.make_async_copy(io.ref("b_tiles").at[me // 2], io.refs["b_rows"], io.sem)
    copy.start()
    copy.wait()


def tile_row(tile, comp, micro, half):
    at = comp * 4 + micro * 2 + half
    return jnp.broadcast_to(tile[at : at + 1, :], (8, 128))


def total(v):
    return jnp.sum(jnp.sum(v, axis=0), axis=0, keepdims=True)


def column_sum(v):
    return jnp.sum(v, axis=0, keepdims=True)


def two_parts(rows):
    high = [v.astype(BF16).astype(F32) for v in rows]
    rest = [v - h for v, h in zip(rows, high)]
    pad = jnp.zeros((16 - 2 * len(rows), rows[0].shape[1]), F32)
    return jnp.concatenate(high + rest + [pad], axis=0).astype(BF16)


def place_smalls(fours, twos):
    out = jnp.zeros((N, 128), F32)
    for rows, each, base in ((fours, 4, 0), (twos, 2, 16)):
        width = rows[0].shape[1]
        block = two_parts(rows)
        at = lax.broadcasted_iota(jnp.int32, (N, width), 0)
        device = 2 * (at % CHIPS) + at // CHIPS
        feature = lax.broadcasted_iota(jnp.int32, (N, width), 1)
        for j in range(each):
            chosen = jnp.where(feature == each * device + j, 1.0, 0.0).astype(BF16)
            above = 32 * j + base
            spread = [block, jnp.zeros((112 - above, width), BF16)] if above < 112 else [block]
            if above:
                spread = [jnp.zeros((above, width), BF16)] + spread
            out = out + dot_nt(chosen, jnp.concatenate(spread, axis=0))
    return out


def chain_rule(rows, d_re, d_im, d_scale):
    u, r, lr, li, scale = rows
    return u * (r * r * d_scale / scale - (lr * d_re + li * d_im)), lr * d_im - li * d_re


def kernel_middle(io):
    me = lax.axis_index("seq")
    core = me % 2
    tables = io.refs["tables"]
    coef, coef8 = coefs_of(tables, "coef", True), coefs_of(tables, "coef8", True)
    carry = gather_carry(io.refs["ends"], me, tables[TABLES["devices_ahead"]], coef, coef8)
    local = split_channels(io.get("local"))
    row = rows_iota((MICRO * GROUPS, 8, 128))
    states, priors, heads = [], [], {}
    for half in range(HALVES):
        table, step8 = pair_of(tables, "ahead", half), pair_of(tables, "step", half)
        x8 = local[half]
        before_r, before_i = [], []
        for micro in range(MICRO):
            init = (tile_row(carry, 0, micro, half), tile_row(carry, 1, micro, half))
            before, _ = chain_from(x8, micro, step8, init, False)
            for g in range(GROUPS):
                edge = edge_bcast(before[g], 7)
                before_r.append(edge[0])
                before_i.append(edge[1])
        br, bi = jnp.stack(before_r), jnp.stack(before_i)
        hr = x8[0] + (table[0] * br - table[1] * bi)
        hi = x8[1] + (table[0] * bi + table[1] * br)
        states.append((hr, hi))
        priors.append((jnp.where(row == 0, br, pltpu.roll(hr, 1, 1)), jnp.where(row == 0, bi, pltpu.roll(hi, 1, 1))))
    hidden = permute(join_channels(states).astype(BF16), io.get("deal_back")).astype(BF16)
    normed = io.get("normed")
    y = dot(hidden, io.get("c")) + io.get("skip") * normed.astype(F32)
    k0, k1 = 0.7978845608028654, 0.044715
    yy = y * y
    t = jnp.tanh(k0 * (y + k1 * (yy * y)))
    act = (0.5 * y * (1.0 + t)).astype(BF16)
    slope = 0.5 * (1.0 + t) + 0.5 * y * (1.0 - t * t) * (k0 * (1.0 + 3.0 * k1 * yy))
    gated = dot(act, io.get("glu"))
    value, gate = gated[:, :512], gated[:, 512:]
    sig = jax.nn.sigmoid(gate)
    go = io.get("go").astype(F32)
    io.put("out", (io.get("x").astype(F32) + value * sig).astype(BF16))
    gs = go * sig
    dgated = jnp.concatenate([gs, gs * value * (1.0 - sig)], axis=1).astype(BF16)
    dy = (dot_nt(dgated, io.get("glu")) * slope).astype(BF16)
    dhidden = dot_nt(dy, io.get("c")).astype(BF16)
    q = split_channels(permute(dhidden, io.get("deal")))
    pairs = split_channels(io.get("pairs").astype(F32))
    parts, projs, rates, angles = {}, [], [], []
    for half in range(HALVES):
        table, step8 = pair_of(tables, "back", half), conj(pair_of(tables, "step", half))
        scale = tables[TABLES["scale", half]]
        levels = [(s, pair_of(tables, "l%d" % s, half)) for s in (1, 2, 4)]
        x8 = group_scan(q[half], levels, True)
        after_r, after_i = [], []
        for micro in range(MICRO):
            zero = (jnp.zeros((8, 128), F32), jnp.zeros((8, 128), F32))
            after, v = chain_from(x8, micro, step8, zero, True)
            parts[(micro, half)] = (v[0][0:1, :], v[1][0:1, :])
            for g in range(GROUPS):
                edge = edge_bcast(after[g], 0)
                after_r.append(edge[0])
                after_i.append(edge[1])
        ar, ai = jnp.stack(after_r), jnp.stack(after_i)
        gr = x8[0] + (table[0] * ar - table[1] * ai)
        gi = x8[1] + (table[0] * ai + table[1] * ar)
        pr, pi = priors[half]
        d_re = total(gr * pr + gi * pi)
        d_im = total(gi * pr - gr * pi)
        d_scale = total(gr * pairs[half][0] + gi * pairs[half][1])
        rows = [tables[TABLES[name, half]][0:1, :] for name in ("u", "r", "lam_r", "lam_i", "scale")]
        rate, turn = chain_rule(rows, d_re, d_im, d_scale)
        rates.append(rate)
        angles.append(turn)
        projs.append((gr * scale, gi * scale))
        for micro in range(MICRO):
            _, v = chain_from(priors[half], micro, conj(step8), None, False)
            m = cmul(v, conj(table))
            heads[(micro, half)] = (column_sum(m[0]), column_sum(m[1]))
    dproj = permute(join_channels(projs).astype(BF16), io.get("deal_back")).astype(BF16)
    dyf = dy.astype(F32)
    dnormed = dot_nt(dproj, io.get("b")) + io.get("skip") * dyf
    io.put("dnormed", dnormed)
    fours = [column_sum(dnormed * io.get("xhat")), column_sum(dnormed), column_sum(dyf * normed.astype(F32))]
    join = lambda two: jnp.concatenate(two, axis=1)
    twos = [join(rates), join(angles)]
    for micro in range(MICRO):
        for comp in range(2):
            twos.append(join([heads[(micro, half)][comp] for half in range(HALVES)]))
    smalls = place_smalls(fours, twos)
    first = tile_rows(parts)
    keep, send = io.refs["keep"], io.refs["send"]
    low = rows_iota((CHIPS, 8, 128)) < 4
    chip = lax.broadcasted_iota(jnp.int32, (CHIPS, 8, 128), 0)
    for ref, flip in ((keep, 0), (send, 1)):
        small = jnp.where((core + flip) % 2 == 0, smalls[:CHIPS], smalls[CHIPS:])[:, None, :]
        ref[:, :, 1024:1152] = jnp.where(low, small, jnp.where(chip == 0, pltpu.roll(first, 4, 0), first)).astype(BF16)
    glu_grad = dot_tn(act, dgated)
    c_grad = dot_tn(hidden, dy)
    b_grad = dot_tn(normed, dproj)
    even, odd = chunk_rows(glu_grad, jnp.concatenate([c_grad, b_grad], axis=1))
    keep[:, :, 0:1024] = jnp.where(core == 0, even, odd).astype(BF16)
    send[:, :, 0:1024] = jnp.where(core == 0, odd, even).astype(BF16)


def kernel_pack(io):
    keep, got, out = io.refs["keep"], io.refs["got"], io.refs["packed"]
    out[:, :, 0:1024] = (keep[:, :, 0:1024].astype(F32) + got[:, :, 0:1024].astype(F32)).astype(BF16)
    low = rows_iota((CHIPS, 8, 128)) < 4
    own, other = keep[:, :, 1024:1152].astype(F32), got[:, :, 1024:1152].astype(F32)
    for at, tiles in ((1024, own), (1152, other)):
        tile = jnp.where(rows_iota() < 4, pltpu.roll(tiles[0], 4, 0), tiles[1])
        out[:, :, at : at + 128] = jnp.broadcast_to(tile.astype(BF16)[None], (CHIPS, 8, 128))
    out[:, :, 1280:1408] = jnp.where(low, own, pltpu.roll(other, 4, 1)).astype(BF16)


def all_carries(first, tables):
    coef, coef8 = coefs_of(tables, "coef", False), coefs_of(tables, "coef8", False)
    groups = first.reshape(16, 8, 8, 128)
    step = lambda c: c * coef[0] + pltpu.roll(c, 4, 1) * coef[1]
    inner = [None] * 8
    inner[7] = jnp.zeros((16, 8, 128), F32)
    for p in range(6, -1, -1):
        inner[p] = groups[:, p + 1] + step(inner[p + 1])
    whole = groups[:, 0] + step(inner[0])
    entering = [None] * 16
    entering[15] = jnp.zeros((8, 128), F32)
    for g in range(14, -1, -1):
        entering[g] = (whole[g + 1] + tile_mul(entering[g + 1], coef8)) * tables[TABLES["joined", g]]
    factor = jnp.stack(entering)
    out = []
    for p in range(7, -1, -1):
        out.append(inner[p] + factor)
        factor = step(factor)
    return jnp.stack(out[::-1], axis=1).reshape(N, 8, 128)


def kernel_last(io, carries):
    me = lax.axis_index("seq")
    core = me % 2
    tables = io.refs["tables"]
    parts = io.refs["parts"]
    own = parts[:, :, 1024:1152].astype(F32)
    other = parts[:, :, 1152:1280].astype(F32)
    first = jnp.stack([jnp.where(core == 0, own, other), jnp.where(core == 0, other, own)], axis=1).reshape(N, 8, 128)
    enter = all_carries(first, tables)
    carries[...] = enter
    mine = carries[me]
    reach = []
    for half in range(HALVES):
        step8 = conj(pair_of(tables, "step", half))
        tiles = [pair_of(tables, "back", half)]
        for _ in range(GROUPS - 1):
            tiles.append(cmul(tiles[-1], step8))
        reach.append(tuple(jnp.concatenate([t[comp] for t in tiles[::-1]], axis=0) for comp in range(2)))
    scale_row = jnp.concatenate([tables[TABLES["scale", half]][0:1, :] for half in (0, 0, 1, 1)], axis=1)
    rows = []
    for micro in range(MICRO):
        cols = []
        for half in range(HALVES):
            nr, ni = tile_row(mine, 0, micro, half)[0:1, :], tile_row(mine, 1, micro, half)[0:1, :]
            lr, li = reach[half]
            cols += [lr * nr - li * ni, lr * ni + li * nr]
        rows.append(jnp.concatenate(cols, axis=1))
    dproj = jnp.concatenate(rows, axis=0) * scale_row
    dproj = permute(dproj.astype(BF16), io.get("deal_back")).astype(BF16)
    dnormed = dot_nt(dproj, io.get("b")) + io.get("dnormed")
    xhat, rstd = io.get("xhat"), io.get("rstd")[:, 0:1]
    dx = dnormed * io.get("gain")
    m1 = jnp.mean(dx, axis=1, keepdims=True)
    m2 = jnp.mean(dx * xhat, axis=1, keepdims=True)
    io.put("in_grad", (io.get("go").astype(F32) + rstd * (dx - m1 - xhat * m2)).astype(BF16))
    summed = jnp.sum(parts[:, :, 0:1024].astype(F32), axis=0)
    io.put("glu_grad", summed[0:4, :])
    io.put("c_grad", summed[4:8, 0:512])
    ends = io.refs["ends"]
    reach_cols = jnp.concatenate([reach[0][0], reach[0][1], reach[1][0], reach[1][1]], axis=1)
    moved = dot(ends[:, 1].reshape(N * 8, 128), reach_cols.astype(BF16))
    low = rows_iota((N, 8, 128)) < 4
    spread = lambda comp, half: jnp.where(low, enter[:, comp * 4 + half : comp * 4 + half + 1, :], enter[:, comp * 4 + 2 + half : comp * 4 + 3 + half, :])
    cols = []
    for half in range(HALVES):
        c = 256 * half
        mr = moved[:, c : c + 128].reshape(N, 8, 128)
        mi = moved[:, c + 128 : c + 256].reshape(N, 8, 128)
        nr, ni = spread(0, half), spread(1, half)
        cols += [jnp.sum(mr * nr - mi * ni, axis=0), jnp.sum(mr * ni + mi * nr, axis=0)]
    rows8 = jnp.concatenate(cols, axis=1)
    rows8 = rows8 + pltpu.roll(rows8, 4, 0)
    enter_sum = jnp.sum(enter, axis=0)
    cols = []
    for half in range(HALVES):
        fold2 = lambda comp: enter_sum[comp * 4 + half : comp * 4 + half + 1, :] + enter_sum[comp * 4 + 2 + half : comp * 4 + 3 + half, :]
        nr, ni = fold2(0), fold2(1)
        lr, li = column_sum(reach[half][0]), column_sum(reach[half][1])
        cols += [lr * nr - li * ni, lr * ni + li * nr]
    sums_row = jnp.concatenate(cols, axis=1)
    low512 = rows_iota((8, 512)) < 4
    both = jnp.where(low512, rows8, sums_row) * scale_row
    back = io.get("deal_back").astype(F32)
    exact = functools.partial(jnp.dot, preferred_element_type=F32, precision=lax.Precision.HIGHEST)
    both = jnp.concatenate([exact(both[:, :256], back), exact(both[:, 256:], back)], axis=1)
    moved_x, moved_one = both, jnp.broadcast_to(both[4:5, :], (8, 512))
    feature = lax.broadcasted_iota(jnp.int32, (8, 512), 1)
    here = feature == 4 * me + rows_iota((8, 512)) % 4
    at_row = lambda name: jnp.sum(jnp.where(here, io.get(name), 0.0), axis=1, keepdims=True)
    gain_f, bias_f = at_row("gain"), at_row("bias")
    io.put("b_grad", summed[4:8, 512:1024] + (gain_f * moved_x + bias_f * moved_one)[0:4, :])
    b_rows = io.get("b_rows").astype(F32)
    b_rows = jnp.where(core == 0, b_rows, pltpu.roll(b_rows, 4, 0))
    gain_carry = jnp.sum(b_rows * moved_x, axis=1, keepdims=True)
    bias_carry = jnp.sum(b_rows * moved_one, axis=1, keepdims=True)
    hsel, lane0 = me // 64, (2 * me) % 128
    lane = lax.broadcasted_iota(jnp.int32, (128, 128), 0)
    col = lax.broadcasted_iota(jnp.int32, (128, 128), 1)
    pick = jnp.where(lane == lane0 + col // 32, 1.0, 0.0).astype(BF16)
    flat = enter.reshape(N * 8, 128)
    high = flat.astype(BF16)
    picked = dot(high, pick) + dot((flat - high.astype(F32)).astype(BF16), pick)
    picked = picked.reshape(CHIPS, 2, 8, 128)
    small = parts[:, :, 1280:1408].astype(F32)
    mine_n = jnp.where(core == 0, picked[:, 0], picked[:, 1])
    other_n = jnp.where(core == 0, picked[:, 1], picked[:, 0])
    products = jnp.sum(mine_n * small[:, 0:1, :] + other_n * small[:, 4:5, :], axis=0)
    sums = jnp.sum(small, axis=0)
    sums = sums[0:1, :] + sums[4:5, :]
    lane8 = lax.broadcasted_iota(jnp.int32, (8, 128), 1)
    w = lane8 % 32 - 16
    comp, micro = w & 1, (w % 6) // 2 - 1
    valid = (w >= 0) & (w < 12) & (micro >= 0) & (lane8 < 64)
    source = lambda c: valid & (rows_iota() == c * 4 + micro * 2 + hsel)
    same = column_sum(jnp.where(source(comp), products, 0.0))
    cross = column_sum(jnp.where(source(1 - comp), jnp.where(comp == 0, products, -products), 0.0))
    v, j = lane % 32, lane // 32
    w = v - 16
    spot = jnp.where(v < 6, 4 * (v % 3) + j, -1)
    spot = jnp.where((w >= 0) & (w < 12) & (j < 2), jnp.where(w % 6 < 2, 12 + 2 * (w % 6) + j, 16 + j), spot)
    gathered = exact(jnp.concatenate([sums, same, cross, jnp.zeros((5, 128), F32)], axis=0), jnp.where(spot == col, 1.0, 0.0))
    e = ends[:, 0].astype(F32)
    straight = jnp.sum(enter * e, axis=0)
    crossed = jnp.sum(enter * pltpu.roll(e, 4, 1), axis=0)
    folded = lambda t, at, half: t[at + half : at + half + 1, :] + t[at + 2 + half : at + 3 + half, :]
    stacked = []
    for half in range(HALVES):
        u, r, lr, li, scale = [tables[TABLES[name, half]][0:1, :] for name in ("u", "r", "lam_r", "lam_i", "scale")]
        z_re = folded(straight, 0, half) + folded(straight, 4, half)
        z_im = folded(crossed, 4, half) - folded(crossed, 0, half)
        d_scale = (lr * z_re + li * z_im) / scale
        stacked.append(jnp.concatenate([u, r, lr, li, scale, d_scale, jnp.zeros((2, 128), F32)], axis=0))
    local = exact(jnp.where(hsel == 0, stacked[0], stacked[1]), jnp.where(lane == lane0 + col % 2, 1.0, 0.0))
    rate, turn = chain_rule([local[i : i + 1, :] for i in range(5)], gathered[1:2, :], gathered[2:3, :], local[5:6, :])
    shift = lambda v, by: pltpu.roll(v, 128 - by, 1)
    diagonal = lane8 == rows_iota()
    to_lanes = lambda v: column_sum(jnp.where(diagonal, v, 0.0))
    sums = gathered[0:1, :]
    io.put("gain_grad", (sums + to_lanes(gain_carry))[:, 0:4])
    io.put("bias_grad", (shift(sums, 4) + to_lanes(bias_carry))[:, 0:4])
    io.put("skip_grad", shift(sums, 8)[:, 0:4])
    io.put("rate_grad", (shift(sums, 12) + shift(rate, 16))[:, 0:2])
    io.put("angle_grad", (shift(sums, 14) + shift(turn, 16))[:, 0:2])


def body(block_in, out_grad, lengths, ln_gain, ln_bias, b_proj, c_proj, glu_weight, skip_gain, log_rate, angle):
    rows = MICRO * TOK
    x = block_in.reshape(rows, 512)
    go = out_grad.reshape(rows, 512)
    gain, bias, skip = (v.reshape(1, 512) for v in (ln_gain, ln_bias, skip_gain))
    rate2, angle2 = log_rate.reshape(2, 128), angle.reshape(2, 128)
    spread = deal()
    deal_m = jnp.asarray(spread, BF16)
    back_m = jnp.asarray(spread.T.copy(), BF16)
    full = (rows, 512)
    k1 = call(
        kernel_first,
        [("x", x, "load"), ("b", b_proj, "load"), ("deal", deal_m, "load"), ("gain", gain, "load"), ("bias", bias, "load")]
        + [("log_rate", rate2, "hbm"), ("angle", angle2, "hbm"), ("lengths", lengths, "smem"), ("deal_back", back_m, "load")]
        + [("c", c_proj, "load"), ("skip", skip, "load"), ("glu", glu_weight, "load"), ("go", go, "load")]
        + [("b_tiles", b_proj.reshape(CHIPS, 8, 512), "any")],
        [("normed", full, BF16, "vmem"), ("xhat", full, F32, "vmem"), ("rstd", (rows, 128), F32, "vmem"), ("pairs", full, BF16, "vmem")]
        + [("local", full, F32, "vmem"), ("ends", (N, 2, 8, 128), BF16, "vmem"), ("tables", (len(TABLES), 8, 128), F32, "vmem")]
        + [("b_rows", (8, 512), BF16, "vmem")],
        flops=300_000_000, nbytes=3_000_000,
    )
    k1["ends"] = lax.all_to_all(k1["ends"], "seq", split_axis=0, concat_axis=0, tiled=True)
    use = lambda group, *names: [(name, group[name], "vmem") for name in names]
    held = (CHIPS, 8, 1152)
    k2 = call(
        kernel_middle,
        use(k1, "ends", "tables", "local", "normed", "xhat", "pairs", "deal", "deal_back", "c", "skip", "glu", "go", "x", "b"),
        [("out", full, BF16, "hbm"), ("dnormed", full, F32, "vmem"), ("keep", held, BF16, "vmem"), ("send", held, BF16, "vmem")],
        flops=1_600_000_000, nbytes=6_000_000,
    )
    got = lax.ppermute(k2["send"], "seq", [(i, i ^ 1) for i in range(N)])
    packed = call(
        kernel_pack, use(k2, "keep") + [("got", got, "vmem")], [("packed", (CHIPS, 8, 1408), BF16, "vmem")], flops=1_000_000, nbytes=2_400_000
    )["packed"]
    same_core = [[2 * t + core for t in range(CHIPS)] for core in range(2)]
    parts = lax.all_to_all(packed, "seq", split_axis=0, concat_axis=0, tiled=True, axis_index_groups=same_core)
    k3 = call(
        kernel_last,
        [("parts", parts, "vmem")] + use(k2, "dnormed") + use(k1, "ends", "tables", "deal_back", "b", "xhat", "rstd", "gain", "bias", "go", "b_rows"),
        [("in_grad", full, BF16, "hbm"), ("b_grad", (4, 512), F32, "hbm"), ("c_grad", (4, 512), F32, "hbm"), ("glu_grad", (4, 1024), F32, "hbm")]
        + [(name, (1, w), F32, "hbm") for name, w in (("gain_grad", 4), ("bias_grad", 4), ("skip_grad", 4), ("rate_grad", 2), ("angle_grad", 2))],
        extra=[pltpu.VMEM((N, 8, 128), F32)], flops=600_000_000, nbytes=5_000_000,
    )
    return (
        k2["out"].reshape(block_in.shape),
        k3["in_grad"].reshape(block_in.shape),
        k3["gain_grad"].reshape(4),
        k3["bias_grad"].reshape(4),
        k3["b_grad"],
        k3["c_grad"],
        k3["glu_grad"],
        k3["skip_grad"].reshape(4),
        k3["rate_grad"].reshape(2),
        k3["angle_grad"].reshape(2),
    )


def solution(mesh):
    tokens = P(None, "seq", None)
    in_specs = (tokens, tokens) + (P(),) * 9
    out_specs = (tokens, tokens, P("seq"), P("seq"), P("seq", None), P("seq", None), P("seq", None), P("seq"), P("seq"), P("seq"))
    return jax.shard_map(body, mesh=mesh, in_specs=in_specs, out_specs=out_specs, check_vma=False)
```

time: 72.5 us -> 66.9 us (0.923)
  Pallas kernels: 16 us -> 10.8 us
    pallas_call x4, Pallas kernels: 16 us -> 10.8 us  [call(): pl.pallas_call(run, out_shape=[pltpu.VMEM(s, d) if mode == 'vmem' else ja...]
where the time goes in v4:
time: 66.9 us; the launch traced here: 66.7 us
  blocking collectives  52.3 us (78%)
  Pallas kernels  10.8 us (16%)
  waiting for transfers between devices  2.83 us (4%)
  between operations  0.68 us (1%)
    all_to_all x1, blocking collectives, body(): lax.all_to_all(packed, 'seq', split_axis=0, concat_axis=0, tiled=True, ax...  27.8 us
    all_to_all x1, blocking collectives, body(): lax.all_to_all(k1['ends'], 'seq', split_axis=0, concat_axis=0, tiled=True)  24.5 us
    pallas_call x4, Pallas kernels, call(): pl.pallas_call(run, out_shape=[pltpu.VMEM(s, d) if mode == 'vmem' else ja...  10.8 us
    ppermute x1, waiting for transfers between devices, body(): got = lax.ppermute(k2['send'], 'seq', [(i, i ^ 1) for i in range(N)])  2.83 us
  transfers between devices with their start and end apart: 1, of which 1 were waited for; matrix products, arithmetic and copies ran while one was open for 0% of the time, Pallas kernels for 0%

profile of v4, /device:TPU:0, one launch (start us, length us, event | category | flops | bytes accessed | tf_op | source)
XLA Modules:
  0.0 66.7 jit_solution(15250249241594892109)
XLA Ops:
  0.6 3.4 %shard_map.204 = (bf16[256,512]{1,0:T(8,128)(2,1)S(1)}, f32[256,512]{1,0:T(8,128)S(1)}, f32[256,128]{1,0:T(8,128)S(1)}, bf16[256,512]{1,0:T(8,128)(2,1)S(1)}, f3...) custom-call(bf16[256,512]{1,0:T(8,128)(2,1)} %bitcast.16, ...), custom_call_target="tpu_custom_call" | custom-call | flops 300000000 | bytes 3000000 | tf_op jit(solution)/shard_map/pallas_call | solution.py:278
  4.1 24.5 %all_to_all.10.refs_0_.refs_2_ = bf16[128,2,8,128]{3,2,1,0:T(8,128)(2,1)S(1)} all-to-all(bf16[128,2,8,128]{3,2,1,0:T(8,128)(2,1)S(1)} %get-tuple-element.41), channel_id=1, replica_groups=mesh['seq'=128] {'seq'}, dimensions={0} | all-to-all | bytes 1048576 | tf_op jit(solution)/shard_map/all_to_all | solution.py:688
  28.6 3.9 %shard_map.205 = (bf16[256,512]{1,0:T(8,128)(2,1)}, f32[256,512]{1,0:T(8,128)S(1)}, bf16[64,8,1152]{2,1,0:T(8,128)(2,1)S(1)}, bf16[64,8,1152]{2,1,0:T(8,128)(2,1)S(1)}) custom-call(bf16[128,2,8,128]{3,2,1,0:T(8,128)(2,1)S(1)} %all_to_all.10.refs_0_.refs_2_, f32[54,8,128]{2,1,0:T(8,128)S(1)} %get-tuple-element.42.refs_1_.refs_3_, ...), custom_call_target="tpu_custom_call" | custom-call | flops 1600000000 | bytes 6000000 | tf_op jit(solution)/shard_map/pallas_call | solution.py:278
  32.5 0.1 collective-permute-start
  32.6 2.8 %collective-permute-done.refs_1_ = bf16[64,8,1152]{2,1,0:T(8,128)(2,1)S(1)} collective-permute-done((bf16[64,8,1152]{2,1,0:T(8,128)(2,1)S(1)}, bf16[64,8,1152]{2,1,0:T(8,128)(2,1)S(1)}, u32[]{:S(2)}, u32[]{:S(2)}) %collective-permute-start) | collective-permute-done | bytes 1179680 | tf_op jit(solution)/shard_map/ppermute | solution.py:697
  35.4 0.3 shard_map.206
  35.7 27.8 %all_to_all.11.refs_0_ = bf16[64,8,1408]{2,1,0:T(8,128)(2,1)S(1)} all-to-all(bf16[64,8,1408]{2,1,0:T(8,128)(2,1)S(1)} %shard_map.206), channel_id=1, replica_groups={{0,2,4,6,8,10,12,14,16,18,20,22,24,26,28,30,32,34,36,38,40,42,44,46,48,..., dimensions={0} | all-to-all | bytes 2883584 | tf_op jit(solution)/shard_map/all_to_all | solution.py:702
  63.6 3.1 %shard_map.207 = (bf16[256,512]{1,0:T(8,128)(2,1)}, f32[4,512]{1,0:T(4,128)}, f32[4,512]{1,0:T(4,128)}, f32[4,1024]{1,0:T(4,128)}, f32[1,4]{1,0:T(1,128)}, /*ind...) custom-call(bf16[64,8,1408]{2,1,0:T(8,128)(2,1)S(1)} %all_to_all.11.refs_0_, ...), custom_call_target="tpu_custom_call" | custom-call | flops 600000000 | bytes 5000000 | tf_op jit(solution)/shard_map/pallas_call | solution.py:278
Async XLA Ops:
  32.5 2.9 %collective-permute-start = (bf16[64,8,1152]{2,1,0:T(8,128)(2,1)S(1)}, bf16[64,8,1152]{2,1,0:T(8,128)(2,1)S(1)}, u32[]{:S(2)}, u32[]{:S(2)}) collective-permute-start(bf16[64,8,1152]{2,1,0:T(8,128)(2,1)S(1)} %get-tuple-element.57), channel_id=1, source_target_pairs={{0,1},{1,0},{2,3},{3,2},{4,5},{5,4},{6,7},{7,6},{8,9},{9,8},{10,11... | collective-permute-start | bytes 3538952 | tf_op jit(solution)/shard_map/ppermute | solution.py:697

commit v5 on v4

v5 whole, which is shorter than its diff:
```python
import functools

import jax
import jax.numpy as jnp
import numpy as np
from jax import lax
from jax.experimental import pallas as pl
from jax.experimental.pallas import tpu as pltpu
from jax.sharding import PartitionSpec as P

F32 = jnp.float32
BF16 = jnp.bfloat16
VMEM_LIMIT = 40 * 1024 * 1024
TOK = 128
GROUPS = TOK // 8
MICRO = 2
HALVES = 2
N = 128
CHIPS = 64


def deal():
    out = np.zeros((256, 256), np.float32)
    for n in range(128):
        out[2 * n, n] = 1.0
        out[2 * n + 1, 128 + n] = 1.0
    return out


def dot(a, b):
    return jnp.dot(a, b, preferred_element_type=F32)


def dot_tn(a, b):
    return lax.dot_general(a, b, (((0,), (0,)), ((), ())), preferred_element_type=F32)


def dot_nt(a, b):
    return lax.dot_general(a, b, (((1,), (1,)), ((), ())), preferred_element_type=F32)


def cmul(a, b):
    return (a[0] * b[0] - a[1] * b[1], a[0] * b[1] + a[1] * b[0])


def conj(a):
    return (a[0], -a[1])


def rows_iota(shape=(8, 128)):
    return lax.broadcasted_iota(jnp.int32, shape, len(shape) - 2)


def rest(w):
    small = jnp.minimum(w, 0.5)
    poly = 1.0 - small * (1.0 / 11.0)
    for k in range(10, 1, -1):
        poly = 1.0 - small * (1.0 / k) * poly
    return jnp.where(w < 0.5, small * poly, 1.0 - jnp.exp(-w))


def params(log_rate, angle):
    u = jnp.exp(log_rate)
    r = jnp.where(u < 0.5, 1.0 - rest(u), jnp.exp(-u))
    lam = (r * jnp.cos(angle), r * jnp.sin(angle))
    return u, r, lam, jnp.sqrt(rest(2.0 * u))


def powers(lam, count):
    out = [lam]
    for _ in range(count):
        out.append(cmul(out[-1], out[-1]))
    return out


def spread_rows(pair, half):
    return tuple(jnp.broadcast_to(v[half : half + 1, :], (8, 128)) for v in pair)


def scan_tables(pows, reverse):
    row = rows_iota()
    pos = (7 - row) if reverse else row
    levels = []
    for s, p in ((1, pows[0]), (2, pows[1]), (4, pows[2])):
        keep = pos >= s
        levels.append((s, (jnp.where(keep, p[0], 0.0), jnp.where(keep, p[1], 0.0))))
    e = pos + 1
    table = (jnp.ones((8, 128), F32), jnp.zeros((8, 128), F32))
    for bit in range(4):
        on = (lax.shift_right_logical(e, bit) & 1) == 1
        table = cmul(table, (jnp.where(on, pows[bit][0], 1.0), jnp.where(on, pows[bit][1], 0.0)))
    return levels, table


def group_scan(x, levels, reverse):
    xr, xi = x
    for s, (mr, mi) in levels:
        shift = 8 - s if reverse else s
        rr = pltpu.roll(xr, shift, 1)
        ri = pltpu.roll(xi, shift, 1)
        xr, xi = xr + (mr * rr - mi * ri), xi + (mr * ri + mi * rr)
    return xr, xi


def tile_rows(parts):
    rows = []
    for comp in range(2):
        for micro in range(MICRO):
            for half in range(HALVES):
                rows.append(parts[(micro, half)][comp])
    return jnp.concatenate(rows, axis=0)


def tile_lam(p):
    row = rows_iota()
    odd = (row & 1) == 1
    re = jnp.where(odd, p[1][0], p[0][0])
    im = jnp.where(odd, p[1][1], p[0][1])
    return re, jnp.where(row < 4, -im, im)


def tile_mul(c, coef):
    return c * coef[0] + pltpu.roll(c, 4, 0) * coef[1]


def gather_carry(ends_ref, chip, dmax, coef, coef8):
    chains = []
    for chain in range(4):
        acc = None
        for i in range(7, -1, -1):
            d = chain * 8 + i
            at = jnp.maximum(chip - 1 - d, 0)
            e = ends_ref[at, 0].astype(F32) + ends_ref[at, 1].astype(F32)
            e = jnp.where(d <= dmax, e, 0.0)
            acc = e if acc is None else tile_mul(acc, coef) + e
        chains.append(acc)
    out = chains[3]
    for chain in range(2, -1, -1):
        out = tile_mul(out, coef8) + chains[chain]
    return out


def segment_tile(lengths_ref, chip):
    second = (rows_iota() & 2) == 2
    base = chip * 2 * TOK
    ahead = []
    for micro in range(MICRO):
        first, at = jnp.int32(0), jnp.int32(0)
        for slot in range(16):
            first = jnp.where(at <= base, jnp.maximum(first, at), first)
            at = at + lengths_ref[micro, slot]
        ahead.append((base - first) // (2 * TOK) - 1)
    return jnp.where(second, ahead[1], ahead[0]).astype(F32)


def groups_of(value, micro_groups=MICRO * GROUPS):
    return value.reshape(micro_groups, 8, 128)


def split_channels(value):
    out = []
    for half in range(HALVES):
        c = 256 * half
        out.append((groups_of(value[:, c : c + 128]), groups_of(value[:, c + 128 : c + 256])))
    return out


def join_channels(halves):
    cols = []
    for re, im in halves:
        cols.append(re.reshape(MICRO * TOK, 128))
        cols.append(im.reshape(MICRO * TOK, 128))
    return jnp.concatenate(cols, axis=1)


def permute(value_bf, matrix):
    return jnp.concatenate([dot(value_bf[:, :256], matrix), dot(value_bf[:, 256:], matrix)], axis=1)


def layer_norm(x):
    mean = jnp.mean(x, axis=1, keepdims=True)
    centered = x - mean
    var = jnp.mean(centered * centered, axis=1, keepdims=True)
    rstd = lax.rsqrt(var + 1e-05)
    return centered * rstd, rstd


def chain_from(x, micro, step8, init, reverse):
    before = {}
    v = init
    order = range(GROUPS - 1, -1, -1) if reverse else range(GROUPS)
    for g in order:
        before[g] = v
        xr, xi = x[0][micro * GROUPS + g], x[1][micro * GROUPS + g]
        if v is None:
            v = (xr, xi)
        else:
            m = cmul(v, step8)
            v = (xr + m[0], xi + m[1])
    return before, v


def edge_bcast(pair, edge):
    return tuple(jnp.broadcast_to(p[edge : edge + 1, :], (8, 128)) for p in pair)


HELD, LOAD, COPY, SCALARS, PLAIN = range(5)


class Bag:
    pass


class Ports:
    def __init__(self, ins, outs, refs):
        n_in, n_out = len(ins), len(outs)
        scratch = list(refs[n_in + n_out :])
        out_refs = {name: ref for (name, _, _, _), ref in zip(outs, refs[n_in:])}
        table, self.pending, self.leaving, self.out_copies = {}, {}, [], {}
        sems = scratch.pop() if scratch else None
        i = 0
        for (name, _, mode), ref in zip(ins, refs):
            table[name] = ref
            if mode == PLAIN:
                self.spare = sems.at[i]
                i += 1
            elif mode != HELD:
                target = out_refs[name] if mode == LOAD else scratch.pop(0)
                self.pending[name] = pltpu.make_async_copy(ref, target, sems.at[i])
                self.pending[name].start()
                table[name] = target
                i += 1
        for name, _, _, mode in outs:
            table.setdefault(name, out_refs[name])
            if mode == COPY:
                table[name] = scratch.pop(0)
                self.out_copies[name] = pltpu.make_async_copy(table[name], out_refs[name], sems.at[i])
                i += 1
        self.table = table
        self.refs = Bag()
        self.refs.__dict__.update(table)

    def __getattr__(self, name):
        if name in self.pending:
            self.pending.pop(name).wait()
        return self.table[name][...]

    def ready(self, **names):
        (name,) = names
        if name in self.pending:
            self.pending.pop(name).wait()
        return self.table[name]

    def settle(self, count):
        for name in list(self.pending)[:count]:
            self.pending.pop(name).wait()

    def put(self, **values):
        for name, value in values.items():
            self.table[name][...] = value
            if name in self.out_copies:
                self.out_copies[name].start()
                self.leaving.append(name)

    def finish(self):
        for copy in self.pending.values():
            copy.wait()
        for name in self.leaving:
            self.out_copies[name].wait()


def call(kernel, ins, outs, extra=(), flops=0, nbytes=0):
    ins = [(name, array, mode) for mode, group in ins for name, array in group.items()]
    outs = [(name, shape, kind, mode) for mode, group in outs for name, (shape, kind) in group.items()]
    outs += [(name, array.shape, array.dtype, HELD) for name, array, mode in ins if mode == LOAD]

    def run(*refs):
        n_extra = len(extra)
        ports = Ports(ins, outs, refs[: len(refs) - n_extra])
        kernel(ports, *refs[len(refs) - n_extra :])
        ports.finish()

    args, scratch, copies = [], [], 0
    for _, array, mode in ins:
        args.append(pltpu.with_memory_space_constraint(array, pltpu.VMEM if mode == HELD else pltpu.HBM))
        copies += mode != HELD
        if mode in (COPY, SCALARS):
            scratch.append((pltpu.VMEM if mode == COPY else pltpu.SMEM)(array.shape, array.dtype))
    for _, shape, kind, mode in outs:
        if mode == COPY:
            scratch.append(pltpu.VMEM(shape, kind))
            copies += 1
    if copies:
        scratch.append(pltpu.SemaphoreType.DMA((copies,)))
    spec = lambda mode: pl.BlockSpec(memory_space=pltpu.VMEM if mode == HELD else pl.ANY)
    out = pl.pallas_call(
        run,
        out_shape=[pltpu.VMEM(s, d) if mode == HELD else jax.ShapeDtypeStruct(s, d) for _, s, d, mode in outs],
        in_specs=[spec(mode) for _, _, mode in ins],
        out_specs=[spec(mode) for _, _, _, mode in outs],
        scratch_shapes=scratch + list(extra),
        compiler_params=pltpu.CompilerParams(vmem_limit_bytes=VMEM_LIMIT),
        cost_estimate=pl.CostEstimate(flops=flops, bytes_accessed=nbytes, transcendentals=0),
    )(*args)
    made = Bag()
    made.__dict__.update({name: array for (name, _, _, _), array in zip(outs, out)})
    return made


def chunk_rows(left, right):
    w = left.shape[1]
    a = left.reshape(CHIPS, 8, w)
    b = right.reshape(CHIPS, 8, w)
    low = rows_iota((CHIPS, 8, w)) < 4
    return jnp.where(low, a, pltpu.roll(b, 4, 1)), jnp.where(low, pltpu.roll(a, 4, 1), b)


AHEAD, BACK, LEVEL, STEP, LAM, SCALE, RATE_U, RADIUS, PER_HALF = 0, 2, 4, 10, 12, 14, 15, 16, 17
COEF, COEF2, COEF8, COEF16, CHIPS_AHEAD, TABLES = 34, 36, 38, 40, 42, 43


def pair_of(tables, at, half):
    return tables[half * PER_HALF + at], tables[half * PER_HALF + at + 1]


def rows_of(tables, half):
    return [tables[half * PER_HALF + at][0:1, :] for at in (RATE_U, RADIUS, LAM, LAM + 1, SCALE)]


def coefs_of(tables, at, forward):
    ci = tables[at + 1]
    return tables[at], (ci if forward else -ci)


def kernel_first(io):
    me = lax.axis_index("seq")
    copy = pltpu.make_async_copy(io.refs.b_tiles.at[me // 2], io.refs.b_rows, io.spare)
    copy.start()
    io.settle(8)
    tables = io.refs.tables
    x = io.x.astype(F32)
    xhat, rstd = layer_norm(x)
    normed = (xhat * io.gain + io.bias).astype(BF16)
    io.put(normed=normed)
    io.put(xhat=xhat)
    io.put(rstd=jnp.broadcast_to(rstd, (MICRO * TOK, 128)))
    u, r, lam, scale = params(io.log_rate, io.angle)
    pows = powers(lam, 11)
    proj = dot(normed, io.b).astype(BF16)
    pairs = permute(proj, io.deal)
    io.put(pairs=pairs.astype(BF16))
    halves = split_channels(pairs)
    parts, scanned = {}, []
    for half in range(HALVES):
        mine = [spread_rows(p, half) for p in pows[:4]]
        (scale8,) = spread_rows((scale,), half)
        levels, table = scan_tables(mine, False)
        re, im = halves[half]
        x8 = group_scan((re * scale8, im * scale8), levels, False)
        scanned.append(x8)
        for micro in range(MICRO):
            _, v = chain_from(x8, micro, mine[3], None, False)
            parts[(micro, half)] = (v[0][7:8, :], v[1][7:8, :])
        back_levels, back_table = scan_tables([conj(p) for p in mine], True)
        values = list(table) + list(back_table) + [v for _, level in back_levels for v in level] + list(mine[3]) + list(mine[0])
        for at, value in enumerate(values + [scale8] + list(spread_rows((u, r), half))):
            tables[half * PER_HALF + at] = value
    last = tile_rows(parts)
    io.put(last=last)
    even, odd = chunk_rows(xhat[:TOK].T, xhat[TOK:].T)
    io.put(columns=jnp.where(me % 2 == 0, even, odd).astype(BF16))
    send = io.refs.send
    send[0:CHIPS] = jnp.where(me % 2 == 0, odd, even).astype(BF16)
    for i, part in enumerate(in_parts(last, 2)):
        send[CHIPS + i] = part
    io.put(local=join_channels(scanned))
    for to, at in ((COEF, 7), (COEF2, 8), (COEF8, 10), (COEF16, 11)):
        tables[to], tables[to + 1] = tile_lam([spread_rows(pows[at], half) for half in range(HALVES)])
    tables[CHIPS_AHEAD] = segment_tile(io.ready(lengths=0), me // 2)
    copy.wait()


def kernel_join(io):
    core = lax.axis_index("seq") % 2
    own, got = io.last, io.refs.got
    other = got[CHIPS].astype(F32) + got[CHIPS + 1].astype(F32)
    first, second = jnp.where(core == 0, own, other), jnp.where(core == 0, other, own)
    whole = second + tile_mul(first, coefs_of(io.refs.tables, COEF, True))
    io.put(inside=jnp.where(core == 0, 0.0, other))
    ends = io.refs.ends
    for i, part in enumerate(in_parts(whole, 2)):
        ends[:, i] = jnp.broadcast_to(part[None], (CHIPS, 8, 128))
    ends[:, 2] = io.columns
    ends[:, 3] = got[0:CHIPS]


def tile_row(tile, comp, micro, half):
    at = comp * 4 + micro * 2 + half
    return jnp.broadcast_to(tile[at : at + 1, :], (8, 128))


def total(v):
    return jnp.sum(jnp.sum(v, axis=0), axis=0, keepdims=True)


def column_sum(v):
    return jnp.sum(v, axis=0, keepdims=True)


def in_parts(value, count):
    parts = []
    for _ in range(count):
        parts.append(value.astype(BF16))
        value = value - parts[-1].astype(F32)
    return parts


def choose(value, one_hot):
    out = dot(jnp.concatenate([p.astype(F32) for p in in_parts(value, 3)], axis=0).astype(BF16), one_hot)
    return out[0:8, :] + out[8:16, :] + out[16:24, :]


def one_hots(each, width):
    at = np.arange(N)
    device = 2 * (at % CHIPS) + at // CHIPS
    out = np.zeros((each, N, width), np.float32)
    for j in range(each):
        out[j, at, each * device + j] = 1.0
    return out


def place_smalls(fours, twos, chosen4, chosen2):
    out = jnp.zeros((N, 128), F32)
    for rows, chosen, each in ((fours, chosen4, 4), (twos, chosen2, 2)):
        width = rows[0].shape[1]
        high = [v.astype(BF16).astype(F32) for v in rows]
        block = high + [v - h for v, h in zip(rows, high)]
        block.append(jnp.zeros((-len(block) % 8, width), F32))
        block = jnp.concatenate(block, axis=0).astype(F32)
        for j in range(each):
            above = 64 * (j // 2) + 40 + 8 * (j % 2) if each == 4 else 64 * j
            spread = [jnp.zeros((above, width), F32)] if above else []
            spread += [block, jnp.zeros((128 - above - block.shape[0], width), F32)]
            out = out + dot_nt(chosen[j], jnp.concatenate(spread, axis=0).astype(BF16))
    return out


def chain_rule(rows, d_re, d_im, d_scale):
    u, r, lr, li, scale = rows
    return u * (r * r * d_scale / scale - (lr * d_re + li * d_im)), lr * d_im - li * d_re


def kernel_middle(io):
    me = lax.axis_index("seq")
    core = me % 2
    tables = io.refs.tables
    carry = gather_carry(io.refs.ends, me // 2, tables[CHIPS_AHEAD], coefs_of(tables, COEF2, True), coefs_of(tables, COEF16, True))
    carry = jnp.where(core == 0, carry, io.inside + tile_mul(carry, coefs_of(tables, COEF, True)))
    local = split_channels(io.local)
    row = rows_iota((MICRO * GROUPS, 8, 128))
    states, priors = [], []
    for half in range(HALVES):
        table, step8 = pair_of(tables, AHEAD, half), pair_of(tables, STEP, half)
        x8 = local[half]
        before_r, before_i = [], []
        for micro in range(MICRO):
            init = (tile_row(carry, 0, micro, half), tile_row(carry, 1, micro, half))
            before, _ = chain_from(x8, micro, step8, init, False)
            for g in range(GROUPS):
                edge = edge_bcast(before[g], 7)
                before_r.append(edge[0])
                before_i.append(edge[1])
        br, bi = jnp.stack(before_r), jnp.stack(before_i)
        hr = x8[0] + (table[0] * br - table[1] * bi)
        hi = x8[1] + (table[0] * bi + table[1] * br)
        states.append((hr, hi))
        priors.append((jnp.where(row == 0, br, pltpu.roll(hr, 1, 1)), jnp.where(row == 0, bi, pltpu.roll(hi, 1, 1))))
    hidden = permute(join_channels(states).astype(BF16), io.deal_back).astype(BF16)
    normed = io.normed
    y = dot(hidden, io.c) + io.skip * normed.astype(F32)
    k0, k1 = 0.7978845608028654, 0.044715
    yy = y * y
    t = jnp.tanh(k0 * (y + k1 * (yy * y)))
    act = (0.5 * y * (1.0 + t)).astype(BF16)
    slope = 0.5 * (1.0 + t) + 0.5 * y * (1.0 - t * t) * (k0 * (1.0 + 3.0 * k1 * yy))
    gated = dot(act, io.glu)
    value, gate = gated[:, :512], gated[:, 512:]
    sig = jax.nn.sigmoid(gate)
    go = io.go.astype(F32)
    io.put(out=(io.x.astype(F32) + value * sig).astype(BF16))
    gs = go * sig
    dgated = jnp.concatenate([gs, gs * value * (1.0 - sig)], axis=1).astype(BF16)
    dy = (dot_nt(dgated, io.glu) * slope).astype(BF16)
    dhidden = dot_nt(dy, io.c).astype(BF16)
    q = split_channels(permute(dhidden, io.deal))
    parts, scanned = {}, []
    for half in range(HALVES):
        step8 = conj(pair_of(tables, STEP, half))
        levels = [(1 << n, pair_of(tables, LEVEL + 2 * n, half)) for n in range(3)]
        x8 = group_scan(q[half], levels, True)
        scanned.append(x8)
        for micro in range(MICRO):
            _, v = chain_from(x8, micro, step8, None, True)
            parts[(micro, half)] = (v[0][0:1, :], v[1][0:1, :])
    io.put(first=tile_rows(parts), carry=carry, act=act, dgated=dgated, hidden=hidden, dy=dy, back=join_channels(scanned), prior=join_channels(priors))


def by_core(ref_keep, ref_send, core, even, odd):
    ref_keep[...] = jnp.where(core == 0, even, odd).astype(BF16)
    ref_send[...] = jnp.where(core == 0, odd, even).astype(BF16)


def kernel_products(io):
    core = lax.axis_index("seq") % 2
    glu_grad = dot_tn(io.act, io.dgated)
    c_grad = dot_tn(io.hidden, io.dy)
    even, odd = chunk_rows(glu_grad[:, :768], jnp.concatenate([glu_grad[:, 768:], c_grad], axis=1))
    by_core(io.refs.keep, io.refs.send, core, even, odd)


def kernel_carried(io):
    core = lax.axis_index("seq") % 2
    tables = io.refs.tables
    own, other = io.first, io.other
    first, second = jnp.where(core == 0, own, other), jnp.where(core == 0, other, own)
    whole = first + tile_mul(second, coefs_of(tables, COEF, False))
    io.put(chip_first=whole.astype(BF16))
    inside = jnp.where(core == 0, other, 0.0)
    far_step = [(tables[COEF][half : half + 1, :], tables[COEF + 1][4 + half : 5 + half, :]) for half in range(HALVES)]
    back, priors, pairs = split_channels(io.back), split_channels(io.prior), split_channels(io.pairs.astype(F32))
    projs, rates, angles, heads, tails = [], [], [], {}, {}
    for half in range(HALVES):
        table, step8 = pair_of(tables, BACK, half), conj(pair_of(tables, STEP, half))
        from_start = conj(pair_of(tables, AHEAD, half))
        from_start = [jnp.where(rows_iota() == 0, edge, pltpu.roll(t, 1, 0)) for edge, t in zip((1.0, 0.0), from_start)]
        scale = tables[half * PER_HALF + SCALE]
        x8 = back[half]
        after_r, after_i = [], []
        for micro in range(MICRO):
            init = (tile_row(inside, 0, micro, half), tile_row(inside, 1, micro, half))
            after, _ = chain_from(x8, micro, step8, init, True)
            for g in range(GROUPS):
                edge = edge_bcast(after[g], 0)
                after_r.append(edge[0])
                after_i.append(edge[1])
        ar, ai = jnp.stack(after_r), jnp.stack(after_i)
        gr = x8[0] + (table[0] * ar - table[1] * ai)
        gi = x8[1] + (table[0] * ai + table[1] * ar)
        pr, pi = priors[half]
        d_re = total(gr * pr + gi * pi)
        d_im = total(gi * pr - gr * pi)
        d_scale = total(gr * pairs[half][0] + gi * pairs[half][1])
        for micro in range(MICRO):
            used = tuple(io.carry[4 * comp + 2 * micro + half : 4 * comp + 2 * micro + half + 1, :] for comp in range(2))
            _, v = chain_from((gr, gi), micro, step8, None, True)
            m = cmul(v, from_start)
            tails[(micro, half)] = (column_sum(m[0]), column_sum(m[1]))
            m = cmul(tails[(micro, half)], conj(used))
            d_re, d_im = d_re - m[0], d_im - m[1]
            _, v = chain_from(priors[half], micro, conj(step8), None, False)
            m = cmul(v, conj(table))
            more = cmul(far_step[half], used)
            m = (column_sum(m[0]) - TOK * more[0], column_sum(m[1]) - TOK * more[1])
            far = cmul(m, far_step[half])
            heads[(micro, half)] = tuple(jnp.where(core == 0, f, n) for f, n in zip(far, m))
        rate, turn = chain_rule(rows_of(tables, half), d_re, d_im, d_scale)
        rates.append(rate)
        angles.append(turn)
        projs.append((gr * scale, gi * scale))
    dproj = permute(join_channels(projs).astype(BF16), io.deal_back).astype(BF16)
    dyf, normed = io.dy.astype(F32), io.normed
    dnormed = dot_nt(dproj, io.b) + io.skip * dyf
    io.put(dnormed=dnormed)
    fours = [column_sum(dnormed * io.xhat), column_sum(dnormed), column_sum(dyf * normed.astype(F32))]
    join = lambda two: jnp.concatenate(two, axis=1)
    twos = [join(rates), join(angles)]
    of_tile = lambda tile, at: join([tile[at : at + 1, :], tile[at + 1 : at + 2, :]])
    last = io.last
    for micro in range(MICRO):
        for sums in (tails, heads):
            twos += [join([sums[(micro, half)][comp] for half in range(HALVES)]) for comp in range(2)]
        twos += [of_tile(tile, 4 * comp + 2 * micro) for tile in (last, whole) for comp in range(2)]
    smalls = place_smalls(fours, twos, io.chosen4, io.chosen2)
    b_grad = dot_tn(normed, dproj)
    even, odd = chunk_rows(b_grad[:, :256], b_grad[:, 256:])
    tiles = [jnp.broadcast_to(v[:, None, :], (CHIPS, 8, 128)) for v in (smalls[:CHIPS], smalls[CHIPS:])]
    by_core(io.refs.keep, io.refs.send, core, jnp.concatenate([even, tiles[0]], axis=2), jnp.concatenate([odd, tiles[1]], axis=2))


def kernel_pack(io):
    out = io.refs.packed
    out[:, :, 0:768] = (io.keep.astype(F32) + io.got.astype(F32)).astype(BF16)
    keep, got = io.keep_b.astype(F32), io.got_b.astype(F32)
    out[:, :, 768:1024] = (keep[:, :, 0:256] + got[:, :, 0:256]).astype(BF16)
    out[:, :, 1024:1152] = jnp.broadcast_to(io.chip_first[None], (CHIPS, 8, 128))
    low = rows_iota((CHIPS, 8, 128)) < 4
    out[:, :, 1152:1280] = jnp.where(low, keep[:, :, 256:384], got[:, :, 256:384]).astype(BF16)


def segment_joins(lengths_ref):
    second = (rows_iota() & 2) == 2
    bits = []
    for micro in range(MICRO):
        mask, at = jnp.int32(0), jnp.int32(0)
        for slot in range(16):
            unit = lax.shift_left(jnp.int32(1), jnp.minimum(at // (8 * TOK), 15))
            mask = jnp.where(at < N * TOK, mask | unit, mask)
            at = at + lengths_ref[micro, slot]
        bits.append(mask)
    pick = lambda two: jnp.where(second, two[1], two[0]).astype(F32)
    return [pick([1 - (lax.shift_right_logical(b, g + 1) & 1) for b in bits]) for g in range(15)], bits


def kernel_ahead(io):
    me = lax.axis_index("seq")
    tables = io.refs.tables
    near, far = [], []
    for half in range(HALVES):
        step8 = conj(pair_of(tables, STEP, half))
        tiles = [pair_of(tables, BACK, half)]
        for _ in range(2 * GROUPS - 1):
            tiles.append(cmul(tiles[-1], step8))
        tiles = tiles[::-1]
        for comp in range(2):
            far.append(jnp.concatenate([t[comp] for t in tiles[:GROUPS]], axis=0))
            near.append(jnp.concatenate([t[comp] for t in tiles[GROUPS:]], axis=0))
    near, far = jnp.concatenate(near, axis=1), jnp.concatenate(far, axis=1)
    sums = jnp.concatenate([column_sum(near) + column_sum(far), jnp.zeros((7, 512), F32)], axis=0)
    io.put(reach=near, reach_sum=sums, reach_low=jnp.concatenate([far, near], axis=0).astype(BF16))
    ends = io.refs.ends
    own, other = (ends[:, i].reshape(CHIPS * 8, 128) for i in (2, 3))
    first = me % 2 == 0
    io.put(columns=jnp.concatenate([jnp.where(first, own, other), jnp.where(first, other, own)], axis=1))
    lane = lax.broadcasted_iota(jnp.int32, (128, 128), 0)
    col = lax.broadcasted_iota(jnp.int32, (128, 128), 1)
    w = lane % 64
    hot = lambda where: jnp.where(where, 1.0, 0.0).astype(BF16)
    spot = jnp.where((w >= 40) & (w < 56) & (w % 8 < 6), 4 * (w % 8 % 3) + 2 * (lane // 64) + (w - 40) // 8, -1)
    spot = jnp.where(w < 36, jnp.where(w % 18 < 2, 12 + 2 * (w % 18) + lane // 64, -1), spot)
    channel = (lane // 64) == col % 2
    wanted = lambda k: hot(channel & (w < 36) & (w % 18 == 2 + 8 * ((col // 2) % 2) + k))
    io.put(pick=jnp.concatenate([hot(spot == col)] + [wanted(k) for k in range(8)], axis=1))
    half_rows = [jnp.concatenate(rows_of(tables, half) + [jnp.zeros((3, 128), F32)], axis=0) for half in range(HALVES)]
    mine = choose(jnp.where(me // 64 == 0, half_rows[0], half_rows[1]), hot(lane == (2 * me) % 128 + col % 2))
    io.put(channels=mine)
    pows = powers((mine[2:3, :], mine[3:4, :]), 10)
    io.put(channel_pows=jnp.concatenate([v for at in (7, 8, 10) for v in pows[at]] + [jnp.zeros((2, 128), F32)], axis=0))
    feature = lax.broadcasted_iota(jnp.int32, (8, 512), 1)
    here = feature == 4 * me + rows_iota((8, 512)) % 4
    b_rows = io.b_rows.astype(F32)
    b_rows = jnp.where(me % 2 == 0, b_rows, pltpu.roll(b_rows, 4, 0))
    at_row = lambda v: jnp.broadcast_to(jnp.sum(jnp.where(here, v, 0.0), axis=1, keepdims=True), (8, 512))
    io.put(mine=jnp.concatenate([at_row(io.gain), at_row(io.bias), b_rows], axis=1))
    joins, bits = segment_joins(io.ready(lengths=0))
    for group, tile in enumerate(joins):
        io.refs.joined[group] = tile
    group = lax.broadcasted_iota(jnp.int32, (16, 128), 0)
    second = (lax.broadcasted_iota(jnp.int32, (16, 128), 1) // 2) % 2 == 1
    opens = lax.shift_right_logical(jnp.where(second, bits[1], bits[0]), group) & 1
    io.put(opens=opens.astype(F32))


def all_carries(first, tables, joined):
    coef2, coef8 = (coefs_of(tables, at, False) for at in (COEF2, COEF8))
    groups = first.reshape(16, 4, 8, 128)
    step = lambda c, by: c * by[0] + pltpu.roll(c, 4, 1) * by[1]
    inner = [None] * 4
    inner[3] = jnp.zeros((16, 8, 128), F32)
    for p in range(2, -1, -1):
        inner[p] = groups[:, p + 1] + step(inner[p + 1], coef2)
    whole = groups[:, 0] + step(inner[0], coef2)
    entering = [None] * 16
    entering[15] = jnp.zeros((8, 128), F32)
    for g in range(14, -1, -1):
        entering[g] = (whole[g + 1] + tile_mul(entering[g + 1], coef8)) * joined[g]
    factor = jnp.stack(entering)
    out = []
    for p in range(3, -1, -1):
        out.append(inner[p] + factor)
        factor = step(factor, coef2)
    return jnp.stack(out[::-1], axis=1).reshape(CHIPS, 8, 128)


def kernel_last(io, carries, split):
    me = lax.axis_index("seq")
    core = me % 2
    tables = io.refs.tables
    parts = io.refs.parts
    enter = all_carries(parts[:, :, 1024:1152].astype(F32), tables, io.refs.joined)
    carries[...] = enter
    mine = carries[me // 2]
    mine = jnp.where(core == 0, tile_mul(mine, coefs_of(tables, COEF, False)), mine)
    reach_cols = io.reach
    reach = [(reach_cols[:, c : c + 128], reach_cols[:, c + 128 : c + 256]) for c in (0, 256)]
    scale_row = jnp.concatenate([tables[half * PER_HALF + SCALE][0:1, :] for half in (0, 0, 1, 1)], axis=1)
    rows = []
    for micro in range(MICRO):
        cols = []
        for half in range(HALVES):
            nr, ni = tile_row(mine, 0, micro, half)[0:1, :], tile_row(mine, 1, micro, half)[0:1, :]
            lr, li = reach[half]
            cols += [lr * nr - li * ni, lr * ni + li * nr]
        rows.append(jnp.concatenate(cols, axis=1))
    dproj = jnp.concatenate(rows, axis=0) * scale_row
    dproj = permute(dproj.astype(BF16), io.deal_back).astype(BF16)
    dnormed = dot_nt(dproj, io.b) + io.dnormed
    xhat, rstd = io.xhat, io.rstd[:, 0:1]
    dx = dnormed * io.gain
    m1 = jnp.mean(dx, axis=1, keepdims=True)
    m2 = jnp.mean(dx * xhat, axis=1, keepdims=True)
    io.put(in_grad=(io.go.astype(F32) + rstd * (dx - m1 - xhat * m2)).astype(BF16))
    summed = jnp.sum(parts[:, :, 0:1024].astype(F32), axis=0)
    io.put(glu_grad=jnp.concatenate([summed[0:4, 0:768], summed[4:8, 0:256]], axis=1))
    io.put(c_grad=summed[4:8, 256:768])
    moved = dot(io.columns, io.reach_low)
    low = rows_iota((CHIPS, 8, 128)) < 4
    spread = lambda comp, half: jnp.where(low, enter[:, comp * 4 + half : comp * 4 + half + 1, :], enter[:, comp * 4 + 2 + half : comp * 4 + 3 + half, :])
    cols = []
    for half in range(HALVES):
        c = 256 * half
        mr = moved[:, c : c + 128].reshape(CHIPS, 8, 128)
        mi = moved[:, c + 128 : c + 256].reshape(CHIPS, 8, 128)
        nr, ni = spread(0, half), spread(1, half)
        cols += [jnp.sum(mr * nr - mi * ni, axis=0), jnp.sum(mr * ni + mi * nr, axis=0)]
    rows8 = jnp.concatenate(cols, axis=1)
    rows8 = rows8 + pltpu.roll(rows8, 4, 0)
    enter_sum = jnp.sum(enter, axis=0)
    reach_sum = io.reach_sum[0:1, :]
    cols = []
    for half in range(HALVES):
        c = 256 * half
        fold2 = lambda comp: enter_sum[comp * 4 + half : comp * 4 + half + 1, :] + enter_sum[comp * 4 + 2 + half : comp * 4 + 3 + half, :]
        nr, ni = fold2(0), fold2(1)
        lr, li = reach_sum[:, c : c + 128], reach_sum[:, c + 128 : c + 256]
        cols += [lr * nr - li * ni, lr * ni + li * nr]
    sums_row = jnp.concatenate(cols, axis=1)
    both = jnp.where(rows_iota((8, 512)) < 4, rows8, sums_row) * scale_row
    moved_x = jnp.concatenate([choose(both[:, :256], io.deal_back), choose(both[:, 256:], io.deal_back)], axis=1)
    moved_one = jnp.broadcast_to(moved_x[4:5, :], (8, 512))
    own = io.mine
    gain_f, bias_f, b_rows = own[:, 0:512], own[:, 512:1024], own[:, 1024:1536]
    b_sum = jnp.concatenate([summed[0:4, 768:1024], summed[4:8, 768:1024]], axis=1)
    io.put(b_grad=b_sum + (gain_f * moved_x + bias_f * moved_one)[0:4, :])
    gain_carry = jnp.sum(b_rows * moved_x, axis=1, keepdims=True)
    bias_carry = jnp.sum(b_rows * moved_one, axis=1, keepdims=True)
    small = parts[:, :, 1152:1280]
    own, other = small[:, 0, :].astype(F32), small[:, 4, :].astype(F32)
    sums = column_sum(own + other)
    gathered = choose(jnp.concatenate([sums, jnp.zeros((7, 128), F32)], axis=0), io.pick[:, 0:128])
    d_re, d_im, d_scale = owned_channels(own, other, core, io, split)
    rate, turn = chain_rule([io.channels[i : i + 1, :] for i in range(5)], d_re, d_im, d_scale)
    shift = lambda v, by: pltpu.roll(v, 128 - by, 1)
    diagonal = lax.broadcasted_iota(jnp.int32, (8, 128), 1) == rows_iota()
    to_lanes = lambda v: column_sum(jnp.where(diagonal, v, 0.0))
    sums = gathered[0:1, :]
    io.put(gain_grad=(sums + to_lanes(gain_carry))[:, 0:4])
    io.put(bias_grad=(shift(sums, 4) + to_lanes(bias_carry))[:, 0:4])
    io.put(skip_grad=shift(sums, 8)[:, 0:4])
    io.put(rate_grad=(shift(sums, 12) + rate)[:, 0:2])
    io.put(angle_grad=(shift(sums, 14) + turn)[:, 0:2])


def group_chain(coef, value, opens, reverse):
    row = lax.broadcasted_iota(jnp.int32, (16, 128), 0)
    pos = 15 - row if reverse else row
    moved = lambda v, by: pltpu.roll(v, 16 - by if reverse else by, 0)
    opens = jnp.where(row == 0, 1.0, opens)
    keep = jnp.where(pos == 0, 0.0, 1.0 - (moved(opens, 1) if reverse else opens))
    a = (keep * coef[0], keep * coef[1])
    b = tuple(keep * moved(v, 1) for v in value)
    for by in (1, 2, 4, 8):
        inside = pos >= by
        before = lambda v: jnp.where(inside, moved(v, by), 0.0)
        pb, pa = tuple(before(v) for v in b), tuple(before(v) for v in a)
        m = cmul(a, pb)
        b = (b[0] + m[0], b[1] + m[1])
        a = cmul(a, pa)
    return b


def owned_channels(own, other, core, io, split):
    first, second = jnp.where(core == 0, own, other), jnp.where(core == 0, other, own)
    values = []
    for rows in (first, second):
        values.append(dot(rows.astype(BF16), io.pick[:, 128:1152]))
    pows = [tuple(io.channel_pows[2 * i + comp : 2 * i + comp + 1, :] for comp in range(2)) for i in range(3)]
    step, step2, step8 = pows
    of = lambda q, k: (values[q][:, 128 * k : 128 * k + 128], values[q][:, 128 * k + 128 : 128 * k + 256])
    plus = lambda x, y: (x[0] + y[0], x[1] + y[1])
    last0, last1 = of(0, 4), of(1, 4)
    kept = [*plus(last1, cmul(last0, step)), *of(0, 6), *of(0, 0), *of(1, 0), *plus(of(0, 2), of(1, 2)), *last0]
    for i, v in enumerate(kept):
        split[i] = v
    at = lambda i, p: (split[i, pl.ds(p, 16, stride=4), :], split[i + 1, pl.ds(p, 16, stride=4), :])
    ends, firsts = [at(0, p) for p in range(4)], [at(2, p) for p in range(4)]
    zero = (jnp.zeros((16, 128), F32), jnp.zeros((16, 128), F32))
    states, grads = [zero], [zero]
    for p in range(1, 4):
        states.append(plus(cmul(states[-1], step2), ends[p - 1]))
        grads.append(plus(cmul(grads[-1], conj(step2)), firsts[4 - p]))
    grads = grads[::-1]
    into = group_chain(step8, plus(cmul(states[3], step2), ends[3]), io.opens, False)
    back = group_chain(conj(step8), plus(cmul(grads[0], conj(step2)), firsts[0]), io.opens, True)
    d_lam, d_scale = zero, zero
    for p in range(4):
        states[p] = plus(states[p], into)
        into = cmul(into, step2)
        grads[3 - p] = plus(grads[3 - p], back)
        back = cmul(back, conj(step2))
    for p in range(4):
        h0, n = states[p], grads[p]
        far = cmul(h0, step)
        h1 = plus(far, at(10, p))
        seen = plus(cmul(far, step), cmul(h1, step))
        seen = plus(at(8, p), (TOK * seen[0], TOK * seen[1]))
        for x, y in ((at(4, p), h0), (at(6, p), h1), (n, seen)):
            d_lam = plus(d_lam, cmul(x, conj(y)))
        d_scale = plus(d_scale, cmul(n, conj(ends[p])))
    both = lambda v: (lambda t: t + pltpu.roll(t, 126, 1))(column_sum(v))
    d_re, d_im, s_re, s_im = (both(v) for v in d_lam + d_scale)
    lr, li, scale = (io.channels[i : i + 1, :] for i in (2, 3, 4))
    return d_re, d_im, (lr * s_re + li * s_im) / scale


def body(block_in, out_grad, lengths, ln_gain, ln_bias, b_proj, c_proj, glu_weight, skip_gain, log_rate, angle):
    rows = MICRO * TOK
    x = block_in.reshape(rows, 512)
    go = out_grad.reshape(rows, 512)
    gain, bias, skip = (v.reshape(1, 512) for v in (ln_gain, ln_bias, skip_gain))
    rate2, angle2 = log_rate.reshape(2, 128), angle.reshape(2, 128)
    spread = deal()
    deal_m = jnp.asarray(spread, BF16)
    back_m = jnp.asarray(spread.T.copy(), BF16)
    chosen4, chosen2 = jnp.asarray(one_hots(4, 512), BF16), jnp.asarray(one_hots(2, 256), BF16)
    full = (rows, 512)
    k1 = call(
        kernel_first,
        [
            (LOAD, dict(x=x, b=b_proj, deal=deal_m, gain=gain, bias=bias)),
            (COPY, dict(log_rate=rate2, angle=angle2)),
            (SCALARS, dict(lengths=lengths)),
            (LOAD, dict(deal_back=back_m, c=c_proj, skip=skip, glu=glu_weight, go=go, chosen4=chosen4, chosen2=chosen2)),
            (PLAIN, dict(b_tiles=b_proj.reshape(CHIPS, 8, 512))),
        ],
        [
            (
                HELD,
                dict(
                    normed=(full, BF16), xhat=(full, F32), rstd=((rows, 128), F32), pairs=(full, BF16), local=(full, F32),
                    send=((CHIPS + 2, 8, 128), BF16), columns=((CHIPS, 8, 128), BF16), tables=((TABLES, 8, 128), F32), b_rows=((8, 512), BF16),
                    last=((8, 128), F32),
                ),
            )
        ],
        flops=300_000_000, nbytes=3_000_000,
    )
    swap = functools.partial(lax.ppermute, axis_name="seq", perm=[(i, i ^ 1) for i in range(N)])
    same_core = [[2 * t + core for t in range(CHIPS)] for core in range(2)]
    exchange = functools.partial(lax.all_to_all, axis_name="seq", split_axis=0, concat_axis=0, tiled=True, axis_index_groups=same_core)
    kj = call(
        kernel_join, [(HELD, dict(last=k1.last, got=swap(k1.send), columns=k1.columns, tables=k1.tables))],
        [(HELD, dict(inside=((8, 128), F32), ends=((CHIPS, 4, 8, 128), BF16)))], flops=1_000_000, nbytes=1_000_000,
    )
    ends = exchange(kj.ends)
    k2 = call(
        kernel_middle,
        [
            (HELD, dict(deal_back=k1.deal_back, c=k1.c, skip=k1.skip, glu=k1.glu, go=k1.go)),
            (HELD, dict(ends=ends, inside=kj.inside, tables=k1.tables, local=k1.local, normed=k1.normed, deal=k1.deal, x=k1.x)),
        ],
        [
            (COPY, dict(out=(full, BF16))),
            (
                HELD,
                dict(
                    first=((8, 128), F32), carry=((8, 128), F32), act=(full, BF16), dgated=((rows, 1024), BF16), hidden=(full, BF16), dy=(full, BF16),
                    back=(full, F32), prior=(full, F32),
                ),
            ),
        ],
        flops=1_000_000_000, nbytes=6_000_000,
    )
    other = swap(k2.first)
    wide, narrow = ((CHIPS, 8, 768), BF16), ((CHIPS, 8, 384), BF16)
    kp = call(
        kernel_products, [(HELD, dict(act=k2.act, dgated=k2.dgated, hidden=k2.hidden, dy=k2.dy))], [(HELD, dict(keep=wide, send=wide))],
        flops=2_000_000_000, nbytes=3_000_000,
    )
    got = swap(kp.send)
    kc = call(
        kernel_carried,
        [
            (HELD, dict(carry=k2.carry, last=k1.last)),
            (HELD, dict(first=k2.first, other=other, back=k2.back, prior=k2.prior, dy=k2.dy, tables=k1.tables, pairs=k1.pairs, b=k1.b)),
            (HELD, dict(deal_back=k1.deal_back, normed=k1.normed, xhat=k1.xhat, skip=k1.skip, chosen4=k1.chosen4, chosen2=k1.chosen2)),
        ],
        [(HELD, dict(chip_first=((8, 128), BF16), dnormed=(full, F32), keep=narrow, send=narrow))],
        flops=6_000_000_000, nbytes=3_000_000,
    )
    got_b = swap(kc.send)
    ka = call(
        kernel_ahead,
        [
            (SCALARS, dict(lengths=lengths)),
            (HELD, dict(tables=k1.tables, ends=ends, gain=k1.gain, bias=k1.bias, b_rows=k1.b_rows, dnormed=kc.dnormed)),
        ],
        [
            (
                HELD,
                dict(
                    reach=((TOK, 512), F32), reach_sum=((8, 512), F32), reach_low=((2 * TOK, 512), BF16), columns=((CHIPS * 8, 256), BF16),
                    channels=((8, 128), F32), channel_pows=((8, 128), F32), opens=((16, 128), F32), pick=((128, 1152), BF16), mine=((8, 1536), F32), joined=((15, 8, 128), F32),
                ),
            )
        ],
        flops=200_000_000, nbytes=3_000_000,
    )
    packed = call(
        kernel_pack, [(HELD, dict(keep=kp.keep, got=got, keep_b=kc.keep, got_b=got_b, chip_first=kc.chip_first, reach=ka.reach))],
        [(HELD, dict(packed=((CHIPS, 8, 1280), BF16)))], flops=1_000_000, nbytes=2_400_000,
    ).packed
    parts = exchange(packed)
    four, two = ((1, 4), F32), ((1, 2), F32)
    k3 = call(
        kernel_last,
        [
            (HELD, dict(parts=parts, dnormed=kc.dnormed, go=k1.go, deal_back=k1.deal_back, tables=k1.tables, b=k1.b, xhat=k1.xhat, rstd=k1.rstd)),
            (HELD, dict(gain=k1.gain, reach=ka.reach, reach_sum=ka.reach_sum, reach_low=ka.reach_low, columns=ka.columns)),
            (HELD, dict(channels=ka.channels, channel_pows=ka.channel_pows, opens=ka.opens, pick=ka.pick, mine=ka.mine, joined=ka.joined)),
        ],
        [
            (COPY, dict(in_grad=(full, BF16), b_grad=((4, 512), F32), c_grad=((4, 512), F32), glu_grad=((4, 1024), F32))),
            (COPY, dict(gain_grad=four, bias_grad=four, skip_grad=four, rate_grad=two, angle_grad=two)),
        ],
        extra=[pltpu.VMEM((CHIPS, 8, 128), F32), pltpu.VMEM((12, CHIPS, 128), F32)], flops=600_000_000, nbytes=5_000_000,
    )
    return (
        k2.out.reshape(block_in.shape),
        k3.in_grad.reshape(block_in.shape),
        k3.gain_grad.reshape(4),
        k3.bias_grad.reshape(4),
        k3.b_grad,
        k3.c_grad,
        k3.glu_grad,
        k3.skip_grad.reshape(4),
        k3.rate_grad.reshape(2),
        k3.angle_grad.reshape(2),
    )


def solution(mesh):
    tokens = P(None, "seq", None)
    in_specs = (tokens, tokens) + (P(),) * 9
    out_specs = (tokens, tokens, P("seq"), P("seq"), P("seq", None), P("seq", None), P("seq", None), P("seq"), P("seq"), P("seq"))
    return jax.shard_map(body, mesh=mesh, in_specs=in_specs, out_specs=out_specs, check_vma=False)
```

time: 66.9 us -> 65.3 us (0.976)
  blocking collectives: 52.3 us -> 51.2 us
  starting transfers between devices: 0.09 us -> 0.85 us
  waiting for transfers between devices: 2.83 us -> 2.11 us
    all_to_all x2, blocking collectives: 52.3 us -> 51.2 us  [the longest x1 26.4 us: body(): parts = exchange(packed)]
    ppermute x1 -> x4, starting transfers between devices: 0.09 us -> 0.85 us  [the longest x1 0.57 us: body(): got = swap(kp.send)]
    ppermute x1 -> x4, waiting for transfers between devices: 2.83 us -> 2.11 us  [the longest x1 1.34 us: body(): swap(k1.send)]
    pallas_call x4 -> x8, Pallas kernels: 10.8 us -> 10.2 us  [call(): pl.pallas_call(run, out_shape=[pltpu.VMEM(s, d) if mode == HELD else jax....]
  transfers between devices with their start and end apart: 1 -> 4, of which waited for: 1 -> 2; matrix products, arithmetic and copies ran while one was open for 0% -> 0% of each run, Pallas kernels for 0% -> 5%
where the time goes in v5:
time: 65.3 us; the launch traced here: 65.1 us
  blocking collectives  51.2 us (78%)
  Pallas kernels  10.2 us (16%)
  waiting for transfers between devices  2.11 us (3%)
  starting transfers between devices  0.85 us (1%)
  between operations  0.72 us (1%)
    all_to_all x1, blocking collectives, body(): parts = exchange(packed)  26.4 us
    all_to_all x1, blocking collectives, body(): ends = exchange(kj.ends)  24.9 us
    pallas_call x8, Pallas kernels, call(): pl.pallas_call(run, out_shape=[pltpu.VMEM(s, d) if mode == HELD else jax....  10.2 us
    ppermute x1, waiting for transfers between devices, body(): swap(k1.send)  1.34 us
  transfers between devices with their start and end apart: 4, of which 2 were waited for; matrix products, arithmetic and copies ran while one was open for 0% of the time, Pallas kernels for 5%

profile of v5, /device:TPU:0, one launch (start us, length us, event | category | flops | bytes accessed | tf_op | source)
XLA Modules:
  0.0 65.1 jit_solution(14189176545348037495)
XLA Ops:
  0.6 2.4 %shard_map.222 = (bf16[256,512]{1,0:T(8,128)(2,1)S(1)}, f32[256,512]{1,0:T(8,128)S(1)}, f32[256,128]{1,0:T(8,128)S(1)}, bf16[256,512]{1,0:T(8,128)(2,1)S(1)}, f3...) custom-call(bf16[256,512]{1,0:T(8,128)(2,1)} %bitcast.16, ...), custom_call_target="tpu_custom_call" | custom-call | flops 300000000 | bytes 3000000 | tf_op jit(solution)/shard_map/pallas_call | solution.py:296
  3.1 0.1 collective-permute-start
  3.2 1.3 %collective-permute-done.refs_1_ = bf16[66,8,128]{2,1,0:T(8,128)(2,1)S(1)} collective-permute-done((bf16[66,8,128]{2,1,0:T(8,128)(2,1)S(1)}, bf16[66,8,128]{2,1,0:T(8,128)(2,1)S(1)}, u32[]{:S(2)}, u32[]{:S(2)}) %collective-permute-start) | collective-permute-done | bytes 135200 | tf_op jit(solution)/shard_map/ppermute | solution.py:861
  4.5 0.1 shard_map.223
  4.6 24.9 %all_to_all.10.refs_5_.refs_2_ = bf16[64,4,8,128]{3,2,1,0:T(8,128)(2,1)S(1)} all-to-all(bf16[64,4,8,128]{3,2,1,0:T(8,128)(2,1)S(1)} %get-tuple-element.77), channel_id=1, replica_groups={{0,2,4,6,8,10,12,14,16,18,20,22,24,26,28,30,32,34,36,38,40,42,44,46,48,..., dimensions={0} | all-to-all | bytes 1048576 | tf_op jit(solution)/shard_map/all_to_all | solution.py:864
  29.5 2.2 %shard_map.224 = (bf16[256,512]{1,0:T(8,128)(2,1)}, f32[8,128]{1,0:T(8,128)S(1)}, f32[8,128]{1,0:T(8,128)S(1)}, bf16[256,512]{1,0:T(8,128)(2,1)S(1)}, bf16[256,1...) custom-call(bf16[256,256]{1,0:T(8,128)(2,1)S(1)} %get-tuple-element., ...), custom_call_target="tpu_custom_call" | custom-call | flops 1000000000 | bytes 6000000 | tf_op jit(solution)/shard_map/pallas_call | solution.py:296
  31.7 0.1 collective-permute-start.2
  31.7 0.7 %shard_map.225 = (bf16[64,8,768]{2,1,0:T(8,128)(2,1)S(1)}, bf16[64,8,768]{2,1,0:T(8,128)(2,1)S(1)}) custom-call(bf16[256,512]{1,0:T(8,128)(2,1)S(1)} %get-tuple-element.84.refs_0_, bf16[256,1024]{1,0:T(8,128)(2,1)S(1)} %get-tuple-element.85.refs_1_, bf16[256,512]{1,0:T(8,128)(2,1)S(1)} %get-tuple-element.86.refs_2_, ...), custom_call_target="tpu_custom_call" | custom-call | flops 2000000000 | bytes 3000000 | tf_op jit(solution)/shard_map/pallas_call | solution.py:296
  32.5 0.6 collective-permute-start.1
  33.1 0.0 collective-permute-done.2.refs_3_
  33.1 1.3 %shard_map.226 = (bf16[8,128]{1,0:T(8,128)(2,1)S(1)}, f32[256,512]{1,0:T(8,128)S(1)}, bf16[64,8,384]{2,1,0:T(8,128)(2,1)S(1)}, bf16[64,8,384]{2,1,0:T(8,128)(2,1)S(1)}) custom-call(f32[8,128]{1,0:T(8,128)S(1)} %get-tuple-element.90.refs_0_, f32[8,128]{1,0:T(8,128)S(1)} %get-tuple-element.73.refs_0_.refs_1_, f32[8,128]{1,0:T(8,128)S(1)} %get-tuple-element.91.refs_2_, ...), custom_call_target="tpu_custom_call" | custom-call | flops 6000000000 | bytes 3000000 | tf_op jit(solution)/shard_map/pallas_call | solution.py:296
  34.4 0.1 collective-permute-start.3
  34.5 0.9 %shard_map.227 = (f32[128,512]{1,0:T(8,128)S(1)}, f32[8,512]{1,0:T(8,128)S(1)}, bf16[256,512]{1,0:T(8,128)(2,1)S(1)}, bf16[512,256]{1,0:T(8,128)(2,1)S(1)}, f32[...) custom-call(s32[2,16]{1,0:T(2,128)} %refs_0_.1, ...), custom_call_target="tpu_custom_call" | custom-call | flops 200000000 | bytes 3000000 | tf_op jit(solution)/shard_map/pallas_call | solution.py:296
  35.4 0.8 %collective-permute-done.3.refs_3_ = bf16[64,8,384]{2,1,0:T(8,128)(2,1)S(1)} collective-permute-done((bf16[64,8,384]{2,1,0:T(8,128)(2,1)S(1)}, bf16[64,8,384]{2,1,0:T(8,128)(2,1)S(1)}, u32[]{:S(2)}, u32[]{:S(2)}) %collective-permute-start.3) | collective-permute-done | bytes 393248 | tf_op jit(solution)/shard_map/ppermute | solution.py:900
  36.2 0.0 collective-permute-done.1.refs_1_
  36.2 0.3 shard_map.228
  36.5 26.4 %all_to_all.11.refs_0_ = bf16[64,8,1280]{2,1,0:T(8,128)(2,1)S(1)} all-to-all(bf16[64,8,1280]{2,1,0:T(8,128)(2,1)S(1)} %shard_map.228), channel_id=1, replica_groups={{0,2,4,6,8,10,12,14,16,18,20,22,24,26,28,30,32,34,36,38,40,42,44,46,48,..., dimensions={0} | all-to-all | bytes 2621440 | tf_op jit(solution)/shard_map/all_to_all | solution.py:922
  62.8 2.3 %shard_map.229 = (bf16[256,512]{1,0:T(8,128)(2,1)}, f32[4,512]{1,0:T(4,128)}, f32[4,512]{1,0:T(4,128)}, f32[4,1024]{1,0:T(4,128)}, f32[1,4]{1,0:T(1,128)}, /*ind...) custom-call(bf16[64,8,1280]{2,1,0:T(8,128)(2,1)S(1)} %all_to_all.11.refs_0_, ...), custom_call_target="tpu_custom_call" | custom-call | flops 600000000 | bytes 5000000 | tf_op jit(solution)/shard_map/pallas_call | solution.py:296
Async XLA Ops:
  3.1 1.4 %collective-permute-start = (bf16[66,8,128]{2,1,0:T(8,128)(2,1)S(1)}, bf16[66,8,128]{2,1,0:T(8,128)(2,1)S(1)}, u32[]{:S(2)}, u32[]{:S(2)}) collective-permute-start(bf16[66,8,128]{2,1,0:T(8,128)(2,1)S(1)} %get-tuple-element.74), channel_id=1, source_target_pairs={{0,1},{1,0},{2,3},{3,2},{4,5},{5,4},{6,7},{7,6},{8,9},{9,8},{10,11... | collective-permute-start | bytes 405512 | tf_op jit(solution)/shard_map/ppermute | solution.py:861
  31.7 1.4 %collective-permute-start.2 = (f32[8,128]{1,0:T(8,128)S(1)}, f32[8,128]{1,0:T(8,128)S(1)}, u32[]{:S(2)}, u32[]{:S(2)}) collective-permute-start(f32[8,128]{1,0:T(8,128)S(1)} %get-tuple-element.91.refs_2_), channel_id=1, source_target_pairs={{0,1},{1,0},{2,3},{3,2},{4,5},{5,4},{6,7},{7,6},{8,9},{9,8},{10,11... | collective-permute-start | bytes 12296 | tf_op jit(solution)/shard_map/ppermute | solution.py:883
  32.5 3.7 %collective-permute-start.1 = (bf16[64,8,768]{2,1,0:T(8,128)(2,1)S(1)}, bf16[64,8,768]{2,1,0:T(8,128)(2,1)S(1)}, u32[]{:S(2)}, u32[]{:S(2)}) collective-permute-start(bf16[64,8,768]{2,1,0:T(8,128)(2,1)S(1)} %get-tuple-element.89), channel_id=1, source_target_pairs={{0,1},{1,0},{2,3},{3,2},{4,5},{5,4},{6,7},{7,6},{8,9},{9,8},{10,11... | collective-permute-start | bytes 2359304 | tf_op jit(solution)/shard_map/ppermute | solution.py:889
  34.4 1.8 %collective-permute-start.3 = (bf16[64,8,384]{2,1,0:T(8,128)(2,1)S(1)}, bf16[64,8,384]{2,1,0:T(8,128)(2,1)S(1)}, u32[]{:S(2)}, u32[]{:S(2)}) collective-permute-start(bf16[64,8,384]{2,1,0:T(8,128)(2,1)S(1)} %get-tuple-element.100), channel_id=1, source_target_pairs={{0,1},{1,0},{2,3},{3,2},{4,5},{5,4},{6,7},{7,6},{8,9},{9,8},{10,11... | collective-permute-start | bytes 1179656 | tf_op jit(solution)/shard_map/ppermute | solution.py:900

commit v6 on v5

--- a/solution.py
+++ b/solution.py
@@ -316,7 +316,7 @@
 
 
 AHEAD, BACK, LEVEL, STEP, LAM, SCALE, RATE_U, RADIUS, PER_HALF = 0, 2, 4, 10, 12, 14, 15, 16, 17
-COEF, COEF2, COEF8, COEF16, CHIPS_AHEAD, TABLES = 34, 36, 38, 40, 42, 43
+COEF, COEF2, COEF8, COEF16, TABLES = 34, 36, 38, 40, 42
 
 
 def pair_of(tables, at, half):
@@ -336,35 +336,28 @@
     me = lax.axis_index("seq")
     copy = pltpu.make_async_copy(io.refs.b_tiles.at[me // 2], io.refs.b_rows, io.spare)
     copy.start()
-    io.settle(8)
-    tables = io.refs.tables
-    x = io.x.astype(F32)
-    xhat, rstd = layer_norm(x)
+    io.settle(6)
+    xhat, _ = layer_norm(io.x.astype(F32))
     normed = (xhat * io.gain + io.bias).astype(BF16)
+    _, _, lam, scale = params(io.log_rate, io.angle)
+    pows = powers(lam, 3)
+    io.settle(2)
     io.put(normed=normed)
-    io.put(xhat=xhat)
-    io.put(rstd=jnp.broadcast_to(rstd, (MICRO * TOK, 128)))
-    u, r, lam, scale = params(io.log_rate, io.angle)
-    pows = powers(lam, 11)
     proj = dot(normed, io.b).astype(BF16)
     pairs = permute(proj, io.deal)
     io.put(pairs=pairs.astype(BF16))
     halves = split_channels(pairs)
     parts, scanned = {}, []
     for half in range(HALVES):
-        mine = [spread_rows(p, half) for p in pows[:4]]
+        mine = [spread_rows(p, half) for p in pows]
         (scale8,) = spread_rows((scale,), half)
-        levels, table = scan_tables(mine, False)
+        levels, _ = scan_tables(mine, False)
         re, im = halves[half]
         x8 = group_scan((re * scale8, im * scale8), levels, False)
         scanned.append(x8)
         for micro in range(MICRO):
             _, v = chain_from(x8, micro, mine[3], None, False)
             parts[(micro, half)] = (v[0][7:8, :], v[1][7:8, :])
-        back_levels, back_table = scan_tables([conj(p) for p in mine], True)
-        values = list(table) + list(back_table) + [v for _, level in back_levels for v in level] + list(mine[3]) + list(mine[0])
-        for at, value in enumerate(values + [scale8] + list(spread_rows((u, r), half))):
-            tables[half * PER_HALF + at] = value
     last = tile_rows(parts)
     io.put(last=last)
     even, odd = chunk_rows(xhat[:TOK].T, xhat[TOK:].T)
@@ -373,11 +366,25 @@
     send[0:CHIPS] = jnp.where(me % 2 == 0, odd, even).astype(BF16)
     for i, part in enumerate(in_parts(last, 2)):
         send[CHIPS + i] = part
-    io.put(local=join_channels(scanned))
+    io.put(local=join_channels(scanned), ahead=segment_tile(io.refs.lengths, me // 2))
+    copy.wait()
+
+
+def kernel_tables(io):
+    tables = io.refs.tables
+    u, r, lam, scale = params(io.log_rate, io.angle)
+    pows = powers(lam, 11)
+    for half in range(HALVES):
+        mine = [spread_rows(p, half) for p in pows[:4]]
+        _, table = scan_tables(mine, False)
+        back_levels, back_table = scan_tables([conj(p) for p in mine], True)
+        values = list(table) + list(back_table) + [v for _, level in back_levels for v in level] + list(mine[3]) + list(mine[0])
+        for at, value in enumerate(values + list(spread_rows((scale, u, r), half))):
+            tables[half * PER_HALF + at] = value
     for to, at in ((COEF, 7), (COEF2, 8), (COEF8, 10), (COEF16, 11)):
         tables[to], tables[to + 1] = tile_lam([spread_rows(pows[at], half) for half in range(HALVES)])
-    tables[CHIPS_AHEAD] = segment_tile(io.ready(lengths=0), me // 2)
-    copy.wait()
+    xhat, rstd = layer_norm(io.x.astype(F32))
+    io.put(xhat=xhat, rstd=jnp.broadcast_to(rstd, (MICRO * TOK, 128)), b_perm=permute(io.b, io.deal).astype(BF16))
 
 
 def kernel_join(io):
@@ -454,7 +461,7 @@
     me = lax.axis_index("seq")
     core = me % 2
     tables = io.refs.tables
-    carry = gather_carry(io.refs.ends, me // 2, tables[CHIPS_AHEAD], coefs_of(tables, COEF2, True), coefs_of(tables, COEF16, True))
+    carry = gather_carry(io.refs.ends, me // 2, io.ahead, coefs_of(tables, COEF2, True), coefs_of(tables, COEF16, True))
     carry = jnp.where(core == 0, carry, io.inside + tile_mul(carry, coefs_of(tables, COEF, True)))
     local = split_channels(io.local)
     row = rows_iota((MICRO * GROUPS, 8, 128))
@@ -567,9 +574,10 @@
         rates.append(rate)
         angles.append(turn)
         projs.append((gr * scale, gi * scale))
-    dproj = permute(join_channels(projs).astype(BF16), io.deal_back).astype(BF16)
+    dealt = join_channels(projs).astype(BF16)
+    dproj = permute(dealt, io.deal_back).astype(BF16)
     dyf, normed = io.dy.astype(F32), io.normed
-    dnormed = dot_nt(dproj, io.b) + io.skip * dyf
+    dnormed = dot_nt(dealt, io.b_perm) + io.skip * dyf
     io.put(dnormed=dnormed)
     fours = [column_sum(dnormed * io.xhat), column_sum(dnormed), column_sum(dyf * normed.astype(F32))]
     join = lambda two: jnp.concatenate(two, axis=1)
@@ -702,8 +710,7 @@
             cols += [lr * nr - li * ni, lr * ni + li * nr]
         rows.append(jnp.concatenate(cols, axis=1))
     dproj = jnp.concatenate(rows, axis=0) * scale_row
-    dproj = permute(dproj.astype(BF16), io.deal_back).astype(BF16)
-    dnormed = dot_nt(dproj, io.b) + io.dnormed
+    dnormed = dot_nt(dproj.astype(BF16), io.b_perm) + io.dnormed
     xhat, rstd = io.xhat, io.rstd[:, 0:1]
     dx = dnormed * io.gain
     m1 = jnp.mean(dx, axis=1, keepdims=True)
@@ -836,9 +843,9 @@
     k1 = call(
         kernel_first,
         [
-            (LOAD, dict(x=x, b=b_proj, deal=deal_m, gain=gain, bias=bias)),
-            (COPY, dict(log_rate=rate2, angle=angle2)),
+            (LOAD, dict(x=x, gain=gain, bias=bias, log_rate=rate2, angle=angle2)),
             (SCALARS, dict(lengths=lengths)),
+            (LOAD, dict(b=b_proj, deal=deal_m)),
             (LOAD, dict(deal_back=back_m, c=c_proj, skip=skip, glu=glu_weight, go=go, chosen4=chosen4, chosen2=chosen2)),
             (PLAIN, dict(b_tiles=b_proj.reshape(CHIPS, 8, 512))),
         ],
@@ -846,9 +853,8 @@
             (
                 HELD,
                 dict(
-                    normed=(full, BF16), xhat=(full, F32), rstd=((rows, 128), F32), pairs=(full, BF16), local=(full, F32),
-                    send=((CHIPS + 2, 8, 128), BF16), columns=((CHIPS, 8, 128), BF16), tables=((TABLES, 8, 128), F32), b_rows=((8, 512), BF16),
-                    last=((8, 128), F32),
+                    normed=(full, BF16), pairs=(full, BF16), local=(full, F32), send=((CHIPS + 2, 8, 128), BF16),
+                    columns=((CHIPS, 8, 128), BF16), ahead=((8, 128), F32), b_rows=((8, 512), BF16), last=((8, 128), F32),
                 ),
             )
         ],
@@ -857,16 +863,24 @@
     swap = functools.partial(lax.ppermute, axis_name="seq", perm=[(i, i ^ 1) for i in range(N)])
     same_core = [[2 * t + core for t in range(CHIPS)] for core in range(2)]
     exchange = functools.partial(lax.all_to_all, axis_name="seq", split_axis=0, concat_axis=0, tiled=True, axis_index_groups=same_core)
+    kt = call(
+        kernel_tables,
+        [(HELD, dict(x=k1.x, log_rate=k1.log_rate, angle=k1.angle, b=k1.b, deal=k1.deal))],
+        [
+            (HELD, dict(tables=((TABLES, 8, 128), F32), xhat=(full, F32), rstd=((rows, 128), F32), b_perm=((512, 512), BF16))),
+        ],
+        flops=600_000_000, nbytes=3_000_000,
+    )
     kj = call(
-        kernel_join, [(HELD, dict(last=k1.last, got=swap(k1.send), columns=k1.columns, tables=k1.tables))],
+        kernel_join, [(HELD, dict(last=k1.last, got=swap(k1.send), columns=k1.columns, tables=kt.tables))],
         [(HELD, dict(inside=((8, 128), F32), ends=((CHIPS, 4, 8, 128), BF16)))], flops=1_000_000, nbytes=1_000_000,
     )
     ends = exchange(kj.ends)
     k2 = call(
         kernel_middle,
         [
-            (HELD, dict(deal_back=k1.deal_back, c=k1.c, skip=k1.skip, glu=k1.glu, go=k1.go)),
-            (HELD, dict(ends=ends, inside=kj.inside, tables=k1.tables, local=k1.local, normed=k1.normed, deal=k1.deal, x=k1.x)),
+            (HELD, dict(deal_back=k1.deal_back, c=k1.c, skip=k1.skip, glu=k1.glu, go=k1.go, ahead=k1.ahead)),
+            (HELD, dict(ends=ends, inside=kj.inside, tables=kt.tables, local=k1.local, normed=k1.normed, deal=k1.deal, x=k1.x)),
         ],
         [
             (COPY, dict(out=(full, BF16))),
@@ -883,7 +897,7 @@
     other = swap(k2.first)
     wide, narrow = ((CHIPS, 8, 768), BF16), ((CHIPS, 8, 384), BF16)
     kp = call(
-        kernel_products, [(HELD, dict(act=k2.act, dgated=k2.dgated, hidden=k2.hidden, dy=k2.dy))], [(HELD, dict(keep=wide, send=wide))],
+        kernel_products, [(HELD, dict(act=k2.act, dgated=k2.dgated, hidden=k2.hidden, dy=k2.dy, deal_back=k1.deal_back))], [(HELD, dict(keep=wide, send=wide))],
         flops=2_000_000_000, nbytes=3_000_000,
     )
     got = swap(kp.send)
@@ -891,8 +905,8 @@
         kernel_carried,
         [
             (HELD, dict(carry=k2.carry, last=k1.last)),
-            (HELD, dict(first=k2.first, other=other, back=k2.back, prior=k2.prior, dy=k2.dy, tables=k1.tables, pairs=k1.pairs, b=k1.b)),
-            (HELD, dict(deal_back=k1.deal_back, normed=k1.normed, xhat=k1.xhat, skip=k1.skip, chosen4=k1.chosen4, chosen2=k1.chosen2)),
+            (HELD, dict(first=k2.first, other=other, back=k2.back, prior=k2.prior, dy=k2.dy, tables=kt.tables, pairs=k1.pairs, b_perm=kt.b_perm)),
+            (HELD, dict(deal_back=k1.deal_back, normed=k1.normed, xhat=kt.xhat, skip=k1.skip, chosen4=k1.chosen4, chosen2=k1.chosen2)),
         ],
         [(HELD, dict(chip_first=((8, 128), BF16), dnormed=(full, F32), keep=narrow, send=narrow))],
         flops=6_000_000_000, nbytes=3_000_000,
@@ -902,7 +916,7 @@
         kernel_ahead,
         [
             (SCALARS, dict(lengths=lengths)),
-            (HELD, dict(tables=k1.tables, ends=ends, gain=k1.gain, bias=k1.bias, b_rows=k1.b_rows, dnormed=kc.dnormed)),
+            (HELD, dict(tables=kt.tables, ends=ends, gain=k1.gain, bias=k1.bias, b_rows=k1.b_rows, dnormed=kc.dnormed)),
         ],
         [
             (
@@ -924,7 +938,7 @@
     k3 = call(
         kernel_last,
         [
-            (HELD, dict(parts=parts, dnormed=kc.dnormed, go=k1.go, deal_back=k1.deal_back, tables=k1.tables, b=k1.b, xhat=k1.xhat, rstd=k1.rstd)),
+            (HELD, dict(parts=parts, dnormed=kc.dnormed, go=k1.go, deal_back=k1.deal_back, tables=kt.tables, b_perm=kt.b_perm, xhat=kt.xhat, rstd=kt.rstd)),
             (HELD, dict(gain=k1.gain, reach=ka.reach, reach_sum=ka.reach_sum, reach_low=ka.reach_low, columns=ka.columns)),
             (HELD, dict(channels=ka.channels, channel_pows=ka.channel_pows, opens=ka.opens, pick=ka.pick, mine=ka.mine, joined=ka.joined)),
         ],

time: 65.3 us -> 65.1 us (level)
    pallas_call x8 -> x9, Pallas kernels: 10.2 us -> 10.3 us  [call(): pl.pallas_call(run, out_shape=[pltpu.VMEM(s, d) if mode == HELD else jax....]
where the time goes in v6:
time: 65.1 us; the launch traced here: 64.9 us
  blocking collectives  51.2 us (79%)
  Pallas kernels  10.3 us (16%)
  waiting for transfers between devices  1.78 us (3%)
  starting transfers between devices  0.85 us (1%)
  between operations  0.72 us (1%)
    all_to_all x1, blocking collectives, body(): parts = exchange(packed)  26.4 us
    all_to_all x1, blocking collectives, body(): ends = exchange(kj.ends)  24.9 us
    pallas_call x9, Pallas kernels, call(): pl.pallas_call(run, out_shape=[pltpu.VMEM(s, d) if mode == HELD else jax....  10.3 us
  transfers between devices with their start and end apart: 4, of which 2 were waited for; matrix products, arithmetic and copies ran while one was open for 0% of the time, Pallas kernels for 5%

profile of v6, /device:TPU:0, one launch (start us, length us, event | category | flops | bytes accessed | tf_op | source)
XLA Modules:
  0.0 64.9 jit_solution(13091081417522215302)
XLA Ops:
  0.6 2.3 %shard_map.222 = (bf16[256,512]{1,0:T(8,128)(2,1)S(1)}, bf16[256,512]{1,0:T(8,128)(2,1)S(1)}, f32[256,512]{1,0:T(8,128)S(1)}, bf16[66,8,128]{2,1,0:T(8,128)(2,1)...) custom-call(bf16[256,512]{1,0:T(8,128)(2,1)} %bitcast.16, ...), custom_call_target="tpu_custom_call" | custom-call | flops 300000000 | bytes 3000000 | tf_op jit(solution)/shard_map/pallas_call | solution.py:296
  2.9 0.1 collective-permute-start
  3.0 0.3 shard_map.223
  3.4 1.0 %collective-permute-done.refs_1_ = bf16[66,8,128]{2,1,0:T(8,128)(2,1)S(1)} collective-permute-done((bf16[66,8,128]{2,1,0:T(8,128)(2,1)S(1)}, bf16[66,8,128]{2,1,0:T(8,128)(2,1)S(1)}, u32[]{:S(2)}, u32[]{:S(2)}) %collective-permute-start) | collective-permute-done | bytes 135200 | tf_op jit(solution)/shard_map/ppermute | solution.py:875
  4.4 0.1 shard_map.224
  4.4 24.9 %all_to_all.10.refs_6_.refs_2_ = bf16[64,4,8,128]{3,2,1,0:T(8,128)(2,1)S(1)} all-to-all(bf16[64,4,8,128]{3,2,1,0:T(8,128)(2,1)S(1)} %get-tuple-element.87), channel_id=1, replica_groups={{0,2,4,6,8,10,12,14,16,18,20,22,24,26,28,30,32,34,36,38,40,42,44,46,48,..., dimensions={0} | all-to-all | bytes 1048576 | tf_op jit(solution)/shard_map/all_to_all | solution.py:878
  29.3 2.2 %shard_map.225 = (bf16[256,512]{1,0:T(8,128)(2,1)}, f32[8,128]{1,0:T(8,128)S(1)}, f32[8,128]{1,0:T(8,128)S(1)}, bf16[256,512]{1,0:T(8,128)(2,1)S(1)}, bf16[256,1...) custom-call(bf16[256,256]{1,0:T(8,128)(2,1)S(1)} %get-tuple-element., ...), custom_call_target="tpu_custom_call" | custom-call | flops 1000000000 | bytes 6000000 | tf_op jit(solution)/shard_map/pallas_call | solution.py:296
  31.5 0.1 collective-permute-start.2
  31.6 0.7 %shard_map.226 = (bf16[64,8,768]{2,1,0:T(8,128)(2,1)S(1)}, bf16[64,8,768]{2,1,0:T(8,128)(2,1)S(1)}) custom-call(bf16[256,512]{1,0:T(8,128)(2,1)S(1)} %get-tuple-element.92.refs_0_, bf16[256,1024]{1,0:T(8,128)(2,1)S(1)} %get-tuple-element.93.refs_1_, bf16[256,512]{1,0:T(8,128)(2,1)S(1)} %get-tuple-element.94.refs_2_, ...), custom_call_target="tpu_custom_call" | custom-call | flops 2000000000 | bytes 3000000 | tf_op jit(solution)/shard_map/pallas_call | solution.py:296
  32.4 0.6 collective-permute-start.1
  32.9 0.0 collective-permute-done.2.refs_3_
  32.9 1.3 %shard_map.227 = (bf16[8,128]{1,0:T(8,128)(2,1)S(1)}, f32[256,512]{1,0:T(8,128)S(1)}, bf16[64,8,384]{2,1,0:T(8,128)(2,1)S(1)}, bf16[64,8,384]{2,1,0:T(8,128)(2,1)S(1)}) custom-call(f32[8,128]{1,0:T(8,128)S(1)} %get-tuple-element.98.refs_0_, f32[8,128]{1,0:T(8,128)S(1)} %get-tuple-element.78.refs_0_.refs_1_, f32[8,128]{1,0:T(8,128)S(1)} %get-tuple-element.99.refs_2_, ...), custom_call_target="tpu_custom_call" | custom-call | flops 6000000000 | bytes 3000000 | tf_op jit(solution)/shard_map/pallas_call | solution.py:296
  34.2 0.1 collective-permute-start.3
  34.3 0.9 %shard_map.228 = (f32[128,512]{1,0:T(8,128)S(1)}, f32[8,512]{1,0:T(8,128)S(1)}, bf16[256,512]{1,0:T(8,128)(2,1)S(1)}, bf16[512,256]{1,0:T(8,128)(2,1)S(1)}, f32[...) custom-call(s32[2,16]{1,0:T(2,128)} %refs_0_.1, ...), custom_call_target="tpu_custom_call" | custom-call | flops 200000000 | bytes 3000000 | tf_op jit(solution)/shard_map/pallas_call | solution.py:296
  35.3 0.8 %collective-permute-done.3.refs_3_ = bf16[64,8,384]{2,1,0:T(8,128)(2,1)S(1)} collective-permute-done((bf16[64,8,384]{2,1,0:T(8,128)(2,1)S(1)}, bf16[64,8,384]{2,1,0:T(8,128)(2,1)S(1)}, u32[]{:S(2)}, u32[]{:S(2)}) %collective-permute-start.3) | collective-permute-done | bytes 393248 | tf_op jit(solution)/shard_map/ppermute | solution.py:914
  36.0 0.0 collective-permute-done.1.refs_1_
  36.0 0.3 shard_map.229
  36.3 26.4 %all_to_all.11.refs_0_ = bf16[64,8,1280]{2,1,0:T(8,128)(2,1)S(1)} all-to-all(bf16[64,8,1280]{2,1,0:T(8,128)(2,1)S(1)} %shard_map.229), channel_id=1, replica_groups={{0,2,4,6,8,10,12,14,16,18,20,22,24,26,28,30,32,34,36,38,40,42,44,46,48,..., dimensions={0} | all-to-all | bytes 2621440 | tf_op jit(solution)/shard_map/all_to_all | solution.py:936
  62.7 2.2 %shard_map.230 = (bf16[256,512]{1,0:T(8,128)(2,1)}, f32[4,512]{1,0:T(4,128)}, f32[4,512]{1,0:T(4,128)}, f32[4,1024]{1,0:T(4,128)}, f32[1,4]{1,0:T(1,128)}, /*ind...) custom-call(bf16[64,8,1280]{2,1,0:T(8,128)(2,1)S(1)} %all_to_all.11.refs_0_, ...), custom_call_target="tpu_custom_call" | custom-call | flops 600000000 | bytes 5000000 | tf_op jit(solution)/shard_map/pallas_call | solution.py:296
Async XLA Ops:
  2.9 1.4 %collective-permute-start = (bf16[66,8,128]{2,1,0:T(8,128)(2,1)S(1)}, bf16[66,8,128]{2,1,0:T(8,128)(2,1)S(1)}, u32[]{:S(2)}, u32[]{:S(2)}) collective-permute-start(bf16[66,8,128]{2,1,0:T(8,128)(2,1)S(1)} %get-tuple-element.79), channel_id=1, source_target_pairs={{0,1},{1,0},{2,3},{3,2},{4,5},{5,4},{6,7},{7,6},{8,9},{9,8},{10,11... | collective-permute-start | bytes 405512 | tf_op jit(solution)/shard_map/ppermute | solution.py:875
  31.5 1.4 %collective-permute-start.2 = (f32[8,128]{1,0:T(8,128)S(1)}, f32[8,128]{1,0:T(8,128)S(1)}, u32[]{:S(2)}, u32[]{:S(2)}) collective-permute-start(f32[8,128]{1,0:T(8,128)S(1)} %get-tuple-element.99.refs_2_), channel_id=1, source_target_pairs={{0,1},{1,0},{2,3},{3,2},{4,5},{5,4},{6,7},{7,6},{8,9},{9,8},{10,11... | collective-permute-start | bytes 12296 | tf_op jit(solution)/shard_map/ppermute | solution.py:897
  32.4 3.7 %collective-permute-start.1 = (bf16[64,8,768]{2,1,0:T(8,128)(2,1)S(1)}, bf16[64,8,768]{2,1,0:T(8,128)(2,1)S(1)}, u32[]{:S(2)}, u32[]{:S(2)}) collective-permute-start(bf16[64,8,768]{2,1,0:T(8,128)(2,1)S(1)} %get-tuple-element.97), channel_id=1, source_target_pairs={{0,1},{1,0},{2,3},{3,2},{4,5},{5,4},{6,7},{7,6},{8,9},{9,8},{10,11... | collective-permute-start | bytes 2359304 | tf_op jit(solution)/shard_map/ppermute | solution.py:903
  34.2 1.8 %collective-permute-start.3 = (bf16[64,8,384]{2,1,0:T(8,128)(2,1)S(1)}, bf16[64,8,384]{2,1,0:T(8,128)(2,1)S(1)}, u32[]{:S(2)}, u32[]{:S(2)}) collective-permute-start(bf16[64,8,384]{2,1,0:T(8,128)(2,1)S(1)} %get-tuple-element.108), channel_id=1, source_target_pairs={{0,1},{1,0},{2,3},{3,2},{4,5},{5,4},{6,7},{7,6},{8,9},{9,8},{10,11... | collective-permute-start | bytes 1179656 | tf_op jit(solution)/shard_map/ppermute | solution.py:914

commit v7 on v5

--- a/solution.py
+++ b/solution.py
@@ -269,7 +269,7 @@
             self.out_copies[name].wait()
 
 
-def call(kernel, ins, outs, extra=(), flops=0, nbytes=0):
+def call(kernel, ins, outs, extra=(), alias=None, flops=0, nbytes=0):
     ins = [(name, array, mode) for mode, group in ins for name, array in group.items()]
     outs = [(name, shape, kind, mode) for mode, group in outs for name, (shape, kind) in group.items()]
     outs += [(name, array.shape, array.dtype, HELD) for name, array, mode in ins if mode == LOAD]
@@ -299,6 +299,7 @@
         in_specs=[spec(mode) for _, _, mode in ins],
         out_specs=[spec(mode) for _, _, _, mode in outs],
         scratch_shapes=scratch + list(extra),
+        input_output_aliases=alias or {},
         compiler_params=pltpu.CompilerParams(vmem_limit_bytes=VMEM_LIMIT),
         cost_estimate=pl.CostEstimate(flops=flops, bytes_accessed=nbytes, transcendentals=0),
     )(*args)
@@ -587,9 +588,12 @@
     by_core(io.refs.keep, io.refs.send, core, jnp.concatenate([even, tiles[0]], axis=2), jnp.concatenate([odd, tiles[1]], axis=2))
 
 
+def kernel_pack_wide(io):
+    io.refs.wide[:, :, 0:768] = (io.keep.astype(F32) + io.got.astype(F32)).astype(BF16)
+
+
 def kernel_pack(io):
     out = io.refs.packed
-    out[:, :, 0:768] = (io.keep.astype(F32) + io.got.astype(F32)).astype(BF16)
     keep, got = io.keep_b.astype(F32), io.got_b.astype(F32)
     out[:, :, 768:1024] = (keep[:, :, 0:256] + got[:, :, 0:256]).astype(BF16)
     out[:, :, 1024:1152] = jnp.broadcast_to(io.chip_first[None], (CHIPS, 8, 128))
@@ -915,9 +919,13 @@
         ],
         flops=200_000_000, nbytes=3_000_000,
     )
+    chunks = ((CHIPS, 8, 1280), BF16)
+    wide_part = call(
+        kernel_pack_wide, [(HELD, dict(keep=kp.keep, got=got, reach=ka.reach))], [(HELD, dict(wide=chunks))], flops=1_000_000, nbytes=2_400_000
+    ).wide
     packed = call(
-        kernel_pack, [(HELD, dict(keep=kp.keep, got=got, keep_b=kc.keep, got_b=got_b, chip_first=kc.chip_first, reach=ka.reach))],
-        [(HELD, dict(packed=((CHIPS, 8, 1280), BF16)))], flops=1_000_000, nbytes=2_400_000,
+        kernel_pack, [(HELD, dict(wide=wide_part, keep_b=kc.keep, got_b=got_b, chip_first=kc.chip_first))],
+        [(HELD, dict(packed=chunks))], alias={0: 0}, flops=1_000_000, nbytes=1_200_000,
     ).packed
     parts = exchange(packed)
     four, two = ((1, 4), F32), ((1, 2), F32)

time: 65.3 us -> 65.1 us (level)
    pallas_call x8 -> x9, Pallas kernels: 10.2 us -> 10.2 us  [call(): pl.pallas_call(run, out_shape=[pltpu.VMEM(s, d) if mode == HELD else jax....]
where the time goes in v7:
time: 65.1 us; the launch traced here: 64.9 us
  blocking collectives  51.2 us (79%)
  Pallas kernels  10.2 us (16%)
  waiting for transfers between devices  1.91 us (3%)
  starting transfers between devices  0.85 us (1%)
  between operations  0.73 us (1%)
    all_to_all x1, blocking collectives, body(): parts = exchange(packed)  26.4 us
    all_to_all x1, blocking collectives, body(): ends = exchange(kj.ends)  24.9 us
    pallas_call x9, Pallas kernels, call(): pl.pallas_call(run, out_shape=[pltpu.VMEM(s, d) if mode == HELD else jax....  10.2 us
    ppermute x1, waiting for transfers between devices, body(): swap(k1.send)  1.34 us
  transfers between devices with their start and end apart: 4, of which 2 were waited for; matrix products, arithmetic and copies ran while one was open for 0% of the time, Pallas kernels for 5%

profile of v7, /device:TPU:0, one launch (start us, length us, event | category | flops | bytes accessed | tf_op | source)
XLA Modules:
  0.0 64.9 jit_solution(8153022197332948905)
XLA Ops:
  0.6 2.4 %shard_map.222 = (bf16[256,512]{1,0:T(8,128)(2,1)S(1)}, f32[256,512]{1,0:T(8,128)S(1)}, f32[256,128]{1,0:T(8,128)S(1)}, bf16[256,512]{1,0:T(8,128)(2,1)S(1)}, f3...) custom-call(bf16[256,512]{1,0:T(8,128)(2,1)} %bitcast.16, ...), custom_call_target="tpu_custom_call" | custom-call | flops 300000000 | bytes 3000000 | tf_op jit(solution)/shard_map/pallas_call | solution.py:296
  3.1 0.1 collective-permute-start
  3.2 1.3 %collective-permute-done.refs_1_ = bf16[66,8,128]{2,1,0:T(8,128)(2,1)S(1)} collective-permute-done((bf16[66,8,128]{2,1,0:T(8,128)(2,1)S(1)}, bf16[66,8,128]{2,1,0:T(8,128)(2,1)S(1)}, u32[]{:S(2)}, u32[]{:S(2)}) %collective-permute-start) | collective-permute-done | bytes 135200 | tf_op jit(solution)/shard_map/ppermute | solution.py:865
  4.5 0.1 shard_map.223
  4.6 24.9 %all_to_all.10.refs_5_.refs_2_ = bf16[64,4,8,128]{3,2,1,0:T(8,128)(2,1)S(1)} all-to-all(bf16[64,4,8,128]{3,2,1,0:T(8,128)(2,1)S(1)} %get-tuple-element.77), channel_id=1, replica_groups={{0,2,4,6,8,10,12,14,16,18,20,22,24,26,28,30,32,34,36,38,40,42,44,46,48,..., dimensions={0} | all-to-all | bytes 1048576 | tf_op jit(solution)/shard_map/all_to_all | solution.py:868
  29.5 2.2 %shard_map.224 = (bf16[256,512]{1,0:T(8,128)(2,1)}, f32[8,128]{1,0:T(8,128)S(1)}, f32[8,128]{1,0:T(8,128)S(1)}, bf16[256,512]{1,0:T(8,128)(2,1)S(1)}, bf16[256,1...) custom-call(bf16[256,256]{1,0:T(8,128)(2,1)S(1)} %get-tuple-element., ...), custom_call_target="tpu_custom_call" | custom-call | flops 1000000000 | bytes 6000000 | tf_op jit(solution)/shard_map/pallas_call | solution.py:296
  31.7 0.1 collective-permute-start.2
  31.7 0.7 %shard_map.225 = (bf16[64,8,768]{2,1,0:T(8,128)(2,1)S(1)}, bf16[64,8,768]{2,1,0:T(8,128)(2,1)S(1)}) custom-call(bf16[256,512]{1,0:T(8,128)(2,1)S(1)} %get-tuple-element.84.refs_0_, bf16[256,1024]{1,0:T(8,128)(2,1)S(1)} %get-tuple-element.85.refs_1_, bf16[256,512]{1,0:T(8,128)(2,1)S(1)} %get-tuple-element.86.refs_2_, ...), custom_call_target="tpu_custom_call" | custom-call | flops 2000000000 | bytes 3000000 | tf_op jit(solution)/shard_map/pallas_call | solution.py:296
  32.5 0.6 collective-permute-start.1
  33.1 0.0 collective-permute-done.2.refs_3_
  33.1 1.3 %shard_map.226 = (bf16[8,128]{1,0:T(8,128)(2,1)S(1)}, f32[256,512]{1,0:T(8,128)S(1)}, bf16[64,8,384]{2,1,0:T(8,128)(2,1)S(1)}, bf16[64,8,384]{2,1,0:T(8,128)(2,1)S(1)}) custom-call(f32[8,128]{1,0:T(8,128)S(1)} %get-tuple-element.93.refs_0_, f32[8,128]{1,0:T(8,128)S(1)} %get-tuple-element.73.refs_0_.refs_1_, f32[8,128]{1,0:T(8,128)S(1)} %get-tuple-element.94.refs_2_, ...), custom_call_target="tpu_custom_call" | custom-call | flops 6000000000 | bytes 3000000 | tf_op jit(solution)/shard_map/pallas_call | solution.py:296
  34.4 0.1 collective-permute-start.3
  34.5 0.9 %shard_map.227 = (f32[128,512]{1,0:T(8,128)S(1)}, f32[8,512]{1,0:T(8,128)S(1)}, bf16[256,512]{1,0:T(8,128)(2,1)S(1)}, bf16[512,256]{1,0:T(8,128)(2,1)S(1)}, f32[...) custom-call(s32[2,16]{1,0:T(2,128)} %refs_0_.1, ...), custom_call_target="tpu_custom_call" | custom-call | flops 200000000 | bytes 3000000 | tf_op jit(solution)/shard_map/pallas_call | solution.py:296
  35.4 0.0 collective-permute-done.1.refs_1_
  35.4 0.2 shard_map.228.refs_0_
  35.6 0.6 collective-permute-done.3.refs_2_
  36.2 0.1 shard_map.229
  36.3 26.4 %all_to_all.11.refs_0_ = bf16[64,8,1280]{2,1,0:T(8,128)(2,1)S(1)} all-to-all(bf16[64,8,1280]{2,1,0:T(8,128)(2,1)S(1)} %shard_map.229), channel_id=1, replica_groups={{0,2,4,6,8,10,12,14,16,18,20,22,24,26,28,30,32,34,36,38,40,42,44,46,48,..., dimensions={0} | all-to-all | bytes 2621440 | tf_op jit(solution)/shard_map/all_to_all | solution.py:930
  62.6 2.3 %shard_map.230 = (bf16[256,512]{1,0:T(8,128)(2,1)}, f32[4,512]{1,0:T(4,128)}, f32[4,512]{1,0:T(4,128)}, f32[4,1024]{1,0:T(4,128)}, f32[1,4]{1,0:T(1,128)}, /*ind...) custom-call(bf16[64,8,1280]{2,1,0:T(8,128)(2,1)S(1)} %all_to_all.11.refs_0_, ...), custom_call_target="tpu_custom_call" | custom-call | flops 600000000 | bytes 5000000 | tf_op jit(solution)/shard_map/pallas_call | solution.py:296
Async XLA Ops:
  3.1 1.4 %collective-permute-start = (bf16[66,8,128]{2,1,0:T(8,128)(2,1)S(1)}, bf16[66,8,128]{2,1,0:T(8,128)(2,1)S(1)}, u32[]{:S(2)}, u32[]{:S(2)}) collective-permute-start(bf16[66,8,128]{2,1,0:T(8,128)(2,1)S(1)} %get-tuple-element.74), channel_id=1, source_target_pairs={{0,1},{1,0},{2,3},{3,2},{4,5},{5,4},{6,7},{7,6},{8,9},{9,8},{10,11... | collective-permute-start | bytes 405512 | tf_op jit(solution)/shard_map/ppermute | solution.py:865
  31.7 1.4 %collective-permute-start.2 = (f32[8,128]{1,0:T(8,128)S(1)}, f32[8,128]{1,0:T(8,128)S(1)}, u32[]{:S(2)}, u32[]{:S(2)}) collective-permute-start(f32[8,128]{1,0:T(8,128)S(1)} %get-tuple-element.94.refs_2_), channel_id=1, source_target_pairs={{0,1},{1,0},{2,3},{3,2},{4,5},{5,4},{6,7},{7,6},{8,9},{9,8},{10,11... | collective-permute-start | bytes 12296 | tf_op jit(solution)/shard_map/ppermute | solution.py:887
  32.5 2.9 %collective-permute-start.1 = (bf16[64,8,768]{2,1,0:T(8,128)(2,1)S(1)}, bf16[64,8,768]{2,1,0:T(8,128)(2,1)S(1)}, u32[]{:S(2)}, u32[]{:S(2)}) collective-permute-start(bf16[64,8,768]{2,1,0:T(8,128)(2,1)S(1)} %get-tuple-element.89), channel_id=1, source_target_pairs={{0,1},{1,0},{2,3},{3,2},{4,5},{5,4},{6,7},{7,6},{8,9},{9,8},{10,11... | collective-permute-start | bytes 2359304 | tf_op jit(solution)/shard_map/ppermute | solution.py:893
  34.4 1.8 %collective-permute-start.3 = (bf16[64,8,384]{2,1,0:T(8,128)(2,1)S(1)}, bf16[64,8,384]{2,1,0:T(8,128)(2,1)S(1)}, u32[]{:S(2)}, u32[]{:S(2)}) collective-permute-start(bf16[64,8,384]{2,1,0:T(8,128)(2,1)S(1)} %get-tuple-element.105), channel_id=1, source_target_pairs={{0,1},{1,0},{2,3},{3,2},{4,5},{5,4},{6,7},{7,6},{8,9},{9,8},{10,11... | collective-permute-start | bytes 1179656 | tf_op jit(solution)/shard_map/ppermute | solution.py:904
